TPU v7x, 32 devices: a whole 2x2x4 slice. The times are simulated.
32 devices in a mesh: seq: 8 (over z, y), head: 4 (over x, core).
Axes of the slice: x: 2, y: 2, z: 4, core: 2. Of those that a mesh axis runs over, the one named last changes fastest.
Arguments:
- tokens: bfloat16 [4096, 2048], P('seq'), may hold values from -24 to 24
- w_query: bfloat16 [2048, 2048], P(None, 'head'), may hold values from -0.125 to 0.125
- w_key: bfloat16 [2048, 2048], P(None, 'head'), may hold values from -0.125 to 0.125
- w_value: bfloat16 [2048, 2048], P(None, 'head'), may hold values from -0.125 to 0.125
- w_out: bfloat16 [2048, 2048], P('head'), may hold values from -0.125 to 0.125
- shared_gate: bfloat16 [2048, 1024], P(None, 'head'), may hold values from -0.125 to 0.125
- shared_up: bfloat16 [2048, 1024], P(None, 'head'), may hold values from -0.125 to 0.125
- shared_down: bfloat16 [1024, 2048], P('head'), may hold values from -0.1875 to 0.1875
- expert_gate: bfloat16 [64, 2048, 1024], P('seq', None, 'head'), may hold values from -0.125 to 0.125
- expert_up: bfloat16 [64, 2048, 1024], P('seq', None, 'head'), may hold values from -0.125 to 0.125
- expert_down: bfloat16 [64, 1024, 2048], P('seq', 'head'), may hold values from -0.1875 to 0.1875
- expert_ids: int32 [4096, 1], P('seq'), may hold values from 0 to 63; in each aligned block of 512 rows (0 to 511, 512 to 1023, ...) at most 16 rows name the same one
Outputs:
- output: bfloat16 [4096, 2048], P('seq', 'head')
Inputs may be any that keep to these rules, and one draw needn't show every extreme that they name: `expert_ids`: among the 512 tokens of one index of seq (aligned blocks of the sequence) at most 16 name the same expert, and in some block of every draw one expert is named by exactly 16 tokens.
All inputs are finite; a program needn't handle non-finite values.
Results may differ from a plain program's by a relative error of at most 0.015.
Values may be sent and summed in bfloat16 or wider, within the bound.
No kernel may reach another device: no remote copies, remote signals or barrier semaphores. Data moves between devices by JAX's collectives and lax.ppermute only.
A program may use at most 128 MiB of HBM per device.

v0:
```python
import jax
import jax.numpy as jnp
from jax import lax
from jax.sharding import PartitionSpec as P

HD = 128
EXPERTS = 64
CAP = 16


def prefix(array, axis, combine, identity):
    length, mine = (lax.axis_size(axis), lax.axis_index(axis))
    everything = lax.all_gather(array, axis)
    start = jnp.broadcast_to(jnp.asarray(identity, array.dtype), array.shape)

    def hop(k, before):
        reached = k < mine
        new = combine(before, everything[k])
        return jnp.where(reached, new, before)

    return lax.fori_loop(0, length, hop, start)


def rms_rows(values):
    return values * lax.rsqrt(jnp.mean(values * values, axis=-1, keepdims=True) + 1e-06)


def add_states(earlier, later):
    return earlier + later


def causal_attention(query_rows, key_rows, value_rows):
    row_count = query_rows.shape[0]
    block_rows = min(512, row_count)
    causal = jnp.arange(block_rows)[:, None] >= jnp.arange(block_rows)[None, :]
    block_states = [
        jnp.einsum("thd,the->hde", key_rows, value_rows, preferred_element_type=jnp.float32)
    ]
    local_state = block_states[0]
    return (local_state, block_rows, causal, block_states)


def shards(
    tokens,
    w_query,
    w_key,
    w_value,
    w_out,
    shared_gate,
    shared_up,
    shared_down,
    expert_gate,
    expert_up,
    expert_down,
    expert_ids,
):
    highest = lax.Precision.HIGHEST
    rows_here = tokens.shape[0]
    model_width = tokens.shape[1]
    heads_here = w_query.shape[1] // HD
    experts_here = expert_gate.shape[0]
    inputs = tokens.astype(jnp.float32)
    normed_input = rms_rows(inputs).astype(jnp.bfloat16)
    query_rows = (
        jnp.dot(normed_input, w_query, preferred_element_type=jnp.float32)
        .astype(jnp.bfloat16)
        .reshape(rows_here, heads_here, HD)
    )
    key_rows = (
        jnp.dot(normed_input, w_key, preferred_element_type=jnp.float32)
        .astype(jnp.bfloat16)
        .reshape(rows_here, heads_here, HD)
    )
    value_rows = (
        jnp.dot(normed_input, w_value, preferred_element_type=jnp.float32)
        .astype(jnp.bfloat16)
        .reshape(rows_here, heads_here, HD)
    )
    local_state, block_rows, causal, block_states = causal_attention(
        query_rows, key_rows, value_rows
    )
    carried = prefix(local_state, "seq", add_states, jnp.zeros_like(local_state))
    scores = jnp.einsum("thd,shd->hts", query_rows, key_rows, preferred_element_type=jnp.float32)
    scores = jnp.where(causal[None], scores, 0.0)
    within = jnp.einsum("hts,shd->thd", scores, value_rows.astype(jnp.float32), precision=highest)
    before = jnp.einsum("thd,hde->the", query_rows.astype(jnp.float32), carried, precision=highest)
    outputs = within + before
    head_normed = rms_rows(outputs).reshape(rows_here, heads_here * HD).astype(jnp.bfloat16)
    head_term = jnp.dot(head_normed, w_out, preferred_element_type=jnp.float32)
    col_width = model_width // lax.axis_size("head")
    head_position = lax.axis_index("head")
    summed = lax.psum(head_term.astype(jnp.bfloat16), "head").astype(jnp.float32)
    residual = inputs + summed
    normed_mid = rms_rows(residual).astype(jnp.bfloat16)
    residual_share = lax.dynamic_slice_in_dim(residual, head_position * col_width, col_width, 1)
    expert_of = expert_ids[:, 0]
    onehot = (expert_of[:, None] == jnp.arange(EXPERTS, dtype=jnp.int32)[None, :]).astype(jnp.int32)
    slot_rank = jnp.sum(jnp.cumsum(onehot, axis=0) * onehot, axis=1) - 1
    slot_index = expert_of * CAP + slot_rank
    source_row = (
        jnp.full((EXPERTS * CAP,), rows_here, jnp.int32)
        .at[slot_index]
        .set(jnp.arange(rows_here, dtype=jnp.int32))
    )
    padded = jnp.concatenate([normed_mid, jnp.zeros((1, model_width), jnp.bfloat16)], axis=0)
    outgoing = jnp.take(padded, source_row, axis=0).reshape(EXPERTS, CAP, model_width)
    arrived = lax.all_to_all(outgoing, "seq", split_axis=0, concat_axis=0, tiled=True)
    sources = arrived.shape[0] // experts_here
    count = arrived.shape[1]
    grouped = arrived.reshape(sources, experts_here, count, model_width)
    gate_act = jnp.einsum(
        "secd,edf->secf", grouped, expert_gate, preferred_element_type=jnp.float32
    )
    up_act = jnp.einsum("secd,edf->secf", grouped, expert_up, preferred_element_type=jnp.float32)
    hidden = (jax.nn.silu(gate_act) * up_act).astype(jnp.bfloat16)
    result = jnp.einsum(
        "secf,efd->secd", hidden, expert_down, preferred_element_type=jnp.float32
    ).astype(jnp.bfloat16)
    result = result.reshape(arrived.shape[0], count, model_width)
    reduced = lax.psum_scatter(
        result.astype(jnp.float32).astype(jnp.bfloat16), "head", scatter_dimension=2, tiled=True
    )
    returned = lax.all_to_all(reduced, "seq", split_axis=0, concat_axis=0, tiled=True)
    returned_width = returned.shape[2]
    routed = jnp.take(returned.reshape(EXPERTS * CAP, returned_width), slot_index, axis=0)
    shared_hidden = (
        jax.nn.silu(jnp.dot(normed_mid, shared_gate, preferred_element_type=jnp.float32))
        * jnp.dot(normed_mid, shared_up, preferred_element_type=jnp.float32)
    ).astype(jnp.bfloat16)
    shared_term = jnp.dot(shared_hidden, shared_down, preferred_element_type=jnp.float32)
    shared_total = lax.psum_scatter(
        shared_term.astype(jnp.bfloat16), "head", scatter_dimension=1, tiled=True
    ).astype(jnp.float32)
    return (residual_share + shared_total + routed.astype(jnp.float32)).astype(jnp.bfloat16)


def solution(mesh):
    return jax.shard_map(
        shards,
        mesh=mesh,
        in_specs=(
            P("seq", None),
            P(None, "head"),
            P(None, "head"),
            P(None, "head"),
            P("head", None),
            P(None, "head"),
            P(None, "head"),
            P("head", None),
            P("seq", None, "head"),
            P("seq", None, "head"),
            P("seq", "head", None),
            P("seq", None),
        ),
        out_specs=P("seq", "head"),
        check_vma=False,
    )
```

profile of v0, /device:TPU:0, one launch (start us, length us, event | category | flops | bytes accessed | tf_op | source)
XLA Modules:
  0.0 345.7 jit_solution(12848984096251182661)
XLA Ops:
  6.5 2.2 fusion.6
  8.8 3.7 %convolution_convert_fusion.2 = bf16[512,512]{0,1:T(8,128)(2,1)S(1)} fusion(bf16[2048,512]{1,0:T(8,128)(2,1)} %param.16, bf16[512,2048]{1,0:T(8,128)(2,1)} %param.14, f32[512]{0:T(512)S(1)} %add_rsqrt_fusion.2), kind=kOutput, calls=%fused_computation.33 | convolution fusion | flops 1077149696 | bytes 4720640 | tf_op jit(solution)/shard_map/dot_general | solution.py:70
  12.6 1.4 convolution_convert_fusion.4
  15.1 1.2 reduce-window.6
  17.1 3.6 %convolution_convert_fusion.3 = bf16[512,512]{0,1:T(8,128)(2,1)S(1)} fusion(bf16[2048,512]{1,0:T(8,128)(2,1)} %param.15, bf16[512,2048]{1,0:T(8,128)(2,1)} %param.14, f32[512]{0:T(512)S(1)} %add_rsqrt_fusion.2), kind=kOutput, calls=%fused_computation.34 | convolution fusion | flops 1077149696 | bytes 4720640 | tf_op jit(solution)/shard_map/dot_general | solution.py:65
  20.7 2.7 fusion.60
  23.4 43.7 %all-gather.3.cloned.1.call-done = f32[32,128,128]{2,1,0:T(8,128)} async-done(((f32[4,128,128]{2,1,0:T(8,128)}), f32[32,128,128]{2,1,0:T(8,128)}) %all-gather.3.cloned.1.call-update) | async-done | bytes 2097168 | tf_op jit(solution)/shard_map/all_gather | solution.py:13
  67.2 8.5 %while.14 = (s32[]{:T(128)}, f32[4,128,128]{2,1,0:T(8,128)S(1)}, s32[]{:T(128)}, f32[8,4,128,128]{3,2,1,0:T(8,128)}, s32[]{:T(128)}, /*index=5*/s32[]{:T(128)}) while((s32[]{:T(128)}, f32[4,128,128]{2,1,0:T(8,128)S(1)}, s32[]{:T(128)}, f32[8,4,128,128]{3,2,1,0:T(8,128)}, s32[]{:T(128)}, /*index=5*/s32[]{:T(128)}) %tuple.46), condition=%wide.region_2.3_spmd.clone, body=%wide.region_1.2_spmd.clone.sunk | while | flops 196612 | bytes 786533 | solution.py:21
  68.2 1.0 add_select_fusion.2
  70.4 1.0 add_select_fusion.2
  72.5 1.0 add_select_fusion.2
  76.3 5.0 %multiply_reduce_fusion.1 = (f32[512,4]{0,1:T(4,128)S(1)}, f32[512,4,128]{0,2,1:T(8,128)S(1)}) fusion(f32[4,128,512]{2,1,0:T(8,128)S(1)} %fusion.62, bf16[512,4,128]{0,2,1:T(8,128)(2,1)S(1)} %bitcast.99, f32[4,512,512]{2,1,0:T(8,128)} %fusion.60, pred[512,512]{1,0:T(8,128)(4,1)} %iota_compare_fusion), kind=kOutput, calls=%fused_computation.40 | convolution fusion | flops 1612445696 | bytes 7086080 | tf_op jit(solution)/shard_map/hts,shd->thd/dot_general | solution.py:85
  81.5 2.6 convolution_convert_fusion.1
  84.6 2.6 scatter_custom_fusion
  87.3 46.8 %all-reduce.3.cloned.1.call-done = bf16[512,2048]{1,0:T(8,128)(2,1)} async-done(((bf16[512,2048]{1,0:T(8,128)(2,1)}), bf16[512,2048]{1,0:T(8,128)(2,1)}) %all-reduce.3.cloned.1.call-update) | async-done | bytes 2097168 | tf_op jit(solution)/shard_map/psum | solution.py:92
  134.1 5.0 %convert_add_fusion = (f32[512,2048]{1,0:T(8,128)}, f32[512]{0:T(512)S(1)}) fusion(bf16[512,2048]{1,0:T(8,128)(2,1)} %param.14, bf16[512,2048]{1,0:T(8,128)(2,1)} %all-reduce.3.cloned.1.call-done), kind=kLoop, calls=%fused_computation.10 | loop fusion | flops 5242368 | bytes 8390656 | tf_op jit(solution)/shard_map/add | solution.py:93
  139.8 1.3 copy-done.5
  141.4 6.1 %gather_fusion = bf16[1024,2048]{1,0:T(8,128)(2,1)} fusion(bf16[513,2048]{1,0:T(8,128)(2,1)S(1)} %concatenate.3, s32[1024]{0:T(1024)S(1)} %fusion.52), kind=kCustom, calls=%fused_computation | custom fusion | bytes 8392704 | tf_op jit(solution)/shard_map/jit(_take)/gather | solution.py:106
  147.4 2.6 broadcast_select_fusion
  150.1 98.7 %all_to_all.10 = bf16[64,16,2048]{2,1,0:T(8,128)(2,1)S(1)} all-to-all(bf16[64,16,2048]{2,1,0:T(8,128)(2,1)S(1)} %broadcast_select_fusion), channel_id=1, replica_groups=mesh['seq'=8,'head'=4] {'seq'}, dimensions={0} | all-to-all | bytes 8388608 | tf_op jit(solution)/shard_map/all_to_all | solution.py:107
  248.8 5.0 %fusion.16 = f32[8,8,16,256]{3,2,0,1:T(8,128)S(1)} fusion(bf16[8,2048,256]{2,1,0:T(8,128)(2,1)} %param.22, bf16[8,8,16,2048]{3,2,1,0:T(8,128)(2,1)S(1)} %bitcast.92), kind=kOutput, calls=%fused_computation.27 | convolution fusion | flops 1073741824 | bytes 13631488 | tf_op jit(solution)/shard_map/secd,edf->secf/dot_general | solution.py:111
  253.8 1.4 fusion.37
  256.2 1.3 convert_bitcast_fusion
  257.5 2.3 copy.30
  259.8 1.5 copy-done.6
  261.6 1.5 fusion.63
  263.1 5.6 %convolution_convert_fusion = bf16[512,2048]{1,0:T(8,128)(2,1)} fusion(bf16[256,2048]{1,0:T(8,128)(2,1)} %param.21, bf16[512,2048]{1,0:T(8,128)(2,1)S(1)} %copy-done.6, bf16[2048,256]{1,0:T(8,128)(2,1)} %param.20, f32[512,256]{1,0:T(8,128)} %fusion.63), kind=kOutput, calls=%fused_computation.23 | convolution fusion | flops 1075576832 | bytes 6815744 | tf_op jit(solution)/shard_map/dot_general | solution.py:130
  268.7 34.0 %reduce-scatter.5.cloned.1.call-done = bf16[64,16,512]{2,1,0:T(8,128)(2,1)} async-done(((bf16[64,16,2048]{2,1,0:T(8,128)(2,1)}), bf16[64,16,512]{2,1,0:T(8,128)(2,1)}) %reduce-scatter.5.cloned.1.call-update) | async-done | bytes 1048592 | tf_op jit(solution)/shard_map/reduce_scatter | solution.py:120
  302.7 5.5 %all-to-all-start.1 = ((bf16[64,16,512]{2,1,0:T(8,128)(2,1)}), bf16[64,16,512]{2,1,0:T(8,128)(2,1)S(1)}, u32[]{:S(2)}, u32[]{:S(2)}) async-start(bf16[64,16,512]{2,1,0:T(8,128)(2,1)} %reduce-scatter.5.cloned.1.call-done), calls=%async_computation.3 | async-start | bytes 2097152 | tf_op jit(solution)/shard_map/all_to_all | solution.py:123
  308.2 25.8 %all-to-all-done.1 = bf16[64,16,512]{2,1,0:T(8,128)(2,1)S(1)} async-done(((bf16[64,16,512]{2,1,0:T(8,128)(2,1)}), bf16[64,16,512]{2,1,0:T(8,128)(2,1)S(1)}, u32[]{:S(2)}, u32[]{:S(2)}) %all-to-all-start.1) | async-done | bytes 1048608 | tf_op jit(solution)/shard_map/all_to_all | solution.py:123
  334.0 2.6 gather_fusion.1
  336.6 2.5 add_convert_fusion
  (68 shorter events, 10.7 us)
Async XLA Ops:
  6.5 74.9 %copy-start = (bf16[512,2048]{1,0:T(8,128)(2,1)S(1)}, bf16[512,2048]{1,0:T(8,128)(2,1)}, u32[]{:S(2)}) copy-start(bf16[512,2048]{1,0:T(8,128)(2,1)} %param.18) | copy-start | bytes 6291460
  6.5 60.6 %all-gather.3.cloned.1.call-start = ((), (), s32[]{:S(2)}) async-start(), calls=%async_computation.7 | async-start | bytes 2359296 | tf_op jit(solution)/shard_map/all_gather | solution.py:13
  8.8 3.8 %copy-start.2 = (bf16[512,2048]{1,0:T(8,128)(2,1)S(1)}, bf16[512,2048]{1,0:T(8,128)(2,1)}, u32[]{:S(2)}) copy-start(bf16[512,2048]{1,0:T(8,128)(2,1)} %param.14) | copy-start | bytes 6291460
  8.8 3.8 %copy-start.10 = (bf16[2048,512]{1,0:T(8,128)(2,1)S(1)}, bf16[2048,512]{1,0:T(8,128)(2,1)}, u32[]{:S(2)}) copy-start(bf16[2048,512]{1,0:T(8,128)(2,1)} %param.17) | copy-start | bytes 6291460
  12.6 2.5 copy-start.9
  14.0 1.0 copy-start.7
  15.0 119.1 %all-reduce.3.cloned.1.call-start = ((), (), s32[]{:S(2)}) async-start(), calls=%async_computation.4 | async-start | bytes 4194304 | tf_op jit(solution)/shard_map/psum | solution.py:92
  23.4 52.9 %copy-start.8 = (bf16[512,512]{0,1:T(8,128)(2,1)S(1)}, bf16[512,512]{0,1:T(8,128)(2,1)}, u32[]{:S(2)}) copy-start(bf16[512,512]{0,1:T(8,128)(2,1)} %copy-done.7) | copy-start | bytes 1572868
  84.1 218.6 %reduce-scatter.5.cloned.1.call-start = ((), (), s32[]{:S(2)}) async-start(), calls=%async_computation.6 | async-start | bytes 5242880 | tf_op jit(solution)/shard_map/reduce_scatter | solution.py:120
  87.3 51.8 %copy-start.3 = (bf16[512,2048]{1,0:T(8,128)(2,1)S(1)}, bf16[512,2048]{1,0:T(8,128)(2,1)}, u32[]{:S(2)}) copy-start(bf16[512,2048]{1,0:T(8,128)(2,1)} %param.14) | copy-start | bytes 6291460
  134.1 5.0 %copy-start.4 = (bf16[512,2048]{1,0:T(8,128)(2,1)S(1)}, bf16[512,2048]{1,0:T(8,128)(2,1)}, u32[]{:S(2)}) copy-start(bf16[512,2048]{1,0:T(8,128)(2,1)} %all-reduce.3.cloned.1.call-done) | copy-start | bytes 6291460
  139.8 1.4 copy-start.5
  150.1 103.7 %slice-start.2 = ((s8[8388608]{0:T(1024)(128)(4,1)}), s8[4194304]{0:T(1024)(128)(4,1)S(1)}, s32[]{:S(2)}) async-start(s8[8388608]{0:T(1024)(128)(4,1)} %bitcast.107), calls=%async_computation.10 | async-start | bytes 8388608
  248.8 5.0 %slice-start.3 = ((s8[8388608]{0:T(1024)(128)(4,1)}), s8[4194304]{0:T(1024)(128)(4,1)S(1)}, s32[]{:S(2)}) async-start(s8[8388608]{0:T(1024)(128)(4,1)} %bitcast.107), calls=%async_computation.11 | async-start | bytes 8388608
  248.8 6.4 %slice-start = ((s8[8388608]{0:T(1024)(128)(4,1)}), s8[4194304]{0:T(1024)(128)(4,1)S(1)}, s32[]{:S(2)}) async-start(s8[8388608]{0:T(1024)(128)(4,1)} %bitcast.90), calls=%async_computation.8 | async-start | bytes 8388608
  253.8 2.4 slice-start.1
  259.7 1.6 copy-start.6
  259.7 1.9 copy-start.11
  259.8 76.9 %reduce-scatter.3.cloned.1.call-start = ((), (), s32[]{:S(2)}) async-start(), calls=%async_computation.5 | async-start | bytes 2621440 | tf_op jit(solution)/shard_map/reduce_scatter | solution.py:131
  302.7 31.3 %all-to-all-start.1 = ((bf16[64,16,512]{2,1,0:T(8,128)(2,1)}), bf16[64,16,512]{2,1,0:T(8,128)(2,1)S(1)}, u32[]{:S(2)}, u32[]{:S(2)}) async-start(bf16[64,16,512]{2,1,0:T(8,128)(2,1)} %reduce-scatter.5.cloned.1.call-done), calls=%async_computation.3 | async-start | bytes 2097152 | tf_op jit(solution)/shard_map/all_to_all | solution.py:123
  308.2 30.9 %copy-start.1 = (bf16[512,2048]{1,0:T(8,128)(2,1)S(1)}, bf16[512,2048]{1,0:T(8,128)(2,1)}, u32[]{:S(2)}) copy-start(bf16[512,2048]{1,0:T(8,128)(2,1)} %param.18) | copy-start | bytes 6291460
Sparse Core Ops, SparseCore 0:
  15.2 51.9 all-gather.2
  84.2 49.8 all-reduce.2
  259.9 42.7 reduce-scatter.4
  305.1 31.3 reduce-scatter.2
where the time goes:
time: 346 us
  waiting for transfers between devices  150 us (43%)
  blocking collectives  98.7 us (29%)
  matrix products  35.4 us (10%)
  other arithmetic  23.7 us (7%)
  local copies, waits for them, and re-layouts  18.3 us (5%)
  between operations  13.5 us (4%)
  starting transfers between devices  5.62 us (2%)
    all_to_all x1, blocking collectives, shards(): lax.all_to_all(outgoing, 'seq', split_axis=0, concat_axis=0, tiled=True)  98.7 us
    psum x1, waiting for transfers between devices, shards(): lax.psum(head_term.astype(jnp.bfloat16), 'head').astype(jnp.float32)  46.8 us
    all_gather x1, waiting for transfers between devices, prefix(): everything = lax.all_gather(array, axis)  43.7 us
    reduce_scatter x1, waiting for transfers between devices, shards(): lax.psum_scatter(result.astype(jnp.float32).astype(jnp.bfloat16), 'head',...  34 us
    all_to_all x1, waiting for transfers between devices, shards(): lax.all_to_all(reduced, 'seq', split_axis=0, concat_axis=0, tiled=True)  25.8 us
    select_n x8, other arithmetic, hop(): return jnp.where(reached, new, before)  8.32 us
  transfers between devices with their start and end apart: 5, of which 4 were waited for; matrix products, arithmetic and copies ran while one was open for 6% of the time, Pallas kernels for 0%

commit v1 on v0

v1 whole, which is shorter than its diff:
```python
import jax
import jax.numpy as jnp
from jax import lax
from jax.sharding import PartitionSpec as P

HD = 128
CAP = 16
EPS = 1e-06
CHUNKS = 2
BF16 = jnp.bfloat16
F32 = jnp.float32


def bits_of(size):
    return size.bit_length() - 1


def bit_reverse(value, size):
    out = value * 0
    for bit in range(bits_of(size)):
        out = out | (((value >> bit) & 1) << (bits_of(size) - 1 - bit))
    return out


def swap(array, axis, mask):
    size = lax.axis_size(axis)
    return lax.ppermute(array, axis, [(i, i ^ mask) for i in range(size)])


def exclusive_sum(state):
    size, mine = lax.axis_size("seq"), lax.axis_index("seq")
    total, before = state, jnp.zeros_like(state)
    for bit in range(bits_of(size)):
        got = swap(total.astype(BF16), "seq", 1 << bit).astype(F32)
        before = before + jnp.where((mine >> bit) & 1 == 1, got, 0.0)
        total = total + got
    return before


def halve(partial, dim):
    for bit in range(bits_of(lax.axis_size("head"))):
        half = partial.shape[dim] // 2
        keep = lax.slice_in_dim(partial, 0, half, axis=dim)
        send = lax.slice_in_dim(partial, half, 2 * half, axis=dim).astype(BF16)
        partial = keep + swap(send, "head", 1 << bit).astype(F32)
    return partial


def double(array, dim):
    for bit in reversed(range(bits_of(lax.axis_size("head")))):
        array = jnp.concatenate([array, swap(array, "head", 1 << bit)], axis=dim)
    return array


def exchange(blocks):
    parts = [blocks[0]]
    for k in range(1, lax.axis_size("seq")):
        parts.append(swap(blocks[k], "seq", k))
    return jnp.stack(parts)


def one_hot(index, size):
    return (jnp.arange(size, dtype=jnp.int32)[:, None] == index[None, :]).astype(BF16)


def shards(
    tokens,
    w_query,
    w_key,
    w_value,
    w_out,
    shared_gate,
    shared_up,
    shared_down,
    expert_gate,
    expert_up,
    expert_down,
    expert_ids,
):
    n_seq, n_head = lax.axis_size("seq"), lax.axis_size("head")
    mine, head = lax.axis_index("seq"), lax.axis_index("head")
    rows, width = tokens.shape
    heads_here = w_query.shape[1] // HD
    experts_here = expert_gate.shape[0]
    part = rows // n_head
    cols = width // n_head
    slots = -(-CAP // n_head)
    chunks = min(CHUNKS, experts_here)
    group = experts_here // chunks

    ids = expert_ids[:, 0]
    order = jnp.arange(rows, dtype=jnp.int32)
    start = jnp.sum((ids[None, :] < ids[:, None]).astype(jnp.int32), axis=1)
    earlier = (ids[None, :] == ids[:, None]) & (order[None, :] < order[:, None])
    rank = jnp.sum(earlier.astype(jnp.int32), axis=1)
    place = start + rank
    quarter = place % n_head
    rel = bit_reverse(quarter ^ head, n_head)
    row = rel * part + place // n_head
    here = order[:, None] == row[None, :]
    deal = here.astype(BF16)
    came_from = jnp.sum(jnp.where(here, order[None, :], 0), axis=1)
    slot = rank // n_head
    owner = (ids // experts_here) ^ mine
    local = ids % experts_here
    cell = (((local // group) * n_seq + owner) * group + local % group) * slots + slot
    own_cell = jnp.sum(jnp.where(here[:part], cell[None, :], 0), axis=1)
    cells = chunks * n_seq * group * slots
    pack = one_hot(own_cell, cells).reshape(chunks, cells // chunks, part)
    back_row = (
        (((local // group) * n_seq + owner) * group + local % group) * n_head + quarter
    ) * slots + slot
    back_rows = cells * n_head
    unpack = (back_row[:, None] == jnp.arange(back_rows, dtype=jnp.int32)[None, :]).astype(BF16)

    block = n_head * group * slots
    at = jnp.arange(block, dtype=jnp.int32)
    at_head = bit_reverse(at // (group * slots), n_head) ^ head
    at_expert = (at // slots) % group
    regroup = one_hot((at_expert * n_head + at_head) * slots + at % slots, block)

    down = jnp.concatenate(
        [
            lax.dynamic_slice_in_dim(
                expert_down, (bit_reverse(i, n_head) ^ head) * cols, cols, 2
            )
            for i in range(n_head)
        ],
        axis=2,
    )
    shared_out = jnp.concatenate(
        [
            lax.dynamic_slice_in_dim(
                shared_down, (bit_reverse(i, n_head) ^ head) * cols, cols, 1
            )
            for i in range(n_head)
        ],
        axis=1,
    )

    inputs = tokens.astype(F32)
    scale = lax.rsqrt(jnp.mean(inputs * inputs, axis=-1, keepdims=True) + EPS)

    def project(weights):
        return (jnp.dot(tokens, weights, preferred_element_type=F32) * scale).astype(BF16)

    key_rows = project(w_key).reshape(rows, heads_here, HD)
    value_rows = project(w_value).reshape(rows, heads_here, HD)
    state = jnp.einsum("thd,the->hde", key_rows, value_rows, preferred_element_type=F32)
    carried = exclusive_sum(state).astype(BF16)
    query_rows = jnp.dot(deal, project(w_query), preferred_element_type=F32)
    query_rows = query_rows.astype(BF16).reshape(rows, heads_here, HD)
    scores = jnp.einsum("thd,shd->hts", query_rows, key_rows, preferred_element_type=F32)
    causal = came_from[:, None] >= order[None, :]
    scores = jnp.where(causal[None], scores, 0.0).astype(BF16)
    attended = jnp.einsum("hts,shd->thd", scores, value_rows, preferred_element_type=F32)
    attended = attended + jnp.einsum(
        "thd,hde->the", query_rows, carried, preferred_element_type=F32
    )
    attended = attended * lax.rsqrt(jnp.mean(attended * attended, axis=-1, keepdims=True) + EPS)
    head_normed = attended.astype(BF16).reshape(rows, heads_here * HD)
    head_term = jnp.dot(head_normed, w_out, preferred_element_type=F32)
    own_tokens = jnp.dot(deal[:part], tokens, preferred_element_type=F32)
    residual = (own_tokens + halve(head_term, 0)).astype(BF16)

    returned = []
    for c in range(chunks):
        outgoing = jnp.dot(pack[c], residual, preferred_element_type=F32).astype(BF16)
        arrived = exchange(outgoing.reshape(n_seq, group * slots, width))
        arrived = double(arrived, 1)
        arrived = jnp.einsum(
            "krq,kqd->krd",
            jnp.broadcast_to(regroup[None], (n_seq, block, block)),
            arrived,
            preferred_element_type=F32,
        ).astype(BF16)
        values = arrived.astype(F32)
        norm = lax.rsqrt(jnp.mean(values * values, axis=-1, keepdims=True) + EPS)
        sorted_rows = arrived.reshape(n_seq, group, n_head * slots, width)
        norm_rows = norm.reshape(n_seq, group, n_head * slots, 1)
        span = slice(c * group, (c + 1) * group)

        def gated(gate, up, by):
            return (jax.nn.silu(gate * by) * (up * by)).astype(BF16)

        hidden = gated(
            jnp.einsum(
                "kecd,edf->kecf", sorted_rows, expert_gate[span], preferred_element_type=F32
            ),
            jnp.einsum("kecd,edf->kecf", sorted_rows, expert_up[span], preferred_element_type=F32),
            norm_rows,
        )
        flat = arrived.reshape(n_seq * block, width)
        shared = gated(
            jnp.dot(flat, shared_gate, preferred_element_type=F32),
            jnp.dot(flat, shared_up, preferred_element_type=F32),
            norm.reshape(n_seq * block, 1),
        )
        total = jnp.einsum("kecf,efd->kecd", hidden, down[span], preferred_element_type=F32)
        total = total.reshape(n_seq * block, width)
        total = total + jnp.dot(shared, shared_out, preferred_element_type=F32)
        total = halve(total, 1)
        total = total + lax.dynamic_slice_in_dim(flat, head * cols, cols, 1).astype(F32)
        back = exchange(total.astype(BF16).reshape(n_seq, block, cols))
        returned.append(back.reshape(n_seq * block, cols))
    result = jnp.dot(unpack, jnp.concatenate(returned), preferred_element_type=F32)
    return result.astype(BF16)


def solution(mesh):
    return jax.shard_map(
        shards,
        mesh=mesh,
        in_specs=(
            P("seq", None),
            P(None, "head"),
            P(None, "head"),
            P(None, "head"),
            P("head", None),
            P(None, "head"),
            P(None, "head"),
            P("head", None),
            P("seq", None, "head"),
            P("seq", None, "head"),
            P("seq", "head", None),
            P("seq", None),
        ),
        out_specs=P("seq", "head"),
        check_vma=False,
    )
```

time: 346 us -> 227 us (0.66)
  blocking collectives: 98.7 us -> 0 us
  waiting for transfers between devices: 150 us -> 66.9 us
  starting transfers between devices: 5.62 us -> 57.8 us
  matrix products: 35.4 us -> 60.6 us
  between operations: 13.5 us -> 0.57 us
  other arithmetic: 23.7 us -> 17.5 us
  local copies, waits for them, and re-layouts: 18.3 us -> 23.4 us
    all_to_all x1 -> x0, blocking collectives: 98.7 us -> none  [shards(): lax.all_to_all(outgoing, 'seq', split_axis=0, concat_axis=0, tiled=True)]
    ppermute x0 -> x41, waiting for transfers between devices: none -> 66.9 us  [swap(): return lax.ppermute(array, axis, [(i, i ^ mask) for i in range(size)])]
    ppermute x0 -> x41, starting transfers between devices: none -> 57.8 us  [swap(): return lax.ppermute(array, axis, [(i, i ^ mask) for i in range(size)])]
    psum x1 -> x0, waiting for transfers between devices: 46.8 us -> none  [shards(): lax.psum(head_term.astype(jnp.bfloat16), 'head').astype(jnp.float32)]
    all_gather x1 -> x0, waiting for transfers between devices: 43.7 us -> none  [prefix(): everything = lax.all_gather(array, axis)]
    reduce_scatter x2 -> x0, waiting for transfers between devices: 34 us -> none  [the longest x1 34 us: shards(): lax.psum_scatter(result.astype(jnp.float32).astype(jnp.bfloat16), 'head',...]
    all_to_all x1 -> x0, waiting for transfers between devices: 25.8 us -> none  [shards(): lax.all_to_all(reduced, 'seq', split_axis=0, concat_axis=0, tiled=True)]
    dot_general x13 -> x21, matrix products: 35.4 us -> 60.6 us  [the longest x2 14.5 us: shards(): total = total + jnp.dot(shared, shared_out, preferred_element_type=F32)]
  transfers between devices with their start and end apart: 5 -> 41, of which waited for: 4 -> 17; matrix products, arithmetic and copies ran while one was open for 6% -> 22% of each run, Pallas kernels for 0% -> 0%
where the time goes in v1:
time: 227 us
  waiting for transfers between devices  66.9 us (29%)
  matrix products  60.6 us (27%)
  starting transfers between devices  57.8 us (25%)
  local copies, waits for them, and re-layouts  23.4 us (10%)
  other arithmetic  17.5 us (8%)
    ppermute x41, waiting for transfers between devices, swap(): return lax.ppermute(array, axis, [(i, i ^ mask) for i in range(size)])  66.9 us
    ppermute x41, starting transfers between devices, swap(): return lax.ppermute(array, axis, [(i, i ^ mask) for i in range(size)])  57.8 us
    dot_general x2, matrix products, shards(): total = total + jnp.dot(shared, shared_out, preferred_element_type=F32)  14.5 us
    dot_general x2, matrix products, shards(): jnp.einsum('kecf,efd->kecd', hidden, down[span], preferred_element_type=F32)  14.2 us
    transpose x2, local copies, waits for them, and re-layouts, shards(): jnp.einsum('kecf,efd->kecd', hidden, down[span], preferred_element_type=F32)  9.62 us
    dot_general x2, matrix products, shards(): jnp.einsum('kecd,edf->kecf', sorted_rows, expert_gate[span], preferred_el...  7.45 us
    slice x6, local copies, waits for them, and re-layouts, halve(): send = lax.slice_in_dim(partial, half, 2 * half, axis=dim).astype(BF16)  4.98 us
    add x3, other arithmetic, halve(): partial = keep + swap(send, 'head', 1 << bit).astype(F32)  4.95 us
  transfers between devices with their start and end apart: 41, of which 17 were waited for; matrix products, arithmetic and copies ran while one was open for 22% of the time, Pallas kernels for 0%

profile of v1, /device:TPU:0, one launch (start us, length us, event | category | flops | bytes accessed | tf_op | source)
XLA Modules:
  0.0 226.9 jit_solution(8206026080444447030)
XLA Ops:
  2.4 3.1 %fusion.34 = bf16[512,512]{0,1:T(8,128)(2,1)S(1)} fusion(bf16[512,2048]{1,0:T(8,128)(2,1)S(1)} %copy-done.4, bf16[2048,512]{1,0:T(8,128)(2,1)} %param.15, f32[512]{0:T(512)S(1)} %add_rsqrt_fusion.3), kind=kOutput, calls=%fused_computation.59 | convolution fusion | flops 1074266112 | bytes 4720640 | tf_op jit(solution)/shard_map/dot_general | solution.py:145
  7.6 3.0 %collective-permute-start = (bf16[4,128,128]{2,1,0:T(8,128)(2,1)S(1)}, bf16[4,128,128]{2,1,0:T(8,128)(2,1)S(1)}, u32[]{:S(2)}, u32[]{:S(2)}) collective-permute-start(bf16[4,128,128]{2,1,0:T(8,128)(2,1)S(1)} %get-tuple-element.45), channel_id=1, source_target_pairs={{0,4},{4,0},{8,12},{12,8},{16,20},{20,16},{24,28},{28,24},{1,5},{5... | collective-permute-start | bytes 393224 | tf_op jit(solution)/shard_map/ppermute | solution.py:27
  11.5 4.6 %convolution_convert_fusion.4 = bf16[512,512]{0,1:T(8,128)(2,1)} fusion(bf16[512,2048]{1,0:T(8,128)(2,1)} %param.12, bf16[2048,512]{1,0:T(8,128)(2,1)} %param.13, f32[512]{0:T(512)S(1)} %add_rsqrt_fusion.3, s32[512]{0:T(512)S(1)} %get-tuple-element.44), kind=kOutput, calls=%fused_computation.58 | convolution fusion | flops 1343225856 | bytes 4722688 | tf_op jit(solution)/shard_map/dot_general | solution.py:151
  18.9 2.5 %collective-permute-done.1 = bf16[4,128,128]{2,1,0:T(8,128)(2,1)S(1)} collective-permute-done((bf16[4,128,128]{2,1,0:T(8,128)(2,1)S(1)}, bf16[4,128,128]{2,1,0:T(8,128)(2,1)S(1)}, u32[]{:S(2)}, u32[]{:S(2)}) %collective-permute-start.1) | collective-permute-done | bytes 131104 | tf_op jit(solution)/shard_map/ppermute | solution.py:27
  22.1 2.6 %collective-permute-start.2 = (bf16[4,128,128]{2,1,0:T(8,128)(2,1)}, bf16[4,128,128]{2,1,0:T(8,128)(2,1)S(1)}, u32[]{:S(2)}, u32[]{:S(2)}) collective-permute-start(bf16[4,128,128]{2,1,0:T(8,128)(2,1)} %fusion.145), channel_id=1, source_target_pairs={{0,16},{4,20},{8,24},{12,28},{16,0},{20,4},{24,8},{28,12},{1,17},{... | collective-permute-start | bytes 393224 | tf_op jit(solution)/shard_map/ppermute | solution.py:27
  24.7 2.8 %fusion.31 = f32[4,128,512]{2,1,0:T(8,128)S(1)} fusion(bf16[512,4,128]{0,2,1:T(8,128)(2,1)} %bitcast.223, bf16[512,4,128]{0,2,1:T(8,128)(2,1)} %bitcast.226, bf16[512,4,128]{0,2,1:T(8,128)(2,1)} %bitcast.225, pred[512,512]{1,0:T(8,128)(4,1)} %iota_compare_fusion.4), kind=kOutput, calls=%fused_computation.51 | convolution fusion | flops 538968064 | bytes 2883584 | tf_op jit(solution)/shard_map/hts,shd->thd/dot_general | solution.py:156
  42.2 4.4 %constant_dynamic-slice_fusion.7 = (bf16[8,256,512]{2,1,0:T(8,128)(2,1)S(1)}, bf16[8,256,512]{2,1,0:T(8,128)(2,1)S(1)}, bf16[8,256,512]{2,1,0:T(8,128)(2,1)S(1)}, bf16[8,256,512]{2,1,0:T(8,128)(2,1)S(1)}) fusion(bf16[8,256,2048]{2,1,0:T(8,128)(2,1)} %param.22, s32[]{:T(128)S(6)} %select_n.180, s32[]{:T(128)S(6)} %select_n.181, s32[]{:T(128)S(6)} %select_n.183, ...), kind=kLoop, calls=%fused_computation.245 | loop fusion | bytes 16777232 | tf_op jit(solution)/shard_map/dynamic_slice | solution.py:124
  46.6 8.0 %collective-permute-done.4 = bf16[128,2048]{1,0:T(8,128)(2,1)S(1)} collective-permute-done((bf16[128,2048]{1,0:T(8,128)(2,1)S(1)}, bf16[128,2048]{1,0:T(8,128)(2,1)S(1)}, u32[]{:S(2)}, u32[]{:S(2)}) %collective-permute-start.4) | collective-permute-done | bytes 524320 | tf_op jit(solution)/shard_map/ppermute | solution.py:27
  62.4 3.1 %collective-permute-start.28 = (bf16[16,2048]{1,0:T(8,128)(2,1)S(1)}, bf16[16,2048]{1,0:T(8,128)(2,1)S(1)}, u32[]{:S(2)}, u32[]{:S(2)}) collective-permute-start(bf16[16,2048]{1,0:T(8,128)(2,1)S(1)} %get-tuple-element.37), channel_id=1, source_target_pairs={{0,24},{4,28},{8,16},{12,20},{16,8},{20,12},{24,0},{28,4},{1,25},{... | collective-permute-start | bytes 196616 | tf_op jit(solution)/shard_map/ppermute | solution.py:27
  68.6 2.3 %collective-permute-done.27 = bf16[16,2048]{1,0:T(8,128)(2,1)S(1)} collective-permute-done((bf16[16,2048]{1,0:T(8,128)(2,1)S(1)}, bf16[16,2048]{1,0:T(8,128)(2,1)S(1)}, u32[]{:S(2)}, u32[]{:S(2)}) %collective-permute-start.27) | collective-permute-done | bytes 65568 | tf_op jit(solution)/shard_map/ppermute | solution.py:27
  70.9 4.3 %collective-permute-start.8 = (bf16[16,2048]{1,0:T(8,128)(2,1)S(1)}, bf16[16,2048]{1,0:T(8,128)(2,1)S(1)}, u32[]{:S(2)}, u32[]{:S(2)}) collective-permute-start(bf16[16,2048]{1,0:T(8,128)(2,1)S(1)} %get-tuple-element.25), channel_id=1, source_target_pairs={{0,16},{4,20},{8,24},{12,28},{16,0},{20,4},{24,8},{28,12},{1,17},{... | collective-permute-start | bytes 196616 | tf_op jit(solution)/shard_map/ppermute | solution.py:27
  77.8 3.0 %collective-permute-start.11 = (bf16[16,2048]{1,0:T(8,128)(2,1)S(1)}, bf16[16,2048]{1,0:T(8,128)(2,1)S(1)}, u32[]{:S(2)}, u32[]{:S(2)}) collective-permute-start(bf16[16,2048]{1,0:T(8,128)(2,1)S(1)} %get-tuple-element.22), channel_id=1, source_target_pairs={{0,28},{4,24},{8,20},{12,16},{16,12},{20,8},{24,4},{28,0},{1,29},{... | collective-permute-start | bytes 196616 | tf_op jit(solution)/shard_map/ppermute | solution.py:27
  86.5 9.2 %collective-permute-done.30 = bf16[8,16,2048]{2,1,0:T(8,128)(2,1)S(1)} collective-permute-done((bf16[8,16,2048]{2,1,0:T(8,128)(2,1)S(1)}, bf16[8,16,2048]{2,1,0:T(8,128)(2,1)S(1)}, u32[]{:S(2)}, u32[]{:S(2)}) %collective-permute-start.30) | collective-permute-done | bytes 524320 | tf_op jit(solution)/shard_map/ppermute | solution.py:27
  96.0 6.9 %collective-permute-done.12 = bf16[8,16,2048]{2,1,0:T(8,128)(2,1)S(1)} collective-permute-done((bf16[8,16,2048]{2,1,0:T(8,128)(2,1)S(1)}, bf16[8,16,2048]{2,1,0:T(8,128)(2,1)S(1)}, u32[]{:S(2)}, u32[]{:S(2)}) %collective-permute-start.12) | collective-permute-done | bytes 524320 | tf_op jit(solution)/shard_map/ppermute | solution.py:27
  104.0 4.0 %pad_maximum_fusion = bf16[8,256,2048]{2,1,0:T(8,128)(2,1)} fusion(bf16[8,256,512]{2,1,0:T(8,128)(2,1)S(1)} %get-tuple-element.9, bf16[8,256,512]{2,1,0:T(8,128)(2,1)S(1)} %get-tuple-element.10, bf16[8,256,512]{2,1,0:T(8,128)(2,1)S(1)} %get-tuple-element.8, bf16[8,256,512]{2,1,0:T(8,128)(2,1)S(1)} %get-tuple-element.7), kind=kLoop, calls=%fused_computation | loop fusion | flops 33554432 | bytes 16777216 | tf_op jit(solution)/shard_map/concatenate | solution.py:122
  109.0 4.1 %multiply_reduce_fusion.1 = (f32[8,64]{1,0:T(8,128)S(1)}, bf16[8,64,2048]{2,1,0:T(8,128)(2,1)}) fusion(bf16[8,32,2048]{2,1,0:T(8,128)(2,1)} %collective-permute-done.13, bf16[8,16,2048]{2,1,0:T(8,128)(2,1)} %copy-done.15, bf16[8,16,2048]{2,1,0:T(8,128)(2,1)} %copy-done.12, bf16[64,64]{1,0:T(8,128)(2,1)S(1)} %fusion.166), kind=kOutput, calls=%fused_computation.19 | convolution fusion | flops 144702976 | bytes 4204544 | tf_op jit(solution)/shard_map/krq,kqd->krd/dot_general | solution.py:171
  113.3 3.7 %fusion.64 = f32[8,4,16,256]{3,2,0,1:T(8,128)} fusion(bf16[8,2048,256]{2,1,0:T(8,128)(2,1)} %param.20, bf16[8,4,16,2048]{3,2,1,0:T(8,128)(2,1)S(1)} %bitcast.211, f32[8,4,16]{2,0,1:T(8,128)S(1)} %copy.38), kind=kOutput, calls=%fused_computation.73 | convolution fusion | flops 537001984 | bytes 6817792 | tf_op jit(solution)/shard_map/kecd,edf->kecf/dot_general | solution.py:187
  117.0 6.9 %fusion.15 = f32[8,4,16,2048]{3,2,0,1:T(8,128)} fusion(bf16[8,256,2048]{2,1,0:T(8,128)(2,1)} %pad_maximum_fusion, bf16[8,2048,256]{2,1,0:T(8,128)(2,1)} %param.21, bf16[8,4,16,2048]{3,2,1,0:T(8,128)(2,1)S(1)} %bitcast.212, f32[8,4,16,256]{3,2,0,1:T(8,128)} %fusion.64, f32[8,4,16]{2,0,1:T(8,128)S(1)} %copy.38), kind=kOutput, calls=%fused_computation.24 | convolution fusion | flops 1074659328 | bytes 15206400 | tf_op jit(solution)/shard_map/kecf,efd->kecd/dot_general | solution.py:199
  123.9 4.8 %copy.40 = f32[8,4,16,2048]{3,2,1,0:T(8,128)} copy(f32[8,4,16,2048]{3,2,0,1:T(8,128)} %fusion.15) | data formatting | bytes 8388608 | tf_op jit(solution)/shard_map/kecf,efd->kecd/transpose | solution.py:199
  129.8 7.2 %bitcast_add_fusion = f32[512,2048]{1,0:T(8,128)} fusion(f32[8,4,16,2048]{3,2,1,0:T(8,128)} %copy.40, bf16[512,2048]{1,0:T(8,128)(2,1)} %bitcast.213, bf16[2048,256]{1,0:T(8,128)(2,1)S(1)} %copy-done.6, f32[512,256]{1,0:T(8,128)S(1)} %convolution_multiply_fusion.4, f32[512]{0:T(512)S(1)} %rsqrt.61, bf16[256,512]{1,0:T(8,128)(2,1)S(1)} %get-tuple-element.13, ...), kind=kOutput, calls=%fused_computation.13 | convolution fusion | flops 1079902208 | bytes 13109248 | tf_op jit(solution)/shard_map/dot_general | solution.py:201
  139.5 3.7 %fusion.74 = f32[8,4,16,256]{3,2,0,1:T(8,128)} fusion(bf16[8,2048,256]{2,1,0:T(8,128)(2,1)} %param.20, bf16[8,4,16,2048]{3,2,1,0:T(8,128)(2,1)S(1)} %bitcast.219, f32[8,4,16]{2,0,1:T(8,128)S(1)} %copy.34), kind=kOutput, calls=%fused_computation.75 | convolution fusion | flops 537001984 | bytes 6817792 | tf_op jit(solution)/shard_map/kecd,edf->kecf/dot_general | solution.py:187
  143.3 7.3 %fusion.14 = f32[8,4,16,2048]{3,2,0,1:T(8,128)} fusion(bf16[8,256,2048]{2,1,0:T(8,128)(2,1)} %pad_maximum_fusion, bf16[8,2048,256]{2,1,0:T(8,128)(2,1)} %param.21, bf16[8,4,16,2048]{3,2,1,0:T(8,128)(2,1)} %bitcast.216, f32[8,4,16,256]{3,2,0,1:T(8,128)} %fusion.74, f32[8,4,16]{2,0,1:T(8,128)S(1)} %copy.34), kind=kOutput, calls=%fused_computation.23 | convolution fusion | flops 1074659328 | bytes 15206400 | tf_op jit(solution)/shard_map/kecf,efd->kecd/dot_general | solution.py:199
  150.6 4.9 %copy.36 = f32[8,4,16,2048]{3,2,1,0:T(8,128)} copy(f32[8,4,16,2048]{3,2,0,1:T(8,128)} %fusion.14) | data formatting | bytes 8388608 | tf_op jit(solution)/shard_map/kecf,efd->kecd/transpose | solution.py:199
  157.0 7.3 %bitcast_add_fusion.1 = f32[512,2048]{1,0:T(8,128)} fusion(f32[8,4,16,2048]{3,2,1,0:T(8,128)} %copy.36, bf16[512,2048]{1,0:T(8,128)(2,1)} %bitcast.217, bf16[2048,256]{1,0:T(8,128)(2,1)S(1)} %copy-done.6, f32[512,256]{1,0:T(8,128)} %convolution_multiply_fusion.6, f32[512]{0:T(512)S(1)} %rsqrt.58, bf16[256,512]{1,0:T(8,128)(2,1)S(1)} %get-tuple-element.13, ...), kind=kOutput, calls=%fused_computation.14 | convolution fusion | flops 1079902208 | bytes 13109248 | tf_op jit(solution)/shard_map/dot_general | solution.py:201
  166.3 2.5 %slice_add_fusion = f32[512,1024]{1,0:T(8,128)S(1)} fusion(f32[512,2048]{1,0:T(8,128)} %bitcast_add_fusion, bf16[512,1024]{1,0:T(8,128)(2,1)} %collective-permute-done.32), kind=kLoop, calls=%fused_computation.30 | loop fusion | flops 1048576 | bytes 5242880 | tf_op jit(solution)/shard_map/add | solution.py:45
  171.8 11.9 %collective-permute-done.33 = bf16[512,512]{1,0:T(8,128)(2,1)S(1)} collective-permute-done((bf16[512,512]{1,0:T(8,128)(2,1)S(1)}, bf16[512,512]{1,0:T(8,128)(2,1)S(1)}, u32[]{:S(2)}, u32[]{:S(2)}) %collective-permute-start.33) | collective-permute-done | bytes 524320 | tf_op jit(solution)/shard_map/ppermute | solution.py:27
  183.7 10.6 %collective-permute-done.15 = bf16[512,512]{1,0:T(8,128)(2,1)S(1)} collective-permute-done((bf16[512,512]{1,0:T(8,128)(2,1)S(1)}, bf16[512,512]{1,0:T(8,128)(2,1)S(1)}, u32[]{:S(2)}, u32[]{:S(2)}) %collective-permute-start.15) | collective-permute-done | bytes 524320 | tf_op jit(solution)/shard_map/ppermute | solution.py:27
  200.8 2.7 %collective-permute-start.38 = (bf16[64,512]{1,0:T(8,128)(2,1)S(1)}, bf16[64,512]{1,0:T(8,128)(2,1)S(1)}, u32[]{:S(2)}, u32[]{:S(2)}) collective-permute-start(bf16[64,512]{1,0:T(8,128)(2,1)S(1)} %get-tuple-element.31), channel_id=1, source_target_pairs={{0,20},{4,16},{8,28},{12,24},{16,4},{20,0},{24,12},{28,8},{1,21},{... | collective-permute-start | bytes 196616 | tf_op jit(solution)/shard_map/ppermute | solution.py:27
  204.6 2.8 %collective-permute-start.40 = (bf16[64,512]{1,0:T(8,128)(2,1)S(1)}, bf16[64,512]{1,0:T(8,128)(2,1)S(1)}, u32[]{:S(2)}, u32[]{:S(2)}) collective-permute-start(bf16[64,512]{1,0:T(8,128)(2,1)S(1)} %get-tuple-element.29), channel_id=1, source_target_pairs={{0,28},{4,24},{8,20},{12,16},{16,12},{20,8},{24,4},{28,0},{1,29},{... | collective-permute-start | bytes 196616 | tf_op jit(solution)/shard_map/ppermute | solution.py:27
  209.1 3.3 %collective-permute-done.38 = bf16[64,512]{1,0:T(8,128)(2,1)S(1)} collective-permute-done((bf16[64,512]{1,0:T(8,128)(2,1)S(1)}, bf16[64,512]{1,0:T(8,128)(2,1)S(1)}, u32[]{:S(2)}, u32[]{:S(2)}) %collective-permute-start.38) | collective-permute-done | bytes 65568 | tf_op jit(solution)/shard_map/ppermute | solution.py:27
  212.5 3.2 %collective-permute-start.19 = (bf16[64,512]{1,0:T(8,128)(2,1)S(1)}, bf16[64,512]{1,0:T(8,128)(2,1)S(1)}, u32[]{:S(2)}, u32[]{:S(2)}) collective-permute-start(bf16[64,512]{1,0:T(8,128)(2,1)S(1)} %get-tuple-element.18), channel_id=1, source_target_pairs={{0,16},{4,20},{8,24},{12,28},{16,0},{20,4},{24,8},{28,12},{1,17},{... | collective-permute-start | bytes 196616 | tf_op jit(solution)/shard_map/ppermute | solution.py:27
  218.2 2.4 %collective-permute-start.22 = (bf16[64,512]{1,0:T(8,128)(2,1)S(1)}, bf16[64,512]{1,0:T(8,128)(2,1)S(1)}, u32[]{:S(2)}, u32[]{:S(2)}) collective-permute-start(bf16[64,512]{1,0:T(8,128)(2,1)S(1)} %get-tuple-element.15), channel_id=1, source_target_pairs={{0,28},{4,24},{8,20},{12,16},{16,12},{20,8},{24,4},{28,0},{1,29},{... | collective-permute-start | bytes 196616 | tf_op jit(solution)/shard_map/ppermute | solution.py:27
  (195 shorter events, 73.3 us)
Async XLA Ops:
  7.6 8.7 %collective-permute-start = (bf16[4,128,128]{2,1,0:T(8,128)(2,1)S(1)}, bf16[4,128,128]{2,1,0:T(8,128)(2,1)S(1)}, u32[]{:S(2)}, u32[]{:S(2)}) collective-permute-start(bf16[4,128,128]{2,1,0:T(8,128)(2,1)S(1)} %get-tuple-element.45), channel_id=1, source_target_pairs={{0,4},{4,0},{8,12},{12,8},{16,20},{20,16},{24,28},{28,24},{1,5},{5... | collective-permute-start | bytes 393224 | tf_op jit(solution)/shard_map/ppermute | solution.py:27
  22.1 7.7 %collective-permute-start.2 = (bf16[4,128,128]{2,1,0:T(8,128)(2,1)}, bf16[4,128,128]{2,1,0:T(8,128)(2,1)S(1)}, u32[]{:S(2)}, u32[]{:S(2)}) collective-permute-start(bf16[4,128,128]{2,1,0:T(8,128)(2,1)} %fusion.145), channel_id=1, source_target_pairs={{0,16},{4,20},{8,24},{12,28},{16,0},{20,4},{24,8},{28,12},{1,17},{... | collective-permute-start | bytes 393224 | tf_op jit(solution)/shard_map/ppermute | solution.py:27
  40.6 14.0 %collective-permute-start.4 = (bf16[128,2048]{1,0:T(8,128)(2,1)S(1)}, bf16[128,2048]{1,0:T(8,128)(2,1)S(1)}, u32[]{:S(2)}, u32[]{:S(2)}) collective-permute-start(bf16[128,2048]{1,0:T(8,128)(2,1)S(1)} %slice.414), channel_id=1, source_target_pairs={{0,2},{1,3},{2,0},{3,1},{4,6},{5,7},{6,4},{7,5},{8,10},{9,11},{10,... | collective-permute-start | bytes 1572872 | tf_op jit(solution)/shard_map/ppermute | solution.py:27
  56.5 9.0 %collective-permute-start.24 = (bf16[16,2048]{1,0:T(8,128)(2,1)S(1)}, bf16[16,2048]{1,0:T(8,128)(2,1)S(1)}, u32[]{:S(2)}, u32[]{:S(2)}) collective-permute-start(bf16[16,2048]{1,0:T(8,128)(2,1)S(1)} %get-tuple-element.41), channel_id=1, source_target_pairs={{0,8},{4,12},{8,0},{12,4},{16,24},{20,28},{24,16},{28,20},{1,9},{5... | collective-permute-start | bytes 196616 | tf_op jit(solution)/shard_map/ppermute | solution.py:27
  56.9 10.0 %collective-permute-start.25 = (bf16[16,2048]{1,0:T(8,128)(2,1)S(1)}, bf16[16,2048]{1,0:T(8,128)(2,1)S(1)}, u32[]{:S(2)}, u32[]{:S(2)}) collective-permute-start(bf16[16,2048]{1,0:T(8,128)(2,1)S(1)} %get-tuple-element.40), channel_id=1, source_target_pairs={{0,12},{4,8},{8,4},{12,0},{16,28},{20,24},{24,20},{28,16},{1,13},{... | collective-permute-start | bytes 196616 | tf_op jit(solution)/shard_map/ppermute | solution.py:27
  59.1 9.5 %collective-permute-start.26 = (bf16[16,2048]{1,0:T(8,128)(2,1)S(1)}, bf16[16,2048]{1,0:T(8,128)(2,1)S(1)}, u32[]{:S(2)}, u32[]{:S(2)}) collective-permute-start(bf16[16,2048]{1,0:T(8,128)(2,1)S(1)} %get-tuple-element.39), channel_id=1, source_target_pairs={{0,16},{4,20},{8,24},{12,28},{16,0},{20,4},{24,8},{28,12},{1,17},{... | collective-permute-start | bytes 196616 | tf_op jit(solution)/shard_map/ppermute | solution.py:27
  61.2 9.7 %collective-permute-start.27 = (bf16[16,2048]{1,0:T(8,128)(2,1)S(1)}, bf16[16,2048]{1,0:T(8,128)(2,1)S(1)}, u32[]{:S(2)}, u32[]{:S(2)}) collective-permute-start(bf16[16,2048]{1,0:T(8,128)(2,1)S(1)} %get-tuple-element.38), channel_id=1, source_target_pairs={{0,20},{4,16},{8,28},{12,24},{16,4},{20,0},{24,12},{28,8},{1,21},{... | collective-permute-start | bytes 196616 | tf_op jit(solution)/shard_map/ppermute | solution.py:27
  62.4 8.5 %collective-permute-start.28 = (bf16[16,2048]{1,0:T(8,128)(2,1)S(1)}, bf16[16,2048]{1,0:T(8,128)(2,1)S(1)}, u32[]{:S(2)}, u32[]{:S(2)}) collective-permute-start(bf16[16,2048]{1,0:T(8,128)(2,1)S(1)} %get-tuple-element.37), channel_id=1, source_target_pairs={{0,24},{4,28},{8,16},{12,20},{16,8},{20,12},{24,0},{28,4},{1,25},{... | collective-permute-start | bytes 196616 | tf_op jit(solution)/shard_map/ppermute | solution.py:27
  65.5 9.7 %collective-permute-start.29 = (bf16[16,2048]{1,0:T(8,128)(2,1)S(1)}, bf16[16,2048]{1,0:T(8,128)(2,1)S(1)}, u32[]{:S(2)}, u32[]{:S(2)}) collective-permute-start(bf16[16,2048]{1,0:T(8,128)(2,1)S(1)} %get-tuple-element.36), channel_id=1, source_target_pairs={{0,28},{4,24},{8,20},{12,16},{16,12},{20,8},{24,4},{28,0},{1,29},{... | collective-permute-start | bytes 196616 | tf_op jit(solution)/shard_map/ppermute | solution.py:27
  66.9 9.5 %collective-permute-start.5 = (bf16[16,2048]{1,0:T(8,128)(2,1)S(1)}, bf16[16,2048]{1,0:T(8,128)(2,1)S(1)}, u32[]{:S(2)}, u32[]{:S(2)}) collective-permute-start(bf16[16,2048]{1,0:T(8,128)(2,1)S(1)} %get-tuple-element.28), channel_id=1, source_target_pairs={{0,4},{4,0},{8,12},{12,8},{16,20},{20,16},{24,28},{28,24},{1,5},{5... | collective-permute-start | bytes 196616 | tf_op jit(solution)/shard_map/ppermute | solution.py:27
  68.6 9.2 %collective-permute-start.6 = (bf16[16,2048]{1,0:T(8,128)(2,1)S(1)}, bf16[16,2048]{1,0:T(8,128)(2,1)S(1)}, u32[]{:S(2)}, u32[]{:S(2)}) collective-permute-start(bf16[16,2048]{1,0:T(8,128)(2,1)S(1)} %get-tuple-element.27), channel_id=1, source_target_pairs={{0,8},{4,12},{8,0},{12,4},{16,24},{20,28},{24,16},{28,20},{1,9},{5... | collective-permute-start | bytes 196616 | tf_op jit(solution)/shard_map/ppermute | solution.py:27
  70.9 9.8 %collective-permute-start.7 = (bf16[16,2048]{1,0:T(8,128)(2,1)S(1)}, bf16[16,2048]{1,0:T(8,128)(2,1)S(1)}, u32[]{:S(2)}, u32[]{:S(2)}) collective-permute-start(bf16[16,2048]{1,0:T(8,128)(2,1)S(1)} %get-tuple-element.26), channel_id=1, source_target_pairs={{0,12},{4,8},{8,4},{12,0},{16,28},{20,24},{24,20},{28,16},{1,13},{... | collective-permute-start | bytes 196616 | tf_op jit(solution)/shard_map/ppermute | solution.py:27
  70.9 11.0 %collective-permute-start.8 = (bf16[16,2048]{1,0:T(8,128)(2,1)S(1)}, bf16[16,2048]{1,0:T(8,128)(2,1)S(1)}, u32[]{:S(2)}, u32[]{:S(2)}) collective-permute-start(bf16[16,2048]{1,0:T(8,128)(2,1)S(1)} %get-tuple-element.25), channel_id=1, source_target_pairs={{0,16},{4,20},{8,24},{12,28},{16,0},{20,4},{24,8},{28,12},{1,17},{... | collective-permute-start | bytes 196616 | tf_op jit(solution)/shard_map/ppermute | solution.py:27
  75.2 8.5 %collective-permute-start.9 = (bf16[16,2048]{1,0:T(8,128)(2,1)S(1)}, bf16[16,2048]{1,0:T(8,128)(2,1)S(1)}, u32[]{:S(2)}, u32[]{:S(2)}) collective-permute-start(bf16[16,2048]{1,0:T(8,128)(2,1)S(1)} %get-tuple-element.24), channel_id=1, source_target_pairs={{0,20},{4,16},{8,28},{12,24},{16,4},{20,0},{24,12},{28,8},{1,21},{... | collective-permute-start | bytes 196616 | tf_op jit(solution)/shard_map/ppermute | solution.py:27
  76.4 7.4 %collective-permute-start.10 = (bf16[16,2048]{1,0:T(8,128)(2,1)S(1)}, bf16[16,2048]{1,0:T(8,128)(2,1)S(1)}, u32[]{:S(2)}, u32[]{:S(2)}) collective-permute-start(bf16[16,2048]{1,0:T(8,128)(2,1)S(1)} %get-tuple-element.23), channel_id=1, source_target_pairs={{0,24},{4,28},{8,16},{12,20},{16,8},{20,12},{24,0},{28,4},{1,25},{... | collective-permute-start | bytes 196616 | tf_op jit(solution)/shard_map/ppermute | solution.py:27
  80.7 14.9 %collective-permute-start.30 = (bf16[8,16,2048]{2,1,0:T(8,128)(2,1)S(1)}, bf16[8,16,2048]{2,1,0:T(8,128)(2,1)S(1)}, u32[]{:S(2)}, u32[]{:S(2)}) collective-permute-start(bf16[8,16,2048]{2,1,0:T(8,128)(2,1)S(1)} %constant_dynamic-update-slice_fusion.16), channel_id=1, source_target_pairs={{0,2},{1,3},{2,0},{3,1},{4,6},{5,7},{6,4},{7,5},{8,10},{9,11},{10,... | collective-permute-start | bytes 1572872 | tf_op jit(solution)/shard_map/ppermute | solution.py:27
  84.9 18.0 %collective-permute-start.12 = (bf16[8,16,2048]{2,1,0:T(8,128)(2,1)S(1)}, bf16[8,16,2048]{2,1,0:T(8,128)(2,1)S(1)}, u32[]{:S(2)}, u32[]{:S(2)}) collective-permute-start(bf16[8,16,2048]{2,1,0:T(8,128)(2,1)S(1)} %constant_dynamic-update-slice_fusion), channel_id=1, source_target_pairs={{0,2},{1,3},{2,0},{3,1},{4,6},{5,7},{6,4},{7,5},{8,10},{9,11},{10,... | collective-permute-start | bytes 1572872 | tf_op jit(solution)/shard_map/ppermute | solution.py:27
  95.8 12.3 %collective-permute-start.31 = (bf16[8,32,2048]{2,1,0:T(8,128)(2,1)S(1)}, bf16[8,32,2048]{2,1,0:T(8,128)(2,1)S(1)}, u32[]{:S(2)}, u32[]{:S(2)}) collective-permute-start(bf16[8,32,2048]{2,1,0:T(8,128)(2,1)S(1)} %pad_maximum_fusion.3), channel_id=1, source_target_pairs={{0,1},{1,0},{2,3},{3,2},{4,5},{5,4},{6,7},{7,6},{8,9},{9,8},{10,11... | collective-permute-start | bytes 3145736 | tf_op jit(solution)/shard_map/ppermute | solution.py:27
  138.9 27.4 %collective-permute-start.32 = (bf16[512,1024]{1,0:T(8,128)(2,1)S(1)}, bf16[512,1024]{1,0:T(8,128)(2,1)}, u32[]{:S(2)}, u32[]{:S(2)}) collective-permute-start(bf16[512,1024]{1,0:T(8,128)(2,1)S(1)} %slice.409), channel_id=1, source_target_pairs={{0,1},{1,0},{2,3},{3,2},{4,5},{5,4},{6,7},{7,6},{8,9},{9,8},{10,11... | collective-permute-start | bytes 3145736 | tf_op jit(solution)/shard_map/ppermute | solution.py:27
  168.9 14.8 %collective-permute-start.33 = (bf16[512,512]{1,0:T(8,128)(2,1)S(1)}, bf16[512,512]{1,0:T(8,128)(2,1)S(1)}, u32[]{:S(2)}, u32[]{:S(2)}) collective-permute-start(bf16[512,512]{1,0:T(8,128)(2,1)S(1)} %slice.412), channel_id=1, source_target_pairs={{0,2},{1,3},{2,0},{3,1},{4,6},{5,7},{6,4},{7,5},{8,10},{9,11},{10,... | collective-permute-start | bytes 1572872 | tf_op jit(solution)/shard_map/ppermute | solution.py:27
  171.2 23.1 %collective-permute-start.15 = (bf16[512,512]{1,0:T(8,128)(2,1)S(1)}, bf16[512,512]{1,0:T(8,128)(2,1)S(1)}, u32[]{:S(2)}, u32[]{:S(2)}) collective-permute-start(bf16[512,512]{1,0:T(8,128)(2,1)S(1)} %slice.413), channel_id=1, source_target_pairs={{0,2},{1,3},{2,0},{3,1},{4,6},{5,7},{6,4},{7,5},{8,10},{9,11},{10,... | collective-permute-start | bytes 1572872 | tf_op jit(solution)/shard_map/ppermute | solution.py:27
  196.0 7.5 %collective-permute-start.34 = (bf16[64,512]{1,0:T(8,128)(2,1)S(1)}, bf16[64,512]{1,0:T(8,128)(2,1)S(1)}, u32[]{:S(2)}, u32[]{:S(2)}) collective-permute-start(bf16[64,512]{1,0:T(8,128)(2,1)S(1)} %get-tuple-element.35), channel_id=1, source_target_pairs={{0,4},{4,0},{8,12},{12,8},{16,20},{20,16},{24,28},{28,24},{1,5},{5... | collective-permute-start | bytes 196616 | tf_op jit(solution)/shard_map/ppermute | solution.py:27
  197.6 9.8 %collective-permute-start.36 = (bf16[64,512]{1,0:T(8,128)(2,1)S(1)}, bf16[64,512]{1,0:T(8,128)(2,1)S(1)}, u32[]{:S(2)}, u32[]{:S(2)}) collective-permute-start(bf16[64,512]{1,0:T(8,128)(2,1)S(1)} %get-tuple-element.33), channel_id=1, source_target_pairs={{0,12},{4,8},{8,4},{12,0},{16,28},{20,24},{24,20},{28,16},{1,13},{... | collective-permute-start | bytes 196616 | tf_op jit(solution)/shard_map/ppermute | solution.py:27
  199.7 9.2 %collective-permute-start.37 = (bf16[64,512]{1,0:T(8,128)(2,1)S(1)}, bf16[64,512]{1,0:T(8,128)(2,1)S(1)}, u32[]{:S(2)}, u32[]{:S(2)}) collective-permute-start(bf16[64,512]{1,0:T(8,128)(2,1)S(1)} %get-tuple-element.32), channel_id=1, source_target_pairs={{0,16},{4,20},{8,24},{12,28},{16,0},{20,4},{24,8},{28,12},{1,17},{... | collective-permute-start | bytes 196616 | tf_op jit(solution)/shard_map/ppermute | solution.py:27
  200.8 11.7 %collective-permute-start.38 = (bf16[64,512]{1,0:T(8,128)(2,1)S(1)}, bf16[64,512]{1,0:T(8,128)(2,1)S(1)}, u32[]{:S(2)}, u32[]{:S(2)}) collective-permute-start(bf16[64,512]{1,0:T(8,128)(2,1)S(1)} %get-tuple-element.31), channel_id=1, source_target_pairs={{0,20},{4,16},{8,28},{12,24},{16,4},{20,0},{24,12},{28,8},{1,21},{... | collective-permute-start | bytes 196616 | tf_op jit(solution)/shard_map/ppermute | solution.py:27
  203.5 9.0 %collective-permute-start.39 = (bf16[64,512]{1,0:T(8,128)(2,1)S(1)}, bf16[64,512]{1,0:T(8,128)(2,1)S(1)}, u32[]{:S(2)}, u32[]{:S(2)}) collective-permute-start(bf16[64,512]{1,0:T(8,128)(2,1)S(1)} %get-tuple-element.30), channel_id=1, source_target_pairs={{0,24},{4,28},{8,16},{12,20},{16,8},{20,12},{24,0},{28,4},{1,25},{... | collective-permute-start | bytes 196616 | tf_op jit(solution)/shard_map/ppermute | solution.py:27
  204.6 11.1 %collective-permute-start.40 = (bf16[64,512]{1,0:T(8,128)(2,1)S(1)}, bf16[64,512]{1,0:T(8,128)(2,1)S(1)}, u32[]{:S(2)}, u32[]{:S(2)}) collective-permute-start(bf16[64,512]{1,0:T(8,128)(2,1)S(1)} %get-tuple-element.29), channel_id=1, source_target_pairs={{0,28},{4,24},{8,20},{12,16},{16,12},{20,8},{24,4},{28,0},{1,29},{... | collective-permute-start | bytes 196616 | tf_op jit(solution)/shard_map/ppermute | solution.py:27
  207.4 9.8 %collective-permute-start.16 = (bf16[64,512]{1,0:T(8,128)(2,1)S(1)}, bf16[64,512]{1,0:T(8,128)(2,1)S(1)}, u32[]{:S(2)}, u32[]{:S(2)}) collective-permute-start(bf16[64,512]{1,0:T(8,128)(2,1)S(1)} %get-tuple-element.21), channel_id=1, source_target_pairs={{0,4},{4,0},{8,12},{12,8},{16,20},{20,16},{24,28},{28,24},{1,5},{5... | collective-permute-start | bytes 196616 | tf_op jit(solution)/shard_map/ppermute | solution.py:27
  208.9 9.3 %collective-permute-start.17 = (bf16[64,512]{1,0:T(8,128)(2,1)S(1)}, bf16[64,512]{1,0:T(8,128)(2,1)S(1)}, u32[]{:S(2)}, u32[]{:S(2)}) collective-permute-start(bf16[64,512]{1,0:T(8,128)(2,1)S(1)} %get-tuple-element.20), channel_id=1, source_target_pairs={{0,8},{4,12},{8,0},{12,4},{16,24},{20,28},{24,16},{28,20},{1,9},{5... | collective-permute-start | bytes 196616 | tf_op jit(solution)/shard_map/ppermute | solution.py:27
  212.4 8.2 %collective-permute-start.18 = (bf16[64,512]{1,0:T(8,128)(2,1)S(1)}, bf16[64,512]{1,0:T(8,128)(2,1)S(1)}, u32[]{:S(2)}, u32[]{:S(2)}) collective-permute-start(bf16[64,512]{1,0:T(8,128)(2,1)S(1)} %get-tuple-element.19), channel_id=1, source_target_pairs={{0,12},{4,8},{8,4},{12,0},{16,28},{20,24},{24,20},{28,16},{1,13},{... | collective-permute-start | bytes 196616 | tf_op jit(solution)/shard_map/ppermute | solution.py:27
  212.5 8.9 %collective-permute-start.19 = (bf16[64,512]{1,0:T(8,128)(2,1)S(1)}, bf16[64,512]{1,0:T(8,128)(2,1)S(1)}, u32[]{:S(2)}, u32[]{:S(2)}) collective-permute-start(bf16[64,512]{1,0:T(8,128)(2,1)S(1)} %get-tuple-element.18), channel_id=1, source_target_pairs={{0,16},{4,20},{8,24},{12,28},{16,0},{20,4},{24,8},{28,12},{1,17},{... | collective-permute-start | bytes 196616 | tf_op jit(solution)/shard_map/ppermute | solution.py:27
  215.6 7.6 %collective-permute-start.20 = (bf16[64,512]{1,0:T(8,128)(2,1)S(1)}, bf16[64,512]{1,0:T(8,128)(2,1)S(1)}, u32[]{:S(2)}, u32[]{:S(2)}) collective-permute-start(bf16[64,512]{1,0:T(8,128)(2,1)S(1)} %get-tuple-element.17), channel_id=1, source_target_pairs={{0,20},{4,16},{8,28},{12,24},{16,4},{20,0},{24,12},{28,8},{1,21},{... | collective-permute-start | bytes 196616 | tf_op jit(solution)/shard_map/ppermute | solution.py:27
  (32 other events, 211.3 us)

commit v2 on v1

v2 whole, which is shorter than its diff:
```python
import functools

import jax
import jax.numpy as jnp
from jax import lax
from jax.experimental import pallas as pl
from jax.experimental.pallas import tpu as pltpu
from jax.sharding import PartitionSpec as P

HD = 128
CAP = 16
EPS = 1e-06
CHUNKS = 2
SCOPED = 24 * 2**20
BF16 = jnp.bfloat16
F32 = jnp.float32


def bits_of(size):
    return size.bit_length() - 1


def bit_reverse(value, size):
    out = value * 0
    for bit in range(bits_of(size)):
        out = out | (((value >> bit) & 1) << (bits_of(size) - 1 - bit))
    return out


def swap(array, axis, mask):
    size = lax.axis_size(axis)
    return lax.ppermute(array, axis, [(i, i ^ mask) for i in range(size)])


def exclusive_sum(state):
    size, mine = lax.axis_size("seq"), lax.axis_index("seq")
    total, before = state, jnp.zeros_like(state)
    for bit in range(bits_of(size)):
        got = swap(total.astype(BF16), "seq", 1 << bit).astype(F32)
        before = before + jnp.where((mine >> bit) & 1 == 1, got, 0.0)
        total = total + got
    return before


def fold(keep, send):
    partial = keep + swap(send, "head", 1).astype(F32)
    for bit in range(1, bits_of(lax.axis_size("head"))):
        half = partial.shape[0] // 2
        sent = swap(partial[half:].astype(BF16), "head", 1 << bit)
        partial = partial[:half] + sent.astype(F32)
    return partial


def fold_columns(own, near, far):
    size = lax.axis_size("head")
    cols = own.shape[-1]
    step = -(-far.shape[0] // 4)
    got = [swap(far[at : at + step], "head", 1) for at in range(0, far.shape[0], step)]
    got = jnp.concatenate(got).astype(F32)
    rest = near.astype(F32) + got[..., cols:]
    own = own + got[..., :cols]
    for bit in range(1, bits_of(size)):
        half = (size >> bit) // 2
        sent = swap(rest[..., (half - 1) * cols :].astype(BF16), "head", 1 << bit).astype(F32)
        own = own + sent[..., :cols]
        rest = rest[..., : (half - 1) * cols] + sent[..., cols:]
    return own


def gather(array, done):
    arrays = [array]
    for bit in reversed(range(bits_of(lax.axis_size("head")))):
        if bit == 0 and done is not None:
            *arrays, _ = lax.optimization_barrier((*arrays, done))
        arrays = arrays + [swap(one, "head", 1 << bit) for one in arrays]
    return arrays


def exchange(blocks):
    parts = [blocks[0]]
    for k in range(1, lax.axis_size("seq")):
        parts.append(swap(blocks[k], "seq", k))
    return jnp.stack(parts)


def one_hot(index, size):
    return (jnp.arange(size, dtype=jnp.int32)[:, None] == index[None, :]).astype(BF16)


def dot(a, b):
    return jnp.dot(a, b, preferred_element_type=F32)


def attention_out_kernel(query, carried, within, w_out, keep, send):
    normed = []
    for i in range(carried.shape[0]):
        span = slice(i * HD, (i + 1) * HD)
        value = within[:, span] + dot(query[:, span], carried[i])
        scale = lax.rsqrt(jnp.mean(value * value, axis=-1, keepdims=True) + EPS)
        normed.append((value * scale).astype(BF16))
    normed = jnp.concatenate(normed, axis=1)
    half = keep.shape[0]
    send[...] = dot(normed[half:], w_out[...]).astype(send.dtype)
    keep[...] = dot(normed[:half], w_out[...])


def attention_out(query, carried, within, w_out):
    rows, width = query.shape[0], w_out.shape[1]
    whole = pl.BlockSpec(memory_space=pltpu.VMEM)
    return pl.pallas_call(
        attention_out_kernel,
        out_shape=(
            jax.ShapeDtypeStruct((rows // 2, width), F32),
            jax.ShapeDtypeStruct((rows // 2, width), BF16),
        ),
        in_specs=[whole] * 4,
        out_specs=(whole, whole),
        cost_estimate=pl.CostEstimate(
            flops=2 * rows * query.shape[1] * (width + HD),
            transcendentals=rows,
            bytes_accessed=8 * rows * width,
        ),
        compiler_params=pltpu.CompilerParams(vmem_limit_bytes=SCOPED),
    )(query, carried, within, w_out)


def expert_kernel(n_head, n_seq, first, group, head, regroup, *refs):
    pieces = refs[:n_head]
    weights = refs[n_head : n_head + 3]
    shared_gate, shared_up, shared_down = refs[n_head + 3 : n_head + 6]
    own, near, far, held, scales = refs[n_head + 6 : n_head + 11]
    gate, up, down, sems = refs[n_head + 11 :]
    copies = {
        (i, e): pltpu.make_async_copy(weights[i].at[first + e], kept.at[e], sems.at[i, e])
        for e in range(group)
        for i, kept in enumerate((gate, up, down))
    }
    for i, e in sorted(copies, key=lambda at: (at[0] == 2, at[1], at[0])):
        copies[i, e].start()
    count = held.shape[0] // group
    size = pieces[0].shape[0]
    cols = own.shape[-1]

    for e in range(group):
        span = slice(e * count, (e + 1) * count)
        value = dot(regroup[span, :size], pieces[0][...])
        for i in range(1, n_head):
            value += dot(regroup[span, i * size : (i + 1) * size], pieces[i][...])
        held[span, :] = value.astype(BF16)
        scale = lax.rsqrt(jnp.mean(value * value, axis=-1, keepdims=True) + EPS)
        scales[span, :] = jnp.broadcast_to(scale, (count, scales.shape[1]))

    def hidden(rows, scale, gate_weight, up_weight):
        value = dot(rows, gate_weight) * scale
        return (value / (1.0 + jnp.exp(-value)) * (dot(rows, up_weight) * scale)).astype(BF16)

    shared = hidden(held[...], scales[:, :1], shared_gate[...], shared_up[...])
    routed = []
    for e in range(group):
        span = slice(e * count, (e + 1) * count)
        copies[0, e].wait()
        copies[1, e].wait()
        routed.append(hidden(held[span, :], scales[span, :1], gate[e], up[e]))
    for e in range(group):
        copies[2, e].wait()

    def columns(i):
        at = (bit_reverse(i, n_head) ^ head[0]) * cols
        return pl.ds(pl.multiple_of(at, cols), cols)

    def store(ref, i, lane):
        at = columns(i)
        common = dot(shared, shared_down[:, at])
        for e in range(group):
            span = slice(e * count, (e + 1) * count)
            value = common[span] + dot(routed[e], down[e, :, at])
            if i == 0:
                value += held[span, at].astype(F32)
            value = value.reshape(n_seq, count // n_seq, cols).astype(ref.dtype)
            ref[:, e, :, lane * cols : (lane + 1) * cols] = value

    half = n_head // 2
    for i in range(half, n_head):
        store(far, i, i - half)
    for i in range(1, half):
        store(near, i, i - 1)
    store(own, 0, 0)


def experts(head, regroup, pieces, first, group, weights, n_seq):
    n_head = len(pieces)
    width = pieces[0].shape[1]
    rows = pieces[0].shape[0] * n_head
    cols = width // n_head

    def result(count, dtype):
        return jax.ShapeDtypeStruct((n_seq, group, rows // group // n_seq, count * cols), dtype)

    whole = pl.BlockSpec(memory_space=pltpu.VMEM)
    return pl.pallas_call(
        functools.partial(expert_kernel, n_head, n_seq, first, group),
        out_shape=[result(1, F32), result(n_head // 2 - 1, BF16), result(n_head // 2, BF16)],
        in_specs=[pl.BlockSpec(memory_space=pltpu.SMEM)]
        + [whole] * (1 + n_head)
        + [pl.BlockSpec(memory_space=pl.ANY)] * 3
        + [whole] * 3,
        out_specs=[whole] * 3,
        scratch_shapes=[pltpu.VMEM((rows, width), BF16), pltpu.VMEM((rows, 128), F32)]
        + [pltpu.VMEM((group,) + w.shape[1:], w.dtype) for w in weights[:3]]
        + [pltpu.SemaphoreType.DMA((3, group))],
        cost_estimate=pl.CostEstimate(
            flops=2 * rows * width * (rows + 6 * weights[0].shape[2]),
            transcendentals=rows * weights[0].shape[2],
            bytes_accessed=6 * (group + 1) * width * weights[0].shape[2] + 8 * rows * width,
        ),
        compiler_params=pltpu.CompilerParams(vmem_limit_bytes=SCOPED),
    )(head, regroup, *pieces, *weights)


def shards(
    tokens,
    w_query,
    w_key,
    w_value,
    w_out,
    shared_gate,
    shared_up,
    shared_down,
    expert_gate,
    expert_up,
    expert_down,
    expert_ids,
):
    n_seq, n_head = lax.axis_size("seq"), lax.axis_size("head")
    mine, head = lax.axis_index("seq"), lax.axis_index("head")
    rows, width = tokens.shape
    heads_here = w_query.shape[1] // HD
    experts_here = expert_gate.shape[0]
    part = rows // n_head
    cols = width // n_head
    slots = -(-CAP // n_head)
    chunks = min(CHUNKS, experts_here)
    group = experts_here // chunks

    ids = expert_ids[:, 0]
    order = jnp.arange(rows, dtype=jnp.int32)
    start = jnp.sum((ids[None, :] < ids[:, None]).astype(jnp.int32), axis=1)
    earlier = (ids[None, :] == ids[:, None]) & (order[None, :] < order[:, None])
    rank = jnp.sum(earlier.astype(jnp.int32), axis=1)
    place = start + rank
    quarter = place % n_head
    rel = bit_reverse(quarter ^ head, n_head)
    row = rel * part + place // n_head
    here = order[:, None] == row[None, :]
    deal = here.astype(BF16)
    came_from = jnp.sum(jnp.where(here, order[None, :], 0), axis=1)
    slot = rank // n_head
    owner = (ids // experts_here) ^ mine
    local = ids % experts_here
    cell = (((local // group) * n_seq + owner) * group + local % group) * slots + slot
    own_cell = jnp.sum(jnp.where(here[:part], cell[None, :], 0), axis=1)
    cells = chunks * n_seq * group * slots
    pack = one_hot(own_cell, cells).reshape(chunks, cells // chunks, part)
    back_row = (
        (((local // group) * n_seq + owner) * group + local % group) * n_head + quarter
    ) * slots + slot
    back_rows = cells * n_head
    unpack = (back_row[:, None] == jnp.arange(back_rows, dtype=jnp.int32)[None, :]).astype(BF16)

    chunk_rows = n_head * n_seq * group * slots
    at = jnp.arange(chunk_rows, dtype=jnp.int32)
    at_slot, at_expert = at % slots, (at // slots) % group
    at_seq = (at // (slots * group)) % n_seq
    at_head = bit_reverse(at // (slots * group * n_seq), n_head) ^ head
    regroup = one_hot(
        ((at_expert * n_seq + at_seq) * n_head + at_head) * slots + at_slot, chunk_rows
    )
    head_index = jnp.reshape(head, (1,)).astype(jnp.int32)

    inputs = tokens.astype(F32)
    scale = lax.rsqrt(jnp.mean(inputs * inputs, axis=-1, keepdims=True) + EPS)

    def project(weights):
        return (jnp.dot(tokens, weights, preferred_element_type=F32) * scale).astype(BF16)

    key_rows = project(w_key).reshape(rows, heads_here, HD)
    value_rows = project(w_value).reshape(rows, heads_here, HD)
    state = jnp.einsum("thd,the->hde", key_rows, value_rows, preferred_element_type=F32)
    carried = exclusive_sum(state).astype(BF16)
    query_rows = jnp.dot(deal, project(w_query), preferred_element_type=F32)
    query_rows = query_rows.astype(BF16).reshape(rows, heads_here, HD)
    scores = jnp.einsum("thd,shd->hts", query_rows, key_rows, preferred_element_type=F32)
    causal = came_from[:, None] >= order[None, :]
    scores = jnp.where(causal[None], scores, 0.0).astype(BF16)
    within = jnp.einsum("hts,shd->thd", scores, value_rows, preferred_element_type=F32)
    keep, send = attention_out(
        query_rows.reshape(rows, heads_here * HD),
        carried,
        within.reshape(rows, heads_here * HD),
        w_out,
    )
    own_tokens = jnp.dot(deal[:part], tokens, preferred_element_type=F32)
    residual = (own_tokens + fold(keep, send)).astype(BF16)

    weights = (expert_gate, expert_up, expert_down, shared_gate, shared_up, shared_down)
    returned = []
    arrivals = []
    for c in range(chunks):
        outgoing = jnp.dot(pack[c], residual, preferred_element_type=F32).astype(BF16)
        arrived = exchange(outgoing.reshape(n_seq, group * slots, width))
        arrivals.append(arrived.reshape(n_seq * group * slots, width))
    done = None
    for c in range(chunks):
        pieces = gather(arrivals[c], done)
        own, near, far = experts(head_index, regroup, pieces, c * group, group, weights, n_seq)
        done = own
        total = fold_columns(own, near, far).astype(BF16)
        back = exchange(total.reshape(n_seq, group * n_head * slots, cols))
        returned.append(back.reshape(n_seq * group * n_head * slots, cols))
    result = jnp.dot(unpack, jnp.concatenate(returned), preferred_element_type=F32)
    return result.astype(BF16)


def solution(mesh):
    return jax.shard_map(
        shards,
        mesh=mesh,
        in_specs=(
            P("seq", None),
            P(None, "head"),
            P(None, "head"),
            P(None, "head"),
            P("head", None),
            P(None, "head"),
            P(None, "head"),
            P("head", None),
            P("seq", None, "head"),
            P("seq", None, "head"),
            P("seq", "head", None),
            P("seq", None),
        ),
        out_specs=P("seq", "head"),
        check_vma=False,
    )
```

time: 227 us -> 155 us (0.68)
  matrix products: 60.6 us -> 12.3 us
  local copies, waits for them, and re-layouts: 23.4 us -> 4.87 us
  Pallas kernels: 0 us -> 16.3 us
  waiting for transfers between devices: 66.9 us -> 51.3 us
  other arithmetic: 17.5 us -> 6.75 us
  starting transfers between devices: 57.8 us -> 62.6 us
    dot_general x12 -> x0, matrix products: 46 us -> none  [the longest x2 14.5 us: shards(): total = total + jnp.dot(shared, shared_out, preferred_element_type=F32)]
    pallas_call x0 -> x3, Pallas kernels: none -> 16.3 us  [the longest x2 14.8 us: experts(): pl.pallas_call(functools.partial(expert_kernel, n_head, n_seq, first, gro...]
    ppermute x41 -> x49, waiting for transfers between devices: 66.9 us -> 51.3 us  [swap(): return lax.ppermute(array, axis, [(i, i ^ mask) for i in range(size)])]
    transpose x2 -> x0, local copies, waits for them, and re-layouts: 9.62 us -> none  [shards(): jnp.einsum('kecf,efd->kecd', hidden, down[span], preferred_element_type=F32)]
    concatenate x3 -> x0, other arithmetic: 5.17 us -> none  [the longest x1 3.98 us: shards(): jnp.concatenate([lax.dynamic_slice_in_dim(expert_down, (bit_reverse(i, n_...]
    ppermute x41 -> x49, starting transfers between devices: 57.8 us -> 62.6 us  [swap(): return lax.ppermute(array, axis, [(i, i ^ mask) for i in range(size)])]
    slice x6 -> x3, local copies, waits for them, and re-layouts: 4.98 us -> 0.26 us  [the longest x2 0.2 us: fold_columns(): far[at:at + step]]
    add x4 -> x2, other arithmetic: 4.96 us -> 0.3 us  [the longest x1 0.29 us: fold(): partial = keep + swap(send, 'head', 1).astype(F32)]
  transfers between devices with their start and end apart: 41 -> 49, of which waited for: 17 -> 17; matrix products, arithmetic and copies ran while one was open for 22% -> 8% of each run, Pallas kernels for 0% -> 10%
where the time goes in v2:
time: 155 us
  starting transfers between devices  62.6 us (40%)
  waiting for transfers between devices  51.3 us (33%)
  Pallas kernels  16.3 us (11%)
  matrix products  12.3 us (8%)
  other arithmetic  6.75 us (4%)
  local copies, waits for them, and re-layouts  4.87 us (3%)
    ppermute x49, starting transfers between devices, swap(): return lax.ppermute(array, axis, [(i, i ^ mask) for i in range(size)])  62.6 us
    ppermute x49, waiting for transfers between devices, swap(): return lax.ppermute(array, axis, [(i, i ^ mask) for i in range(size)])  51.3 us
    pallas_call x2, Pallas kernels, experts(): pl.pallas_call(functools.partial(expert_kernel, n_head, n_seq, first, gro...  14.8 us
    dot_general x1, matrix products, shards(): jnp.einsum('hts,shd->thd', scores, value_rows, preferred_element_type=F32)  3.56 us
    dot_general x1, matrix products, shards(): query_rows = jnp.dot(deal, project(w_query), preferred_element_type=F32)  3.28 us
  transfers between devices with their start and end apart: 49, of which 17 were waited for; matrix products, arithmetic and copies ran while one was open for 8% of the time, Pallas kernels for 10%

profile of v2, /device:TPU:0, one launch (start us, length us, event | category | flops | bytes accessed | tf_op | source)
XLA Modules:
  0.0 154.8 jit_solution(6418152063435720275)
XLA Ops:
  0.0 2.2 %multiply_reduce_fusion = f32[512]{0:T(512)S(1)} fusion(bf16[512,2048]{1,0:T(8,128)(2,1)} %param.12), kind=kLoop, calls=%fused_computation.1 | loop fusion | flops 3145216 | bytes 2099200 | tf_op jit(solution)/shard_map/reduce_sum | solution.py:281
  6.6 3.0 %collective-permute-start = (bf16[4,128,128]{2,1,0:T(8,128)(2,1)S(1)}, bf16[4,128,128]{2,1,0:T(8,128)(2,1)S(1)}, u32[]{:S(2)}, u32[]{:S(2)}) collective-permute-start(bf16[4,128,128]{2,1,0:T(8,128)(2,1)S(1)} %get-tuple-element.67), channel_id=1, source_target_pairs={{0,4},{4,0},{8,12},{12,8},{16,20},{20,16},{24,28},{28,24},{1,5},{5... | collective-permute-start | bytes 393224 | tf_op jit(solution)/shard_map/ppermute | solution.py:32
  10.5 3.3 %convolution_convert_fusion.2.query = bf16[512,512]{1,0:T(8,128)(2,1)S(1)} fusion(bf16[512,2048]{1,0:T(8,128)(2,1)S(1)} %copy-done.9, bf16[2048,512]{1,0:T(8,128)(2,1)} %param.13, f32[512]{0:T(512)S(1)} %add_rsqrt_fusion, s32[512]{0:T(512)S(1)} %get-tuple-element.66), kind=kOutput, calls=%fused_computation.12 | convolution fusion | flops 1343225856 | bytes 4722688 | tf_op jit(solution)/shard_map/dot_general | solution.py:290
  14.0 1.6 %collective-permute-start.1 = (bf16[4,128,128]{2,1,0:T(8,128)(2,1)S(1)}, bf16[4,128,128]{2,1,0:T(8,128)(2,1)S(1)}, u32[]{:S(2)}, u32[]{:S(2)}) collective-permute-start(bf16[4,128,128]{2,1,0:T(8,128)(2,1)S(1)} %fusion.32), channel_id=1, source_target_pairs={{0,8},{4,12},{8,0},{12,4},{16,24},{20,28},{24,16},{28,20},{1,9},{5... | collective-permute-start | bytes 393224 | tf_op jit(solution)/shard_map/ppermute | solution.py:32
  15.8 3.2 %collective-permute-done.1 = bf16[4,128,128]{2,1,0:T(8,128)(2,1)S(1)} collective-permute-done((bf16[4,128,128]{2,1,0:T(8,128)(2,1)S(1)}, bf16[4,128,128]{2,1,0:T(8,128)(2,1)S(1)}, u32[]{:S(2)}, u32[]{:S(2)}) %collective-permute-start.1) | collective-permute-done | bytes 131104 | tf_op jit(solution)/shard_map/ppermute | solution.py:32
  19.7 2.6 %collective-permute-start.2 = (bf16[4,128,128]{2,1,0:T(8,128)(2,1)}, bf16[4,128,128]{2,1,0:T(8,128)(2,1)S(1)}, u32[]{:S(2)}, u32[]{:S(2)}) collective-permute-start(bf16[4,128,128]{2,1,0:T(8,128)(2,1)} %fusion.29), channel_id=1, source_target_pairs={{0,16},{4,20},{8,24},{12,28},{16,0},{20,4},{24,8},{28,12},{1,17},{... | collective-permute-start | bytes 393224 | tf_op jit(solution)/shard_map/ppermute | solution.py:32
  22.3 3.6 %fusion.1 = f32[4,128,512]{2,1,0:T(8,128)} fusion(bf16[512,4,128]{0,2,1:T(8,128)(2,1)} %bitcast.130, bf16[512,4,128]{0,2,1:T(8,128)(2,1)} %bitcast.128, pred[512,512]{1,0:T(8,128)(4,1)S(1)} %iota_compare_fusion.4, bf16[512,512]{1,0:T(8,128)(2,1)S(1)} %convolution_convert_fusion.2.query), kind=kOutput, calls=%fused_computation.7 | convolution fusion | flops 538968064 | bytes 2883584 | tf_op jit(solution)/shard_map/hts,shd->thd/dot_general | solution.py:295
  25.9 1.7 %copy.22.within = f32[512,512]{1,0:T(8,128)S(1)} copy(f32[512,512]{0,1:T(8,128)} %bitcast.126) | data formatting | bytes 2097152 | tf_op jit(solution)/shard_map/reshape | solution.py:299
  30.9 2.2 %collective-permute-done.3 = bf16[256,2048]{1,0:T(8,128)(2,1)S(1)} collective-permute-done((bf16[256,2048]{1,0:T(8,128)(2,1)S(1)}, bf16[256,2048]{1,0:T(8,128)(2,1)S(1)}, u32[]{:S(2)}, u32[]{:S(2)}) %collective-permute-start.3) | collective-permute-done | bytes 1048608 | tf_op jit(solution)/shard_map/ppermute | solution.py:32
  35.5 11.9 %collective-permute-done.4 = bf16[128,2048]{1,0:T(8,128)(2,1)S(1)} collective-permute-done((bf16[128,2048]{1,0:T(8,128)(2,1)S(1)}, bf16[128,2048]{1,0:T(8,128)(2,1)S(1)}, u32[]{:S(2)}, u32[]{:S(2)}) %collective-permute-start.4) | collective-permute-done | bytes 524320 | tf_op jit(solution)/shard_map/ppermute | solution.py:32
  49.3 1.6 %collective-permute-start.6 = (bf16[16,2048]{1,0:T(8,128)(2,1)S(1)}, bf16[16,2048]{1,0:T(8,128)(2,1)S(1)}, u32[]{:S(2)}, u32[]{:S(2)}) collective-permute-start(bf16[16,2048]{1,0:T(8,128)(2,1)S(1)} %get-tuple-element.56), channel_id=1, source_target_pairs={{0,8},{4,12},{8,0},{12,4},{16,24},{20,28},{24,16},{28,20},{1,9},{5... | collective-permute-start | bytes 196616 | tf_op jit(solution)/shard_map/ppermute | solution.py:32
  52.0 1.9 %collective-permute-start.8 = (bf16[16,2048]{1,0:T(8,128)(2,1)S(1)}, bf16[16,2048]{1,0:T(8,128)(2,1)S(1)}, u32[]{:S(2)}, u32[]{:S(2)}) collective-permute-start(bf16[16,2048]{1,0:T(8,128)(2,1)S(1)} %get-tuple-element.54), channel_id=1, source_target_pairs={{0,16},{4,20},{8,24},{12,28},{16,0},{20,4},{24,8},{28,12},{1,17},{... | collective-permute-start | bytes 196616 | tf_op jit(solution)/shard_map/ppermute | solution.py:32
  55.2 3.0 %collective-permute-start.10 = (bf16[16,2048]{1,0:T(8,128)(2,1)S(1)}, bf16[16,2048]{1,0:T(8,128)(2,1)S(1)}, u32[]{:S(2)}, u32[]{:S(2)}) collective-permute-start(bf16[16,2048]{1,0:T(8,128)(2,1)S(1)} %get-tuple-element.52), channel_id=1, source_target_pairs={{0,24},{4,28},{8,16},{12,20},{16,8},{20,12},{24,0},{28,4},{1,25},{... | collective-permute-start | bytes 196616 | tf_op jit(solution)/shard_map/ppermute | solution.py:32
  63.9 3.8 %collective-permute-start.30 = (bf16[16,2048]{1,0:T(8,128)(2,1)S(1)}, bf16[16,2048]{1,0:T(8,128)(2,1)S(1)}, u32[]{:S(2)}, u32[]{:S(2)}) collective-permute-start(bf16[16,2048]{1,0:T(8,128)(2,1)S(1)} %get-tuple-element.61), channel_id=1, source_target_pairs={{0,16},{4,20},{8,24},{12,28},{16,0},{20,4},{24,8},{28,12},{1,17},{... | collective-permute-start | bytes 196616 | tf_op jit(solution)/shard_map/ppermute | solution.py:32
  67.7 1.9 %collective-permute-start.31 = (bf16[16,2048]{1,0:T(8,128)(2,1)S(1)}, bf16[16,2048]{1,0:T(8,128)(2,1)S(1)}, u32[]{:S(2)}, u32[]{:S(2)}) collective-permute-start(bf16[16,2048]{1,0:T(8,128)(2,1)S(1)} %get-tuple-element.60), channel_id=1, source_target_pairs={{0,20},{4,16},{8,28},{12,24},{16,4},{20,0},{24,12},{28,8},{1,21},{... | collective-permute-start | bytes 196616 | tf_op jit(solution)/shard_map/ppermute | solution.py:32
  70.2 3.4 %collective-permute-start.33 = (bf16[16,2048]{1,0:T(8,128)(2,1)S(1)}, bf16[16,2048]{1,0:T(8,128)(2,1)S(1)}, u32[]{:S(2)}, u32[]{:S(2)}) collective-permute-start(bf16[16,2048]{1,0:T(8,128)(2,1)S(1)} %get-tuple-element.58), channel_id=1, source_target_pairs={{0,28},{4,24},{8,20},{12,16},{16,12},{20,8},{24,4},{28,0},{1,29},{... | collective-permute-start | bytes 196616 | tf_op jit(solution)/shard_map/ppermute | solution.py:32
  76.3 7.6 %collective-permute-done.12.refs_1_ = bf16[128,2048]{1,0:T(8,128)(2,1)S(1)} collective-permute-done((bf16[128,2048]{1,0:T(8,128)(2,1)S(1)}, bf16[128,2048]{1,0:T(8,128)(2,1)S(1)}, u32[]{:S(2)}, u32[]{:S(2)}) %collective-permute-start.12) | collective-permute-done | bytes 524320 | tf_op jit(solution)/shard_map/ppermute | solution.py:32
  85.9 7.3 %shard_map.119 = (f32[8,4,16,512]{3,2,1,0:T(8,128)S(1)}, bf16[8,4,16,512]{3,2,1,0:T(8,128)(2,1)S(1)}, bf16[8,4,16,1024]{3,2,1,0:T(8,128)(2,1)S(1)}) custom-call(s32[1]{0:T(128)} %bitcast.4.head, bf16[512,512]{1,0:T(8,128)(2,1)S(1)} %fusion.19.regroup, bf16[128,2048]{1,0:T(8,128)(2,1)S(1)} %bitcast.125, ...), custom_call_target="tpu_custom_call" | custom-call | flops 4294967296 | bytes 24117248 | tf_op jit(solution)/shard_map/pallas_call | solution.py:200
  94.4 4.0 %collective-permute-done.34.refs_1_ = bf16[128,2048]{1,0:T(8,128)(2,1)S(1)} collective-permute-done((bf16[128,2048]{1,0:T(8,128)(2,1)S(1)}, bf16[128,2048]{1,0:T(8,128)(2,1)S(1)}, u32[]{:S(2)}, u32[]{:S(2)}) %collective-permute-start.34) | collective-permute-done | bytes 524320 | tf_op jit(solution)/shard_map/ppermute | solution.py:32
  101.0 7.5 %shard_map.120 = (f32[8,4,16,512]{3,2,1,0:T(8,128)S(1)}, bf16[8,4,16,512]{3,2,1,0:T(8,128)(2,1)S(1)}, bf16[8,4,16,1024]{3,2,1,0:T(8,128)(2,1)S(1)}) custom-call(s32[1]{0:T(128)} %bitcast.4.head, bf16[512,512]{1,0:T(8,128)(2,1)S(1)} %fusion.19.regroup, bf16[128,2048]{1,0:T(8,128)(2,1)S(1)} %bitcast.122, ...), custom_call_target="tpu_custom_call" | custom-call | flops 4294967296 | bytes 24117248 | tf_op jit(solution)/shard_map/pallas_call | solution.py:200
  109.7 3.5 %collective-permute-done.19 = bf16[8,4,16,512]{3,2,1,0:T(8,128)(2,1)S(1)} collective-permute-done((bf16[8,4,16,512]{3,2,1,0:T(8,128)(2,1)S(1)}, bf16[8,4,16,512]{3,2,1,0:T(8,128)(2,1)S(1)}, u32[]{:S(2)}, u32[]{:S(2)}) %collective-permute-start.19) | collective-permute-done | bytes 524320 | tf_op jit(solution)/shard_map/ppermute | solution.py:32
  113.6 1.9 %collective-permute-start.20 = (bf16[64,512]{1,0:T(8,128)(2,1)S(1)}, bf16[64,512]{1,0:T(8,128)(2,1)S(1)}, u32[]{:S(2)}, u32[]{:S(2)}) collective-permute-start(bf16[64,512]{1,0:T(8,128)(2,1)S(1)} %bitcast.143), channel_id=1, source_target_pairs={{0,4},{4,0},{8,12},{12,8},{16,20},{20,16},{24,28},{28,24},{1,5},{5... | collective-permute-start | bytes 196616 | tf_op jit(solution)/shard_map/ppermute | solution.py:32
  118.8 2.6 %collective-permute-start.24 = (bf16[64,512]{1,0:T(8,128)(2,1)S(1)}, bf16[64,512]{1,0:T(8,128)(2,1)S(1)}, u32[]{:S(2)}, u32[]{:S(2)}) collective-permute-start(bf16[64,512]{1,0:T(8,128)(2,1)S(1)} %bitcast.135), channel_id=1, source_target_pairs={{0,20},{4,16},{8,28},{12,24},{16,4},{20,0},{24,12},{28,8},{1,21},{... | collective-permute-start | bytes 196616 | tf_op jit(solution)/shard_map/ppermute | solution.py:32
  123.1 2.3 %collective-permute-start.26 = (bf16[64,512]{1,0:T(8,128)(2,1)S(1)}, bf16[64,512]{1,0:T(8,128)(2,1)S(1)}, u32[]{:S(2)}, u32[]{:S(2)}) collective-permute-start(bf16[64,512]{1,0:T(8,128)(2,1)S(1)} %bitcast.133), channel_id=1, source_target_pairs={{0,28},{4,24},{8,20},{12,16},{16,12},{20,8},{24,4},{28,0},{1,29},{... | collective-permute-start | bytes 196616 | tf_op jit(solution)/shard_map/ppermute | solution.py:32
  127.0 2.3 %collective-permute-done.24 = bf16[64,512]{1,0:T(8,128)(2,1)S(1)} collective-permute-done((bf16[64,512]{1,0:T(8,128)(2,1)S(1)}, bf16[64,512]{1,0:T(8,128)(2,1)S(1)}, u32[]{:S(2)}, u32[]{:S(2)}) %collective-permute-start.24) | collective-permute-done | bytes 65568 | tf_op jit(solution)/shard_map/ppermute | solution.py:32
  130.2 6.4 %collective-permute-done.41 = bf16[8,4,16,512]{3,2,1,0:T(8,128)(2,1)S(1)} collective-permute-done((bf16[8,4,16,512]{3,2,1,0:T(8,128)(2,1)S(1)}, bf16[8,4,16,512]{3,2,1,0:T(8,128)(2,1)S(1)}, u32[]{:S(2)}, u32[]{:S(2)}) %collective-permute-start.41) | collective-permute-done | bytes 524320 | tf_op jit(solution)/shard_map/ppermute | solution.py:32
  137.0 1.8 %collective-permute-start.42 = (bf16[64,512]{1,0:T(8,128)(2,1)S(1)}, bf16[64,512]{1,0:T(8,128)(2,1)S(1)}, u32[]{:S(2)}, u32[]{:S(2)}) collective-permute-start(bf16[64,512]{1,0:T(8,128)(2,1)S(1)} %bitcast.146), channel_id=1, source_target_pairs={{0,4},{4,0},{8,12},{12,8},{16,20},{20,16},{24,28},{28,24},{1,5},{5... | collective-permute-start | bytes 196616 | tf_op jit(solution)/shard_map/ppermute | solution.py:32
  138.8 1.8 %collective-permute-start.44 = (bf16[64,512]{1,0:T(8,128)(2,1)S(1)}, bf16[64,512]{1,0:T(8,128)(2,1)S(1)}, u32[]{:S(2)}, u32[]{:S(2)}) collective-permute-start(bf16[64,512]{1,0:T(8,128)(2,1)S(1)} %bitcast.144), channel_id=1, source_target_pairs={{0,12},{4,8},{8,4},{12,0},{16,28},{20,24},{24,20},{28,16},{1,13},{... | collective-permute-start | bytes 196616 | tf_op jit(solution)/shard_map/ppermute | solution.py:32
  142.0 2.7 %collective-permute-start.46 = (bf16[64,512]{1,0:T(8,128)(2,1)S(1)}, bf16[64,512]{1,0:T(8,128)(2,1)S(1)}, u32[]{:S(2)}, u32[]{:S(2)}) collective-permute-start(bf16[64,512]{1,0:T(8,128)(2,1)S(1)} %bitcast.141), channel_id=1, source_target_pairs={{0,20},{4,16},{8,28},{12,24},{16,4},{20,0},{24,12},{28,8},{1,21},{... | collective-permute-start | bytes 196616 | tf_op jit(solution)/shard_map/ppermute | solution.py:32
  146.2 2.2 %collective-permute-start.48 = (bf16[64,512]{1,0:T(8,128)(2,1)S(1)}, bf16[64,512]{1,0:T(8,128)(2,1)S(1)}, u32[]{:S(2)}, u32[]{:S(2)}) collective-permute-start(bf16[64,512]{1,0:T(8,128)(2,1)S(1)} %bitcast.137), channel_id=1, source_target_pairs={{0,28},{4,24},{8,20},{12,16},{16,12},{20,8},{24,4},{28,0},{1,29},{... | collective-permute-start | bytes 196616 | tf_op jit(solution)/shard_map/ppermute | solution.py:32
  148.6 2.3 %collective-permute-done.47 = bf16[64,512]{1,0:T(8,128)(2,1)S(1)} collective-permute-done((bf16[64,512]{1,0:T(8,128)(2,1)S(1)}, bf16[64,512]{1,0:T(8,128)(2,1)S(1)}, u32[]{:S(2)}, u32[]{:S(2)}) %collective-permute-start.47) | collective-permute-done | bytes 65568 | tf_op jit(solution)/shard_map/ppermute | solution.py:32
  150.9 2.3 %collective-permute-done.48 = bf16[64,512]{1,0:T(8,128)(2,1)S(1)} collective-permute-done((bf16[64,512]{1,0:T(8,128)(2,1)S(1)}, bf16[64,512]{1,0:T(8,128)(2,1)S(1)}, u32[]{:S(2)}, u32[]{:S(2)}) %collective-permute-start.48) | collective-permute-done | bytes 65568 | tf_op jit(solution)/shard_map/ppermute | solution.py:32
  (183 shorter events, 44.8 us)
Async XLA Ops:
  19.7 7.9 %collective-permute-start.2 = (bf16[4,128,128]{2,1,0:T(8,128)(2,1)}, bf16[4,128,128]{2,1,0:T(8,128)(2,1)S(1)}, u32[]{:S(2)}, u32[]{:S(2)}) collective-permute-start(bf16[4,128,128]{2,1,0:T(8,128)(2,1)} %fusion.29), channel_id=1, source_target_pairs={{0,16},{4,20},{8,24},{12,28},{16,0},{20,4},{24,8},{28,12},{1,17},{... | collective-permute-start | bytes 393224 | tf_op jit(solution)/shard_map/ppermute | solution.py:32
  33.4 14.0 %collective-permute-start.4 = (bf16[128,2048]{1,0:T(8,128)(2,1)S(1)}, bf16[128,2048]{1,0:T(8,128)(2,1)S(1)}, u32[]{:S(2)}, u32[]{:S(2)}) collective-permute-start(bf16[128,2048]{1,0:T(8,128)(2,1)S(1)} %slice.320), channel_id=1, source_target_pairs={{0,2},{1,3},{2,0},{3,1},{4,6},{5,7},{6,4},{7,5},{8,10},{9,11},{10,... | collective-permute-start | bytes 1572872 | tf_op jit(solution)/shard_map/ppermute | solution.py:32
  49.3 8.9 %collective-permute-start.6 = (bf16[16,2048]{1,0:T(8,128)(2,1)S(1)}, bf16[16,2048]{1,0:T(8,128)(2,1)S(1)}, u32[]{:S(2)}, u32[]{:S(2)}) collective-permute-start(bf16[16,2048]{1,0:T(8,128)(2,1)S(1)} %get-tuple-element.56), channel_id=1, source_target_pairs={{0,8},{4,12},{8,0},{12,4},{16,24},{20,28},{24,16},{28,20},{1,9},{5... | collective-permute-start | bytes 196616 | tf_op jit(solution)/shard_map/ppermute | solution.py:32
  50.9 8.8 %collective-permute-start.7 = (bf16[16,2048]{1,0:T(8,128)(2,1)S(1)}, bf16[16,2048]{1,0:T(8,128)(2,1)S(1)}, u32[]{:S(2)}, u32[]{:S(2)}) collective-permute-start(bf16[16,2048]{1,0:T(8,128)(2,1)S(1)} %get-tuple-element.55), channel_id=1, source_target_pairs={{0,12},{4,8},{8,4},{12,0},{16,28},{20,24},{24,20},{28,16},{1,13},{... | collective-permute-start | bytes 196616 | tf_op jit(solution)/shard_map/ppermute | solution.py:32
  52.0 10.1 %collective-permute-start.8 = (bf16[16,2048]{1,0:T(8,128)(2,1)S(1)}, bf16[16,2048]{1,0:T(8,128)(2,1)S(1)}, u32[]{:S(2)}, u32[]{:S(2)}) collective-permute-start(bf16[16,2048]{1,0:T(8,128)(2,1)S(1)} %get-tuple-element.54), channel_id=1, source_target_pairs={{0,16},{4,20},{8,24},{12,28},{16,0},{20,4},{24,8},{28,12},{1,17},{... | collective-permute-start | bytes 196616 | tf_op jit(solution)/shard_map/ppermute | solution.py:32
  53.9 9.8 %collective-permute-start.9 = (bf16[16,2048]{1,0:T(8,128)(2,1)S(1)}, bf16[16,2048]{1,0:T(8,128)(2,1)S(1)}, u32[]{:S(2)}, u32[]{:S(2)}) collective-permute-start(bf16[16,2048]{1,0:T(8,128)(2,1)S(1)} %get-tuple-element.53), channel_id=1, source_target_pairs={{0,20},{4,16},{8,28},{12,24},{16,4},{20,0},{24,12},{28,8},{1,21},{... | collective-permute-start | bytes 196616 | tf_op jit(solution)/shard_map/ppermute | solution.py:32
  55.2 8.8 %collective-permute-start.10 = (bf16[16,2048]{1,0:T(8,128)(2,1)S(1)}, bf16[16,2048]{1,0:T(8,128)(2,1)S(1)}, u32[]{:S(2)}, u32[]{:S(2)}) collective-permute-start(bf16[16,2048]{1,0:T(8,128)(2,1)S(1)} %get-tuple-element.52), channel_id=1, source_target_pairs={{0,24},{4,28},{8,16},{12,20},{16,8},{20,12},{24,0},{28,4},{1,25},{... | collective-permute-start | bytes 196616 | tf_op jit(solution)/shard_map/ppermute | solution.py:32
  58.2 9.5 %collective-permute-start.11 = (bf16[16,2048]{1,0:T(8,128)(2,1)S(1)}, bf16[16,2048]{1,0:T(8,128)(2,1)S(1)}, u32[]{:S(2)}, u32[]{:S(2)}) collective-permute-start(bf16[16,2048]{1,0:T(8,128)(2,1)S(1)} %get-tuple-element.51), channel_id=1, source_target_pairs={{0,28},{4,24},{8,20},{12,16},{16,12},{20,8},{24,4},{28,0},{1,29},{... | collective-permute-start | bytes 196616 | tf_op jit(solution)/shard_map/ppermute | solution.py:32
  59.8 9.9 %collective-permute-start.27 = (bf16[16,2048]{1,0:T(8,128)(2,1)S(1)}, bf16[16,2048]{1,0:T(8,128)(2,1)S(1)}, u32[]{:S(2)}, u32[]{:S(2)}) collective-permute-start(bf16[16,2048]{1,0:T(8,128)(2,1)S(1)} %get-tuple-element.64), channel_id=1, source_target_pairs={{0,4},{4,0},{8,12},{12,8},{16,20},{20,16},{24,28},{28,24},{1,5},{5... | collective-permute-start | bytes 196616 | tf_op jit(solution)/shard_map/ppermute | solution.py:32
  62.1 8.1 %collective-permute-start.28 = (bf16[16,2048]{1,0:T(8,128)(2,1)S(1)}, bf16[16,2048]{1,0:T(8,128)(2,1)S(1)}, u32[]{:S(2)}, u32[]{:S(2)}) collective-permute-start(bf16[16,2048]{1,0:T(8,128)(2,1)S(1)} %get-tuple-element.63), channel_id=1, source_target_pairs={{0,8},{4,12},{8,0},{12,4},{16,24},{20,28},{24,16},{28,20},{1,9},{5... | collective-permute-start | bytes 196616 | tf_op jit(solution)/shard_map/ppermute | solution.py:32
  63.7 10.0 %collective-permute-start.29 = (bf16[16,2048]{1,0:T(8,128)(2,1)S(1)}, bf16[16,2048]{1,0:T(8,128)(2,1)S(1)}, u32[]{:S(2)}, u32[]{:S(2)}) collective-permute-start(bf16[16,2048]{1,0:T(8,128)(2,1)S(1)} %get-tuple-element.62), channel_id=1, source_target_pairs={{0,12},{4,8},{8,4},{12,0},{16,28},{20,24},{24,20},{28,16},{1,13},{... | collective-permute-start | bytes 196616 | tf_op jit(solution)/shard_map/ppermute | solution.py:32
  63.9 11.3 %collective-permute-start.30 = (bf16[16,2048]{1,0:T(8,128)(2,1)S(1)}, bf16[16,2048]{1,0:T(8,128)(2,1)S(1)}, u32[]{:S(2)}, u32[]{:S(2)}) collective-permute-start(bf16[16,2048]{1,0:T(8,128)(2,1)S(1)} %get-tuple-element.61), channel_id=1, source_target_pairs={{0,16},{4,20},{8,24},{12,28},{16,0},{20,4},{24,8},{28,12},{1,17},{... | collective-permute-start | bytes 196616 | tf_op jit(solution)/shard_map/ppermute | solution.py:32
  67.7 8.6 %collective-permute-start.31 = (bf16[16,2048]{1,0:T(8,128)(2,1)S(1)}, bf16[16,2048]{1,0:T(8,128)(2,1)S(1)}, u32[]{:S(2)}, u32[]{:S(2)}) collective-permute-start(bf16[16,2048]{1,0:T(8,128)(2,1)S(1)} %get-tuple-element.60), channel_id=1, source_target_pairs={{0,20},{4,16},{8,28},{12,24},{16,4},{20,0},{24,12},{28,8},{1,21},{... | collective-permute-start | bytes 196616 | tf_op jit(solution)/shard_map/ppermute | solution.py:32
  69.6 14.3 %collective-permute-start.32 = (bf16[16,2048]{1,0:T(8,128)(2,1)S(1)}, bf16[16,2048]{1,0:T(8,128)(2,1)S(1)}, u32[]{:S(2)}, u32[]{:S(2)}) collective-permute-start(bf16[16,2048]{1,0:T(8,128)(2,1)S(1)} %get-tuple-element.59), channel_id=1, source_target_pairs={{0,24},{4,28},{8,16},{12,20},{16,8},{20,12},{24,0},{28,4},{1,25},{... | collective-permute-start | bytes 196616 | tf_op jit(solution)/shard_map/ppermute | solution.py:32
  70.2 13.7 %collective-permute-start.33 = (bf16[16,2048]{1,0:T(8,128)(2,1)S(1)}, bf16[16,2048]{1,0:T(8,128)(2,1)S(1)}, u32[]{:S(2)}, u32[]{:S(2)}) collective-permute-start(bf16[16,2048]{1,0:T(8,128)(2,1)S(1)} %get-tuple-element.58), channel_id=1, source_target_pairs={{0,28},{4,24},{8,20},{12,16},{16,12},{20,8},{24,4},{28,0},{1,29},{... | collective-permute-start | bytes 196616 | tf_op jit(solution)/shard_map/ppermute | solution.py:32
  73.7 10.2 %collective-permute-start.12 = (bf16[128,2048]{1,0:T(8,128)(2,1)S(1)}, bf16[128,2048]{1,0:T(8,128)(2,1)S(1)}, u32[]{:S(2)}, u32[]{:S(2)}) collective-permute-start(bf16[128,2048]{1,0:T(8,128)(2,1)S(1)} %bitcast.123), channel_id=1, source_target_pairs={{0,2},{1,3},{2,0},{3,1},{4,6},{5,7},{6,4},{7,5},{8,10},{9,11},{10,... | collective-permute-start | bytes 1572872 | tf_op jit(solution)/shard_map/ppermute | solution.py:32
  75.3 10.2 %collective-permute-start.13 = (bf16[128,2048]{1,0:T(8,128)(2,1)S(1)}, bf16[128,2048]{1,0:T(8,128)(2,1)S(1)}, u32[]{:S(2)}, u32[]{:S(2)}) collective-permute-start(bf16[128,2048]{1,0:T(8,128)(2,1)S(1)} %bitcast.124), channel_id=1, source_target_pairs={{0,1},{1,0},{2,3},{3,2},{4,5},{5,4},{6,7},{7,6},{8,9},{9,8},{10,11... | collective-permute-start | bytes 1572872 | tf_op jit(solution)/shard_map/ppermute | solution.py:32
  83.9 14.4 %collective-permute-start.34 = (bf16[128,2048]{1,0:T(8,128)(2,1)S(1)}, bf16[128,2048]{1,0:T(8,128)(2,1)S(1)}, u32[]{:S(2)}, u32[]{:S(2)}) collective-permute-start(bf16[128,2048]{1,0:T(8,128)(2,1)S(1)} %bitcast.120), channel_id=1, source_target_pairs={{0,2},{1,3},{2,0},{3,1},{4,6},{5,7},{6,4},{7,5},{8,10},{9,11},{10,... | collective-permute-start | bytes 1572872 | tf_op jit(solution)/shard_map/ppermute | solution.py:32
  99.3 13.9 %collective-permute-start.19 = (bf16[8,4,16,512]{3,2,1,0:T(8,128)(2,1)S(1)}, bf16[8,4,16,512]{3,2,1,0:T(8,128)(2,1)S(1)}, u32[]{:S(2)}, u32[]{:S(2)}) collective-permute-start(bf16[8,4,16,512]{3,2,1,0:T(8,128)(2,1)S(1)} %fusion.9), channel_id=1, source_target_pairs={{0,2},{1,3},{2,0},{3,1},{4,6},{5,7},{6,4},{7,5},{8,10},{9,11},{10,... | collective-permute-start | bytes 1572872 | tf_op jit(solution)/shard_map/ppermute | solution.py:32
  109.2 8.1 %collective-permute-start.39 = (bf16[2,4,16,1024]{3,2,1,0:T(8,128)(2,1)S(1)}, bf16[2,4,16,1024]{3,2,1,0:T(8,128)(2,1)S(1)}, u32[]{:S(2)}, u32[]{:S(2)}) collective-permute-start(bf16[2,4,16,1024]{3,2,1,0:T(8,128)(2,1)S(1)} %get-tuple-element.33), channel_id=1, source_target_pairs={{0,1},{1,0},{2,3},{3,2},{4,5},{5,4},{6,7},{7,6},{8,9},{9,8},{10,11... | collective-permute-start | bytes 786440 | tf_op jit(solution)/shard_map/ppermute | solution.py:32
  109.3 9.5 %collective-permute-start.40 = (bf16[2,4,16,1024]{3,2,1,0:T(8,128)(2,1)S(1)}, bf16[2,4,16,1024]{3,2,1,0:T(8,128)(2,1)S(1)}, u32[]{:S(2)}, u32[]{:S(2)}) collective-permute-start(bf16[2,4,16,1024]{3,2,1,0:T(8,128)(2,1)S(1)} %get-tuple-element.32), channel_id=1, source_target_pairs={{0,1},{1,0},{2,3},{3,2},{4,5},{5,4},{6,7},{7,6},{8,9},{9,8},{10,11... | collective-permute-start | bytes 786440 | tf_op jit(solution)/shard_map/ppermute | solution.py:32
  113.6 8.2 %collective-permute-start.20 = (bf16[64,512]{1,0:T(8,128)(2,1)S(1)}, bf16[64,512]{1,0:T(8,128)(2,1)S(1)}, u32[]{:S(2)}, u32[]{:S(2)}) collective-permute-start(bf16[64,512]{1,0:T(8,128)(2,1)S(1)} %bitcast.143), channel_id=1, source_target_pairs={{0,4},{4,0},{8,12},{12,8},{16,20},{20,16},{24,28},{28,24},{1,5},{5... | collective-permute-start | bytes 196616 | tf_op jit(solution)/shard_map/ppermute | solution.py:32
  115.5 7.6 %collective-permute-start.21 = (bf16[64,512]{1,0:T(8,128)(2,1)S(1)}, bf16[64,512]{1,0:T(8,128)(2,1)S(1)}, u32[]{:S(2)}, u32[]{:S(2)}) collective-permute-start(bf16[64,512]{1,0:T(8,128)(2,1)S(1)} %bitcast.140), channel_id=1, source_target_pairs={{0,8},{4,12},{8,0},{12,4},{16,24},{20,28},{24,16},{28,20},{1,9},{5... | collective-permute-start | bytes 196616 | tf_op jit(solution)/shard_map/ppermute | solution.py:32
  115.6 9.8 %collective-permute-start.22 = (bf16[64,512]{1,0:T(8,128)(2,1)S(1)}, bf16[64,512]{1,0:T(8,128)(2,1)S(1)}, u32[]{:S(2)}, u32[]{:S(2)}) collective-permute-start(bf16[64,512]{1,0:T(8,128)(2,1)S(1)} %bitcast.138), channel_id=1, source_target_pairs={{0,12},{4,8},{8,4},{12,0},{16,28},{20,24},{24,20},{28,16},{1,13},{... | collective-permute-start | bytes 196616 | tf_op jit(solution)/shard_map/ppermute | solution.py:32
  117.2 9.8 %collective-permute-start.23 = (bf16[64,512]{1,0:T(8,128)(2,1)S(1)}, bf16[64,512]{1,0:T(8,128)(2,1)S(1)}, u32[]{:S(2)}, u32[]{:S(2)}) collective-permute-start(bf16[64,512]{1,0:T(8,128)(2,1)S(1)} %bitcast.136), channel_id=1, source_target_pairs={{0,16},{4,20},{8,24},{12,28},{16,0},{20,4},{24,8},{28,12},{1,17},{... | collective-permute-start | bytes 196616 | tf_op jit(solution)/shard_map/ppermute | solution.py:32
  118.8 10.5 %collective-permute-start.24 = (bf16[64,512]{1,0:T(8,128)(2,1)S(1)}, bf16[64,512]{1,0:T(8,128)(2,1)S(1)}, u32[]{:S(2)}, u32[]{:S(2)}) collective-permute-start(bf16[64,512]{1,0:T(8,128)(2,1)S(1)} %bitcast.135), channel_id=1, source_target_pairs={{0,20},{4,16},{8,28},{12,24},{16,4},{20,0},{24,12},{28,8},{1,21},{... | collective-permute-start | bytes 196616 | tf_op jit(solution)/shard_map/ppermute | solution.py:32
  121.8 7.5 %collective-permute-start.25 = (bf16[64,512]{1,0:T(8,128)(2,1)S(1)}, bf16[64,512]{1,0:T(8,128)(2,1)S(1)}, u32[]{:S(2)}, u32[]{:S(2)}) collective-permute-start(bf16[64,512]{1,0:T(8,128)(2,1)S(1)} %bitcast.134), channel_id=1, source_target_pairs={{0,24},{4,28},{8,16},{12,20},{16,8},{20,12},{24,0},{28,4},{1,25},{... | collective-permute-start | bytes 196616 | tf_op jit(solution)/shard_map/ppermute | solution.py:32
  125.4 11.2 %collective-permute-start.41 = (bf16[8,4,16,512]{3,2,1,0:T(8,128)(2,1)S(1)}, bf16[8,4,16,512]{3,2,1,0:T(8,128)(2,1)S(1)}, u32[]{:S(2)}, u32[]{:S(2)}) collective-permute-start(bf16[8,4,16,512]{3,2,1,0:T(8,128)(2,1)S(1)} %fusion.6), channel_id=1, source_target_pairs={{0,2},{1,3},{2,0},{3,1},{4,6},{5,7},{6,4},{7,5},{8,10},{9,11},{10,... | collective-permute-start | bytes 1572872 | tf_op jit(solution)/shard_map/ppermute | solution.py:32
  137.0 7.6 %collective-permute-start.42 = (bf16[64,512]{1,0:T(8,128)(2,1)S(1)}, bf16[64,512]{1,0:T(8,128)(2,1)S(1)}, u32[]{:S(2)}, u32[]{:S(2)}) collective-permute-start(bf16[64,512]{1,0:T(8,128)(2,1)S(1)} %bitcast.146), channel_id=1, source_target_pairs={{0,4},{4,0},{8,12},{12,8},{16,20},{20,16},{24,28},{28,24},{1,5},{5... | collective-permute-start | bytes 196616 | tf_op jit(solution)/shard_map/ppermute | solution.py:32
  138.8 7.4 %collective-permute-start.43 = (bf16[64,512]{1,0:T(8,128)(2,1)S(1)}, bf16[64,512]{1,0:T(8,128)(2,1)S(1)}, u32[]{:S(2)}, u32[]{:S(2)}) collective-permute-start(bf16[64,512]{1,0:T(8,128)(2,1)S(1)} %bitcast.145), channel_id=1, source_target_pairs={{0,8},{4,12},{8,0},{12,4},{16,24},{20,28},{24,16},{28,20},{1,9},{5... | collective-permute-start | bytes 196616 | tf_op jit(solution)/shard_map/ppermute | solution.py:32
  138.8 9.6 %collective-permute-start.44 = (bf16[64,512]{1,0:T(8,128)(2,1)S(1)}, bf16[64,512]{1,0:T(8,128)(2,1)S(1)}, u32[]{:S(2)}, u32[]{:S(2)}) collective-permute-start(bf16[64,512]{1,0:T(8,128)(2,1)S(1)} %bitcast.144), channel_id=1, source_target_pairs={{0,12},{4,8},{8,4},{12,0},{16,28},{20,24},{24,20},{28,16},{1,13},{... | collective-permute-start | bytes 196616 | tf_op jit(solution)/shard_map/ppermute | solution.py:32
  140.6 7.8 %collective-permute-start.45 = (bf16[64,512]{1,0:T(8,128)(2,1)S(1)}, bf16[64,512]{1,0:T(8,128)(2,1)S(1)}, u32[]{:S(2)}, u32[]{:S(2)}) collective-permute-start(bf16[64,512]{1,0:T(8,128)(2,1)S(1)} %bitcast.142), channel_id=1, source_target_pairs={{0,16},{4,20},{8,24},{12,28},{16,0},{20,4},{24,8},{28,12},{1,17},{... | collective-permute-start | bytes 196616 | tf_op jit(solution)/shard_map/ppermute | solution.py:32
  (37 other events, 460.1 us)

commit v3 on v2

--- a/solution.py
+++ b/solution.py
@@ -11,7 +11,7 @@
 CAP = 16
 EPS = 1e-06
 CHUNKS = 2
-SCOPED = 24 * 2**20
+SCOPED = 40 * 2**20
 BF16 = jnp.bfloat16
 F32 = jnp.float32
 
@@ -34,24 +34,43 @@
 
 def exclusive_sum(state):
     size, mine = lax.axis_size("seq"), lax.axis_index("seq")
-    total, before = state, jnp.zeros_like(state)
+    total, before, first = state, jnp.zeros_like(state), None
     for bit in range(bits_of(size)):
-        got = swap(total.astype(BF16), "seq", 1 << bit).astype(F32)
+        got = swap(total.astype(BF16), "seq", 1 << bit)
+        first = got if first is None else first
+        got = got.astype(F32)
         before = before + jnp.where((mine >> bit) & 1 == 1, got, 0.0)
         total = total + got
-    return before
+    return before, first
 
 
 def fold(keep, send):
-    partial = keep + swap(send, "head", 1).astype(F32)
+    partial, got = keep, swap(send, "head", 1)
     for bit in range(1, bits_of(lax.axis_size("head"))):
         half = partial.shape[0] // 2
-        sent = swap(partial[half:].astype(BF16), "head", 1 << bit)
-        partial = partial[:half] + sent.astype(F32)
-    return partial
-
-
-def fold_columns(own, near, far):
+        late = partial[half:] + got[half:].astype(F32)
+        partial = partial[:half] + got[:half].astype(F32)
+        got = swap(late.astype(BF16), "head", 1 << bit)
+    return partial, got
+
+
+def pack_kernel(pack, own_tokens, partial, got, out):
+    residual = own_tokens[...].astype(F32) + partial[...] + got[...].astype(F32)
+    out[...] = dot(pack[...], residual.astype(BF16)).astype(BF16)
+
+
+def pack_rows(pack, own_tokens, partial, got):
+    whole = pl.BlockSpec(memory_space=pltpu.VMEM)
+    return pl.pallas_call(
+        pack_kernel,
+        out_shape=jax.ShapeDtypeStruct((pack.shape[0], got.shape[1]), BF16),
+        in_specs=[whole] * 4,
+        out_specs=whole,
+        compiler_params=pltpu.CompilerParams(vmem_limit_bytes=12 * 2**20),
+    )(pack, own_tokens, partial, got)
+
+
+def fold_columns(own, near, far, earlier):
     size = lax.axis_size("head")
     cols = own.shape[-1]
     step = -(-far.shape[0] // 4)
@@ -59,6 +78,8 @@
     got = jnp.concatenate(got).astype(F32)
     rest = near.astype(F32) + got[..., cols:]
     own = own + got[..., :cols]
+    if earlier:
+        rest, earlier[-1] = lax.optimization_barrier((rest, earlier[-1]))
     for bit in range(1, bits_of(size)):
         half = (size >> bit) // 2
         sent = swap(rest[..., (half - 1) * cols :].astype(BF16), "head", 1 << bit).astype(F32)
@@ -76,11 +97,14 @@
     return arrays
 
 
-def exchange(blocks):
-    parts = [blocks[0]]
-    for k in range(1, lax.axis_size("seq")):
-        parts.append(swap(blocks[k], "seq", k))
-    return jnp.stack(parts)
+def unstack(rows, half, chunks, size):
+    near = [rows[k * chunks * size : (k + 1) * chunks * size] for k in range(half)]
+    at = half * chunks * size
+    far = [
+        [rows[at + (c * half + k) * size : at + (c * half + k + 1) * size] for k in range(half)]
+        for c in range(chunks)
+    ]
+    return near, far
 
 
 def one_hot(index, size):
@@ -95,7 +119,7 @@
     normed = []
     for i in range(carried.shape[0]):
         span = slice(i * HD, (i + 1) * HD)
-        value = within[:, span] + dot(query[:, span], carried[i])
+        value = within[i] + dot(query[:, span], carried[i])
         scale = lax.rsqrt(jnp.mean(value * value, axis=-1, keepdims=True) + EPS)
         normed.append((value * scale).astype(BF16))
     normed = jnp.concatenate(normed, axis=1)
@@ -120,21 +144,23 @@
             transcendentals=rows,
             bytes_accessed=8 * rows * width,
         ),
-        compiler_params=pltpu.CompilerParams(vmem_limit_bytes=SCOPED),
+        compiler_params=pltpu.CompilerParams(vmem_limit_bytes=12 * 2**20),
     )(query, carried, within, w_out)
 
 
 def expert_kernel(n_head, n_seq, first, group, head, regroup, *refs):
     pieces = refs[:n_head]
     weights = refs[n_head : n_head + 3]
-    shared_gate, shared_up, shared_down = refs[n_head + 3 : n_head + 6]
+    shared_in = refs[n_head + 3 : n_head + 6]
     own, near, far, held, scales = refs[n_head + 6 : n_head + 11]
-    gate, up, down, sems = refs[n_head + 11 :]
+    gate, up, down, shared_gate, shared_up, shared_down, sems = refs[n_head + 11 :]
     copies = {
         (i, e): pltpu.make_async_copy(weights[i].at[first + e], kept.at[e], sems.at[i, e])
         for e in range(group)
         for i, kept in enumerate((gate, up, down))
     }
+    for i, kept in enumerate((shared_gate, shared_up, shared_down)):
+        copies[i, group] = pltpu.make_async_copy(shared_in[i], kept, sems.at[i, group])
     for i, e in sorted(copies, key=lambda at: (at[0] == 2, at[1], at[0])):
         copies[i, e].start()
     count = held.shape[0] // group
@@ -154,14 +180,16 @@
         value = dot(rows, gate_weight) * scale
         return (value / (1.0 + jnp.exp(-value)) * (dot(rows, up_weight) * scale)).astype(BF16)
 
-    shared = hidden(held[...], scales[:, :1], shared_gate[...], shared_up[...])
     routed = []
     for e in range(group):
         span = slice(e * count, (e + 1) * count)
         copies[0, e].wait()
         copies[1, e].wait()
         routed.append(hidden(held[span, :], scales[span, :1], gate[e], up[e]))
-    for e in range(group):
+    copies[0, group].wait()
+    copies[1, group].wait()
+    shared = hidden(held[...], scales[:, :1], shared_gate[...], shared_up[...])
+    for e in range(group + 1):
         copies[2, e].wait()
 
     def columns(i):
@@ -202,12 +230,12 @@
         out_shape=[result(1, F32), result(n_head // 2 - 1, BF16), result(n_head // 2, BF16)],
         in_specs=[pl.BlockSpec(memory_space=pltpu.SMEM)]
         + [whole] * (1 + n_head)
-        + [pl.BlockSpec(memory_space=pl.ANY)] * 3
-        + [whole] * 3,
+        + [pl.BlockSpec(memory_space=pltpu.HBM)] * 6,
         out_specs=[whole] * 3,
         scratch_shapes=[pltpu.VMEM((rows, width), BF16), pltpu.VMEM((rows, 128), F32)]
         + [pltpu.VMEM((group,) + w.shape[1:], w.dtype) for w in weights[:3]]
-        + [pltpu.SemaphoreType.DMA((3, group))],
+        + [pltpu.VMEM(w.shape, w.dtype) for w in weights[3:]]
+        + [pltpu.SemaphoreType.DMA((3, group + 1))],
         cost_estimate=pl.CostEstimate(
             flops=2 * rows * width * (rows + 6 * weights[0].shape[2]),
             transcendentals=rows * weights[0].shape[2],
@@ -257,15 +285,21 @@
     slot = rank // n_head
     owner = (ids // experts_here) ^ mine
     local = ids % experts_here
-    cell = (((local // group) * n_seq + owner) * group + local % group) * slots + slot
+    half = n_seq // 2
+
+    def place_in(inner, size):
+        near = (owner * chunks + local // group) * size
+        far = (half * chunks + (local // group) * half + owner - half) * size
+        return jnp.where(owner < half, near, far) + inner
+
+    sent_rows, back_size = group * slots, group * slots * n_head
+    cell = place_in((local % group) * slots + slot, sent_rows)
     own_cell = jnp.sum(jnp.where(here[:part], cell[None, :], 0), axis=1)
-    cells = chunks * n_seq * group * slots
-    pack = one_hot(own_cell, cells).reshape(chunks, cells // chunks, part)
-    back_row = (
-        (((local // group) * n_seq + owner) * group + local % group) * n_head + quarter
-    ) * slots + slot
-    back_rows = cells * n_head
-    unpack = (back_row[:, None] == jnp.arange(back_rows, dtype=jnp.int32)[None, :]).astype(BF16)
+    pack = one_hot(own_cell, n_seq * chunks * sent_rows)
+    back_row = place_in(((local % group) * n_head + quarter) * slots + slot, back_size)
+    unpack = (
+        back_row[:, None] == jnp.arange(n_seq * chunks * back_size, dtype=jnp.int32)[None, :]
+    ).astype(BF16)
 
     chunk_rows = n_head * n_seq * group * slots
     at = jnp.arange(chunk_rows, dtype=jnp.int32)
@@ -280,44 +314,50 @@
     inputs = tokens.astype(F32)
     scale = lax.rsqrt(jnp.mean(inputs * inputs, axis=-1, keepdims=True) + EPS)
 
-    def project(weights):
+    def project(weights, scale):
         return (jnp.dot(tokens, weights, preferred_element_type=F32) * scale).astype(BF16)
 
-    key_rows = project(w_key).reshape(rows, heads_here, HD)
-    value_rows = project(w_value).reshape(rows, heads_here, HD)
+    key_rows = project(w_key, scale).reshape(rows, heads_here, HD)
+    value_rows = project(w_value, scale).reshape(rows, heads_here, HD)
     state = jnp.einsum("thd,the->hde", key_rows, value_rows, preferred_element_type=F32)
-    carried = exclusive_sum(state).astype(BF16)
-    query_rows = jnp.dot(deal, project(w_query), preferred_element_type=F32)
+    carried, first = exclusive_sum(state)
+    carried = carried.astype(BF16)
+    scale, _ = lax.optimization_barrier((scale, first))
+    query_rows = jnp.dot(deal, project(w_query, scale), preferred_element_type=F32)
     query_rows = query_rows.astype(BF16).reshape(rows, heads_here, HD)
     scores = jnp.einsum("thd,shd->hts", query_rows, key_rows, preferred_element_type=F32)
     causal = came_from[:, None] >= order[None, :]
     scores = jnp.where(causal[None], scores, 0.0).astype(BF16)
-    within = jnp.einsum("hts,shd->thd", scores, value_rows, preferred_element_type=F32)
+    within = jnp.einsum("hts,shd->htd", scores, value_rows, preferred_element_type=F32)
     keep, send = attention_out(
         query_rows.reshape(rows, heads_here * HD),
         carried,
-        within.reshape(rows, heads_here * HD),
+        within,
         w_out,
     )
-    own_tokens = jnp.dot(deal[:part], tokens, preferred_element_type=F32)
-    residual = (own_tokens + fold(keep, send)).astype(BF16)
+    own_tokens = dot(deal[:part], tokens).astype(BF16)
+    partial, got = fold(keep, send)
 
     weights = (expert_gate, expert_up, expert_down, shared_gate, shared_up, shared_down)
-    returned = []
-    arrivals = []
-    for c in range(chunks):
-        outgoing = jnp.dot(pack[c], residual, preferred_element_type=F32).astype(BF16)
-        arrived = exchange(outgoing.reshape(n_seq, group * slots, width))
-        arrivals.append(arrived.reshape(n_seq * group * slots, width))
+    outgoing = pack_rows(pack, own_tokens, partial, got)
+    near, far = unstack(outgoing, half, chunks, sent_rows)
+    near = [near[0]] + [swap(near[k], "seq", k) for k in range(1, half)]
+    far = [[swap(far[c][k], "seq", half + k) for k in range(half)] for c in range(chunks)]
+    totals = []
     done = None
     for c in range(chunks):
-        pieces = gather(arrivals[c], done)
-        own, near, far = experts(head_index, regroup, pieces, c * group, group, weights, n_seq)
+        blocks = [block[c * sent_rows : (c + 1) * sent_rows] for block in near] + far[c]
+        pieces = gather(jnp.concatenate(blocks), done)
+        own, rest, other = experts(head_index, regroup, pieces, c * group, group, weights, n_seq)
         done = own
-        total = fold_columns(own, near, far).astype(BF16)
-        back = exchange(total.reshape(n_seq, group * n_head * slots, cols))
-        returned.append(back.reshape(n_seq * group * n_head * slots, cols))
-    result = jnp.dot(unpack, jnp.concatenate(returned), preferred_element_type=F32)
+        total = fold_columns(own, rest, other, totals).astype(BF16)
+        totals.append(total.reshape(n_seq, back_size, cols))
+    back = [jnp.concatenate([total[k] for total in totals]) for k in range(half)]
+    far = [[swap(total[k], "seq", k) for k in range(half, n_seq)] for total in totals]
+    tied = lax.optimization_barrier((*back[1:], *far[0]))
+    back = back[:1] + [swap(tied[k], "seq", k + 1) for k in range(half - 1)]
+    back = back + list(tied[half - 1 :]) + [one for blocks in far[1:] for one in blocks]
+    result = dot(unpack, jnp.concatenate(back))
     return result.astype(BF16)
 
 

time: 155 us -> 141 us (0.910)
  starting transfers between devices: 62.6 us -> 55.7 us
  waiting for transfers between devices: 51.3 us -> 45.8 us
  local copies, waits for them, and re-layouts: 4.87 us -> 2.97 us
    ppermute x49 -> x43, starting transfers between devices: 62.6 us -> 55.7 us  [swap(): return lax.ppermute(array, axis, [(i, i ^ mask) for i in range(size)])]
    ppermute x49 -> x43, waiting for transfers between devices: 51.3 us -> 45.8 us  [swap(): return lax.ppermute(array, axis, [(i, i ^ mask) for i in range(size)])]
    reshape x1 -> x0, local copies, waits for them, and re-layouts: 1.7 us -> none  [shards(): within.reshape(rows, heads_here * HD)]
    dot_general x6 -> x4, matrix products: 9.43 us -> 8.64 us  [the longest x1 3.97 us: shards(): jnp.dot(deal, project(w_query, scale), preferred_element_type=F32)]
  transfers between devices with their start and end apart: 49 -> 43, of which waited for: 17 -> 16; matrix products, arithmetic and copies ran while one was open for 8% -> 8% of each run, Pallas kernels for 10% -> 11%
where the time goes in v3:
time: 141 us
  starting transfers between devices  55.7 us (40%)
  waiting for transfers between devices  45.8 us (32%)
  Pallas kernels  16.8 us (12%)
  matrix products  11.5 us (8%)
  other arithmetic  7.3 us (5%)
  local copies, waits for them, and re-layouts  2.97 us (2%)
    ppermute x43, starting transfers between devices, swap(): return lax.ppermute(array, axis, [(i, i ^ mask) for i in range(size)])  55.7 us
    ppermute x43, waiting for transfers between devices, swap(): return lax.ppermute(array, axis, [(i, i ^ mask) for i in range(size)])  45.8 us
    pallas_call x2, Pallas kernels, experts(): pl.pallas_call(functools.partial(expert_kernel, n_head, n_seq, first, gro...  14.9 us
    dot_general x1, matrix products, shards(): jnp.dot(deal, project(w_query, scale), preferred_element_type=F32)  3.97 us
  transfers between devices with their start and end apart: 43, of which 16 were waited for; matrix products, arithmetic and copies ran while one was open for 8% of the time, Pallas kernels for 11%

profile of v3, /device:TPU:0, one launch (start us, length us, event | category | flops | bytes accessed | tf_op | source)
XLA Modules:
  0.0 140.8 jit_solution(4190434344774715457)
XLA Ops:
  0.0 2.2 %multiply_reduce_fusion = f32[512]{0:T(512)S(1)} fusion(bf16[512,2048]{1,0:T(8,128)(2,1)} %param.12), kind=kLoop, calls=%fused_computation.1 | loop fusion | flops 3145216 | bytes 2099200 | tf_op jit(solution)/shard_map/reduce_sum | solution.py:315
  6.6 3.0 %collective-permute-start = (bf16[4,128,128]{2,1,0:T(8,128)(2,1)S(1)}, bf16[4,128,128]{2,1,0:T(8,128)(2,1)S(1)}, u32[]{:S(2)}, u32[]{:S(2)}) collective-permute-start(bf16[4,128,128]{2,1,0:T(8,128)(2,1)S(1)} %get-tuple-element.93), channel_id=1, source_target_pairs={{0,4},{4,0},{8,12},{12,8},{16,20},{20,16},{24,28},{28,24},{1,5},{5... | collective-permute-start | bytes 393224 | tf_op jit(solution)/shard_map/ppermute | solution.py:32
  13.1 1.9 %collective-permute-start.1 = (bf16[4,128,128]{2,1,0:T(8,128)(2,1)S(1)}, bf16[4,128,128]{2,1,0:T(8,128)(2,1)S(1)}, u32[]{:S(2)}, u32[]{:S(2)}) collective-permute-start(bf16[4,128,128]{2,1,0:T(8,128)(2,1)S(1)} %fusion.24), channel_id=1, source_target_pairs={{0,8},{4,12},{8,0},{12,4},{16,24},{20,28},{24,16},{28,20},{1,9},{5... | collective-permute-start | bytes 393224 | tf_op jit(solution)/shard_map/ppermute | solution.py:32
  14.9 4.0 %convolution_convert_fusion.1.query = bf16[512,512]{1,0:T(8,128)(2,1)} fusion(f32[512]{0:T(512)S(1)} %add_rsqrt_fusion, s32[512]{0:T(512)S(1)} %get-tuple-element.92, bf16[512,2048]{1,0:T(8,128)(2,1)S(1)} %copy-done.8, bf16[2048,512]{1,0:T(8,128)(2,1)} %param.13), kind=kOutput, calls=%fused_computation.9 | convolution fusion | flops 1343225856 | bytes 4722688 | tf_op jit(solution)/shard_map/dot_general | solution.py:326
  19.6 2.6 %collective-permute-start.2 = (bf16[4,128,128]{2,1,0:T(8,128)(2,1)}, bf16[4,128,128]{2,1,0:T(8,128)(2,1)S(1)}, u32[]{:S(2)}, u32[]{:S(2)}) collective-permute-start(bf16[4,128,128]{2,1,0:T(8,128)(2,1)} %fusion.22), channel_id=1, source_target_pairs={{0,16},{4,20},{8,24},{12,28},{16,0},{20,4},{24,8},{28,12},{1,17},{... | collective-permute-start | bytes 393224 | tf_op jit(solution)/shard_map/ppermute | solution.py:32
  22.2 2.7 %fusion.1.within = f32[4,512,128]{2,1,0:T(8,128)S(1)} fusion(bf16[512,4,128]{0,2,1:T(8,128)(2,1)} %bitcast.60, bf16[512,4,128]{0,2,1:T(8,128)(2,1)} %bitcast.58, pred[512,512]{1,0:T(8,128)(4,1)} %iota_compare_fusion.4, bf16[512,512]{1,0:T(8,128)(2,1)} %convolution_convert_fusion.1.query), kind=kOutput, calls=%fused_computation.5 | convolution fusion | flops 538968064 | bytes 2883584 | tf_op jit(solution)/shard_map/hts,shd->htd/dot_general | solution.py:331
  24.9 2.7 %collective-permute-done.2 = bf16[4,128,128]{2,1,0:T(8,128)(2,1)S(1)} collective-permute-done((bf16[4,128,128]{2,1,0:T(8,128)(2,1)}, bf16[4,128,128]{2,1,0:T(8,128)(2,1)S(1)}, u32[]{:S(2)}, u32[]{:S(2)}) %collective-permute-start.2) | collective-permute-done | bytes 131104 | tf_op jit(solution)/shard_map/ppermute | solution.py:32
  30.5 2.5 %collective-permute-done.3 = bf16[256,2048]{1,0:T(8,128)(2,1)S(1)} collective-permute-done((bf16[256,2048]{1,0:T(8,128)(2,1)S(1)}, bf16[256,2048]{1,0:T(8,128)(2,1)S(1)}, u32[]{:S(2)}, u32[]{:S(2)}) %collective-permute-start.3) | collective-permute-done | bytes 1048608 | tf_op jit(solution)/shard_map/ppermute | solution.py:32
  35.4 11.9 %collective-permute-done.4.got = bf16[128,2048]{1,0:T(8,128)(2,1)S(1)} collective-permute-done((bf16[128,2048]{1,0:T(8,128)(2,1)S(1)}, bf16[128,2048]{1,0:T(8,128)(2,1)S(1)}, u32[]{:S(2)}, u32[]{:S(2)}) %collective-permute-start.4) | collective-permute-done | bytes 524320 | tf_op jit(solution)/shard_map/ppermute | solution.py:32
  49.4 2.0 %collective-permute-start.7 = (bf16[32,2048]{1,0:T(8,128)(2,1)S(1)}, bf16[32,2048]{1,0:T(8,128)(2,1)S(1)}, u32[]{:S(2)}, u32[]{:S(2)}) collective-permute-start(bf16[32,2048]{1,0:T(8,128)(2,1)S(1)} %get-tuple-element.67), channel_id=1, source_target_pairs={{0,12},{4,8},{8,4},{12,0},{16,28},{20,24},{24,20},{28,16},{1,13},{... | collective-permute-start | bytes 393224 | tf_op jit(solution)/shard_map/ppermute | solution.py:32
  52.6 2.7 %collective-permute-start.14 = (bf16[16,2048]{1,0:T(8,128)(2,1)S(1)}, bf16[16,2048]{1,0:T(8,128)(2,1)S(1)}, u32[]{:S(2)}, u32[]{:S(2)}) collective-permute-start(bf16[16,2048]{1,0:T(8,128)(2,1)S(1)} %get-tuple-element.59), channel_id=1, source_target_pairs={{0,20},{4,16},{8,28},{12,24},{16,4},{20,0},{24,12},{28,8},{1,21},{... | collective-permute-start | bytes 196616 | tf_op jit(solution)/shard_map/ppermute | solution.py:32
  55.3 2.6 %collective-permute-start.15 = (bf16[16,2048]{1,0:T(8,128)(2,1)S(1)}, bf16[16,2048]{1,0:T(8,128)(2,1)S(1)}, u32[]{:S(2)}, u32[]{:S(2)}) collective-permute-start(bf16[16,2048]{1,0:T(8,128)(2,1)S(1)} %get-tuple-element.58), channel_id=1, source_target_pairs={{0,24},{4,28},{8,16},{12,20},{16,8},{20,12},{24,0},{28,4},{1,25},{... | collective-permute-start | bytes 196616 | tf_op jit(solution)/shard_map/ppermute | solution.py:32
  59.3 4.6 %collective-permute-done.14 = bf16[16,2048]{1,0:T(8,128)(2,1)S(1)} collective-permute-done((bf16[16,2048]{1,0:T(8,128)(2,1)S(1)}, bf16[16,2048]{1,0:T(8,128)(2,1)S(1)}, u32[]{:S(2)}, u32[]{:S(2)}) %collective-permute-start.14) | collective-permute-done | bytes 65568 | tf_op jit(solution)/shard_map/ppermute | solution.py:32
  66.6 2.2 %collective-permute-start.8 = (bf16[16,2048]{1,0:T(8,128)(2,1)S(1)}, bf16[16,2048]{1,0:T(8,128)(2,1)S(1)}, u32[]{:S(2)}, u32[]{:S(2)}) collective-permute-start(bf16[16,2048]{1,0:T(8,128)(2,1)S(1)} %get-tuple-element.65), channel_id=1, source_target_pairs={{0,16},{4,20},{8,24},{12,28},{16,0},{20,4},{24,8},{28,12},{1,17},{... | collective-permute-start | bytes 196616 | tf_op jit(solution)/shard_map/ppermute | solution.py:32
  69.9 1.8 %collective-permute-start.10 = (bf16[16,2048]{1,0:T(8,128)(2,1)S(1)}, bf16[16,2048]{1,0:T(8,128)(2,1)S(1)}, u32[]{:S(2)}, u32[]{:S(2)}) collective-permute-start(bf16[16,2048]{1,0:T(8,128)(2,1)S(1)} %get-tuple-element.63), channel_id=1, source_target_pairs={{0,24},{4,28},{8,16},{12,20},{16,8},{20,12},{24,0},{28,4},{1,25},{... | collective-permute-start | bytes 196616 | tf_op jit(solution)/shard_map/ppermute | solution.py:32
  71.7 2.7 %collective-permute-start.11 = (bf16[16,2048]{1,0:T(8,128)(2,1)S(1)}, bf16[16,2048]{1,0:T(8,128)(2,1)S(1)}, u32[]{:S(2)}, u32[]{:S(2)}) collective-permute-start(bf16[16,2048]{1,0:T(8,128)(2,1)S(1)} %get-tuple-element.62), channel_id=1, source_target_pairs={{0,28},{4,24},{8,20},{12,16},{16,12},{20,8},{24,4},{28,0},{1,29},{... | collective-permute-start | bytes 196616 | tf_op jit(solution)/shard_map/ppermute | solution.py:32
  74.4 2.0 %collective-permute-done.8 = bf16[16,2048]{1,0:T(8,128)(2,1)S(1)} collective-permute-done((bf16[16,2048]{1,0:T(8,128)(2,1)S(1)}, bf16[16,2048]{1,0:T(8,128)(2,1)S(1)}, u32[]{:S(2)}, u32[]{:S(2)}) %collective-permute-start.8) | collective-permute-done | bytes 65568 | tf_op jit(solution)/shard_map/ppermute | solution.py:32
  77.0 2.0 %collective-permute-done.9 = bf16[16,2048]{1,0:T(8,128)(2,1)S(1)} collective-permute-done((bf16[16,2048]{1,0:T(8,128)(2,1)S(1)}, bf16[16,2048]{1,0:T(8,128)(2,1)S(1)}, u32[]{:S(2)}, u32[]{:S(2)}) %collective-permute-start.9) | collective-permute-done | bytes 65568 | tf_op jit(solution)/shard_map/ppermute | solution.py:32
  79.6 7.4 %shard_map.120 = (f32[8,4,16,512]{3,2,1,0:T(8,128)S(1)}, bf16[8,4,16,512]{3,2,1,0:T(8,128)(2,1)S(1)}, bf16[8,4,16,1024]{3,2,1,0:T(8,128)(2,1)S(1)}) custom-call(s32[1]{0:T(128)} %bitcast.4.head, bf16[512,512]{1,0:T(8,128)(2,1)S(1)} %fusion.12.regroup, bf16[128,2048]{1,0:T(8,128)(2,1)S(1)} %constant_dynamic-update-slice_fusion.4.refs_0_, ...), custom_call_target="tpu_custom_call" | custom-call | flops 4294967296 | bytes 24117248 | tf_op jit(solution)/shard_map/pallas_call | solution.py:228
  88.2 2.7 %collective-permute-done.12.refs_1_ = bf16[128,2048]{1,0:T(8,128)(2,1)S(1)} collective-permute-done((bf16[128,2048]{1,0:T(8,128)(2,1)S(1)}, bf16[128,2048]{1,0:T(8,128)(2,1)S(1)}, u32[]{:S(2)}, u32[]{:S(2)}) %collective-permute-start.12) | collective-permute-done | bytes 524320 | tf_op jit(solution)/shard_map/ppermute | solution.py:32
  93.6 7.5 %shard_map.121 = (f32[8,4,16,512]{3,2,1,0:T(8,128)S(1)}, bf16[8,4,16,512]{3,2,1,0:T(8,128)(2,1)S(1)}, bf16[8,4,16,1024]{3,2,1,0:T(8,128)(2,1)S(1)}) custom-call(s32[1]{0:T(128)} %bitcast.4.head, bf16[512,512]{1,0:T(8,128)(2,1)S(1)} %fusion.12.regroup, bf16[128,2048]{1,0:T(8,128)(2,1)S(1)} %constant_dynamic-update-slice_fusion.refs_0_, ...), custom_call_target="tpu_custom_call" | custom-call | flops 4294967296 | bytes 24117248 | tf_op jit(solution)/shard_map/pallas_call | solution.py:228
  102.3 3.5 %collective-permute-done.30 = bf16[8,4,16,512]{3,2,1,0:T(8,128)(2,1)S(1)} collective-permute-done((bf16[8,4,16,512]{3,2,1,0:T(8,128)(2,1)S(1)}, bf16[8,4,16,512]{3,2,1,0:T(8,128)(2,1)S(1)}, u32[]{:S(2)}, u32[]{:S(2)}) %collective-permute-start.30) | collective-permute-done | bytes 524320 | tf_op jit(solution)/shard_map/ppermute | solution.py:32
  107.7 3.5 %collective-permute-start.32 = (bf16[64,512]{1,0:T(8,128)(2,1)S(1)}, bf16[64,512]{1,0:T(8,128)(2,1)S(1)}, u32[]{:S(2)}, u32[]{:S(2)}) collective-permute-start(bf16[64,512]{1,0:T(8,128)(2,1)S(1)} %get-tuple-element.81), channel_id=1, source_target_pairs={{0,16},{4,20},{8,24},{12,28},{16,0},{20,4},{24,8},{28,12},{1,17},{... | collective-permute-start | bytes 196616 | tf_op jit(solution)/shard_map/ppermute | solution.py:32
  111.4 3.0 %collective-permute-start.34 = (bf16[64,512]{1,0:T(8,128)(2,1)S(1)}, bf16[64,512]{1,0:T(8,128)(2,1)S(1)}, u32[]{:S(2)}, u32[]{:S(2)}) collective-permute-start(bf16[64,512]{1,0:T(8,128)(2,1)S(1)} %get-tuple-element.79), channel_id=1, source_target_pairs={{0,24},{4,28},{8,16},{12,20},{16,8},{20,12},{24,0},{28,4},{1,25},{... | collective-permute-start | bytes 196616 | tf_op jit(solution)/shard_map/ppermute | solution.py:32
  114.4 1.6 %collective-permute-start.35 = (bf16[64,512]{1,0:T(8,128)(2,1)S(1)}, bf16[64,512]{1,0:T(8,128)(2,1)S(1)}, u32[]{:S(2)}, u32[]{:S(2)}) collective-permute-start(bf16[64,512]{1,0:T(8,128)(2,1)S(1)} %get-tuple-element.78), channel_id=1, source_target_pairs={{0,28},{4,24},{8,20},{12,16},{16,12},{20,8},{24,4},{28,0},{1,29},{... | collective-permute-start | bytes 196616 | tf_op jit(solution)/shard_map/ppermute | solution.py:32
  116.0 3.6 %collective-permute-done.31 = bf16[8,4,16,512]{3,2,1,0:T(8,128)(2,1)S(1)} collective-permute-done((bf16[8,4,16,512]{3,2,1,0:T(8,128)(2,1)S(1)}, bf16[8,4,16,512]{3,2,1,0:T(8,128)(2,1)S(1)}, u32[]{:S(2)}, u32[]{:S(2)}) %collective-permute-start.31) | collective-permute-done | bytes 524320 | tf_op jit(solution)/shard_map/ppermute | solution.py:32
  122.5 2.7 %collective-permute-start.37 = (bf16[128,512]{1,0:T(8,128)(2,1)S(1)}, bf16[128,512]{1,0:T(8,128)(2,1)S(1)}, u32[]{:S(2)}, u32[]{:S(2)}) collective-permute-start(bf16[128,512]{1,0:T(8,128)(2,1)S(1)} %get-tuple-element.39), channel_id=1, source_target_pairs={{0,8},{4,12},{8,0},{12,4},{16,24},{20,28},{24,16},{28,20},{1,9},{5... | collective-permute-start | bytes 393224 | tf_op jit(solution)/shard_map/ppermute | solution.py:32
  125.7 2.2 %collective-permute-start.39 = (bf16[64,512]{1,0:T(8,128)(2,1)S(1)}, bf16[64,512]{1,0:T(8,128)(2,1)S(1)}, u32[]{:S(2)}, u32[]{:S(2)}) collective-permute-start(bf16[64,512]{1,0:T(8,128)(2,1)S(1)} %bitcast.68), channel_id=1, source_target_pairs={{0,16},{4,20},{8,24},{12,28},{16,0},{20,4},{24,8},{28,12},{1,17},{... | collective-permute-start | bytes 196616 | tf_op jit(solution)/shard_map/ppermute | solution.py:32
  129.1 1.9 %collective-permute-start.41 = (bf16[64,512]{1,0:T(8,128)(2,1)S(1)}, bf16[64,512]{1,0:T(8,128)(2,1)S(1)}, u32[]{:S(2)}, u32[]{:S(2)}) collective-permute-start(bf16[64,512]{1,0:T(8,128)(2,1)S(1)} %bitcast.66), channel_id=1, source_target_pairs={{0,24},{4,28},{8,16},{12,20},{16,8},{20,12},{24,0},{28,4},{1,25},{... | collective-permute-start | bytes 196616 | tf_op jit(solution)/shard_map/ppermute | solution.py:32
  131.0 2.5 %collective-permute-start.42 = (bf16[64,512]{1,0:T(8,128)(2,1)S(1)}, bf16[64,512]{1,0:T(8,128)(2,1)S(1)}, u32[]{:S(2)}, u32[]{:S(2)}) collective-permute-start(bf16[64,512]{1,0:T(8,128)(2,1)S(1)} %bitcast.65), channel_id=1, source_target_pairs={{0,28},{4,24},{8,20},{12,16},{16,12},{20,8},{24,4},{28,0},{1,29},{... | collective-permute-start | bytes 196616 | tf_op jit(solution)/shard_map/ppermute | solution.py:32
  134.8 4.4 %collective-permute-done.40 = bf16[64,512]{1,0:T(8,128)(2,1)S(1)} collective-permute-done((bf16[64,512]{1,0:T(8,128)(2,1)S(1)}, bf16[64,512]{1,0:T(8,128)(2,1)S(1)}, u32[]{:S(2)}, u32[]{:S(2)}) %collective-permute-start.40) | collective-permute-done | bytes 65568 | tf_op jit(solution)/shard_map/ppermute | solution.py:32
  139.2 1.5 %fusion.2 = bf16[512,512]{1,0:T(8,128)(2,1)} fusion(bf16[1024,512]{1,0:T(8,128)(2,1)S(1)} %constant_dynamic-update-slice_fusion.8, s32[512]{0:T(512)S(1)} %bitcast.73), kind=kOutput, calls=%fused_computation.8 | convolution fusion | flops 537657344 | bytes 1574912 | tf_op jit(solution)/shard_map/dot_general | solution.py:115
  (149 shorter events, 36.2 us)
Async XLA Ops:
  6.6 6.5 %collective-permute-start = (bf16[4,128,128]{2,1,0:T(8,128)(2,1)S(1)}, bf16[4,128,128]{2,1,0:T(8,128)(2,1)S(1)}, u32[]{:S(2)}, u32[]{:S(2)}) collective-permute-start(bf16[4,128,128]{2,1,0:T(8,128)(2,1)S(1)} %get-tuple-element.93), channel_id=1, source_target_pairs={{0,4},{4,0},{8,12},{12,8},{16,20},{20,16},{24,28},{28,24},{1,5},{5... | collective-permute-start | bytes 393224 | tf_op jit(solution)/shard_map/ppermute | solution.py:32
  13.1 5.8 %collective-permute-start.1 = (bf16[4,128,128]{2,1,0:T(8,128)(2,1)S(1)}, bf16[4,128,128]{2,1,0:T(8,128)(2,1)S(1)}, u32[]{:S(2)}, u32[]{:S(2)}) collective-permute-start(bf16[4,128,128]{2,1,0:T(8,128)(2,1)S(1)} %fusion.24), channel_id=1, source_target_pairs={{0,8},{4,12},{8,0},{12,4},{16,24},{20,28},{24,16},{28,20},{1,9},{5... | collective-permute-start | bytes 393224 | tf_op jit(solution)/shard_map/ppermute | solution.py:32
  19.6 8.0 %collective-permute-start.2 = (bf16[4,128,128]{2,1,0:T(8,128)(2,1)}, bf16[4,128,128]{2,1,0:T(8,128)(2,1)S(1)}, u32[]{:S(2)}, u32[]{:S(2)}) collective-permute-start(bf16[4,128,128]{2,1,0:T(8,128)(2,1)} %fusion.22), channel_id=1, source_target_pairs={{0,16},{4,20},{8,24},{12,28},{16,0},{20,4},{24,8},{28,12},{1,17},{... | collective-permute-start | bytes 393224 | tf_op jit(solution)/shard_map/ppermute | solution.py:32
  33.3 14.0 %collective-permute-start.4 = (bf16[128,2048]{1,0:T(8,128)(2,1)S(1)}, bf16[128,2048]{1,0:T(8,128)(2,1)S(1)}, u32[]{:S(2)}, u32[]{:S(2)}) collective-permute-start(bf16[128,2048]{1,0:T(8,128)(2,1)S(1)} %get-tuple-element.47), channel_id=1, source_target_pairs={{0,2},{1,3},{2,0},{3,1},{4,6},{5,7},{6,4},{7,5},{8,10},{9,11},{10,... | collective-permute-start | bytes 1572872 | tf_op jit(solution)/shard_map/ppermute | solution.py:32
  47.8 7.5 %collective-permute-start.5 = (bf16[32,2048]{1,0:T(8,128)(2,1)S(1)}, bf16[32,2048]{1,0:T(8,128)(2,1)S(1)}, u32[]{:S(2)}, u32[]{:S(2)}) collective-permute-start(bf16[32,2048]{1,0:T(8,128)(2,1)S(1)} %get-tuple-element.69), channel_id=1, source_target_pairs={{0,4},{4,0},{8,12},{12,8},{16,20},{20,16},{24,28},{28,24},{1,5},{5... | collective-permute-start | bytes 393224 | tf_op jit(solution)/shard_map/ppermute | solution.py:32
  49.4 8.5 %collective-permute-start.6 = (bf16[32,2048]{1,0:T(8,128)(2,1)S(1)}, bf16[32,2048]{1,0:T(8,128)(2,1)S(1)}, u32[]{:S(2)}, u32[]{:S(2)}) collective-permute-start(bf16[32,2048]{1,0:T(8,128)(2,1)S(1)} %get-tuple-element.68), channel_id=1, source_target_pairs={{0,8},{4,12},{8,0},{12,4},{16,24},{20,28},{24,16},{28,20},{1,9},{5... | collective-permute-start | bytes 393224 | tf_op jit(solution)/shard_map/ppermute | solution.py:32
  49.4 9.8 %collective-permute-start.7 = (bf16[32,2048]{1,0:T(8,128)(2,1)S(1)}, bf16[32,2048]{1,0:T(8,128)(2,1)S(1)}, u32[]{:S(2)}, u32[]{:S(2)}) collective-permute-start(bf16[32,2048]{1,0:T(8,128)(2,1)S(1)} %get-tuple-element.67), channel_id=1, source_target_pairs={{0,12},{4,8},{8,4},{12,0},{16,28},{20,24},{24,20},{28,16},{1,13},{... | collective-permute-start | bytes 393224 | tf_op jit(solution)/shard_map/ppermute | solution.py:32
  51.5 7.8 %collective-permute-start.13 = (bf16[16,2048]{1,0:T(8,128)(2,1)S(1)}, bf16[16,2048]{1,0:T(8,128)(2,1)S(1)}, u32[]{:S(2)}, u32[]{:S(2)}) collective-permute-start(bf16[16,2048]{1,0:T(8,128)(2,1)S(1)} %get-tuple-element.60), channel_id=1, source_target_pairs={{0,16},{4,20},{8,24},{12,28},{16,0},{20,4},{24,8},{28,12},{1,17},{... | collective-permute-start | bytes 196616 | tf_op jit(solution)/shard_map/ppermute | solution.py:32
  52.6 11.3 %collective-permute-start.14 = (bf16[16,2048]{1,0:T(8,128)(2,1)S(1)}, bf16[16,2048]{1,0:T(8,128)(2,1)S(1)}, u32[]{:S(2)}, u32[]{:S(2)}) collective-permute-start(bf16[16,2048]{1,0:T(8,128)(2,1)S(1)} %get-tuple-element.59), channel_id=1, source_target_pairs={{0,20},{4,16},{8,28},{12,24},{16,4},{20,0},{24,12},{28,8},{1,21},{... | collective-permute-start | bytes 196616 | tf_op jit(solution)/shard_map/ppermute | solution.py:32
  55.3 8.6 %collective-permute-start.15 = (bf16[16,2048]{1,0:T(8,128)(2,1)S(1)}, bf16[16,2048]{1,0:T(8,128)(2,1)S(1)}, u32[]{:S(2)}, u32[]{:S(2)}) collective-permute-start(bf16[16,2048]{1,0:T(8,128)(2,1)S(1)} %get-tuple-element.58), channel_id=1, source_target_pairs={{0,24},{4,28},{8,16},{12,20},{16,8},{20,12},{24,0},{28,4},{1,25},{... | collective-permute-start | bytes 196616 | tf_op jit(solution)/shard_map/ppermute | solution.py:32
  57.9 7.1 %collective-permute-start.16 = (bf16[16,2048]{1,0:T(8,128)(2,1)S(1)}, bf16[16,2048]{1,0:T(8,128)(2,1)S(1)}, u32[]{:S(2)}, u32[]{:S(2)}) collective-permute-start(bf16[16,2048]{1,0:T(8,128)(2,1)S(1)} %get-tuple-element.57), channel_id=1, source_target_pairs={{0,28},{4,24},{8,20},{12,16},{16,12},{20,8},{24,4},{28,0},{1,29},{... | collective-permute-start | bytes 196616 | tf_op jit(solution)/shard_map/ppermute | solution.py:32
  65.0 11.4 %collective-permute-start.17 = (bf16[128,2048]{1,0:T(8,128)(2,1)S(1)}, bf16[128,2048]{1,0:T(8,128)(2,1)S(1)}, u32[]{:S(2)}, u32[]{:S(2)}) collective-permute-start(bf16[128,2048]{1,0:T(8,128)(2,1)S(1)} %constant_dynamic-update-slice_fusion.4.refs_0_), channel_id=1, source_target_pairs={{0,2},{1,3},{2,0},{3,1},{4,6},{5,7},{6,4},{7,5},{8,10},{9,11},{10,... | collective-permute-start | bytes 1572872 | tf_op jit(solution)/shard_map/ppermute | solution.py:32
  66.6 9.8 %collective-permute-start.8 = (bf16[16,2048]{1,0:T(8,128)(2,1)S(1)}, bf16[16,2048]{1,0:T(8,128)(2,1)S(1)}, u32[]{:S(2)}, u32[]{:S(2)}) collective-permute-start(bf16[16,2048]{1,0:T(8,128)(2,1)S(1)} %get-tuple-element.65), channel_id=1, source_target_pairs={{0,16},{4,20},{8,24},{12,28},{16,0},{20,4},{24,8},{28,12},{1,17},{... | collective-permute-start | bytes 196616 | tf_op jit(solution)/shard_map/ppermute | solution.py:32
  68.9 10.0 %collective-permute-start.9 = (bf16[16,2048]{1,0:T(8,128)(2,1)S(1)}, bf16[16,2048]{1,0:T(8,128)(2,1)S(1)}, u32[]{:S(2)}, u32[]{:S(2)}) collective-permute-start(bf16[16,2048]{1,0:T(8,128)(2,1)S(1)} %get-tuple-element.64), channel_id=1, source_target_pairs={{0,20},{4,16},{8,28},{12,24},{16,4},{20,0},{24,12},{28,8},{1,21},{... | collective-permute-start | bytes 196616 | tf_op jit(solution)/shard_map/ppermute | solution.py:32
  69.9 9.0 %collective-permute-start.10 = (bf16[16,2048]{1,0:T(8,128)(2,1)S(1)}, bf16[16,2048]{1,0:T(8,128)(2,1)S(1)}, u32[]{:S(2)}, u32[]{:S(2)}) collective-permute-start(bf16[16,2048]{1,0:T(8,128)(2,1)S(1)} %get-tuple-element.63), channel_id=1, source_target_pairs={{0,24},{4,28},{8,16},{12,20},{16,8},{20,12},{24,0},{28,4},{1,25},{... | collective-permute-start | bytes 196616 | tf_op jit(solution)/shard_map/ppermute | solution.py:32
  71.7 7.3 %collective-permute-start.11 = (bf16[16,2048]{1,0:T(8,128)(2,1)S(1)}, bf16[16,2048]{1,0:T(8,128)(2,1)S(1)}, u32[]{:S(2)}, u32[]{:S(2)}) collective-permute-start(bf16[16,2048]{1,0:T(8,128)(2,1)S(1)} %get-tuple-element.62), channel_id=1, source_target_pairs={{0,28},{4,24},{8,20},{12,16},{16,12},{20,8},{24,4},{28,0},{1,29},{... | collective-permute-start | bytes 196616 | tf_op jit(solution)/shard_map/ppermute | solution.py:32
  79.0 12.0 %collective-permute-start.12 = (bf16[128,2048]{1,0:T(8,128)(2,1)S(1)}, bf16[128,2048]{1,0:T(8,128)(2,1)S(1)}, u32[]{:S(2)}, u32[]{:S(2)}) collective-permute-start(bf16[128,2048]{1,0:T(8,128)(2,1)S(1)} %constant_dynamic-update-slice_fusion.refs_0_), channel_id=1, source_target_pairs={{0,2},{1,3},{2,0},{3,1},{4,6},{5,7},{6,4},{7,5},{8,10},{9,11},{10,... | collective-permute-start | bytes 1572872 | tf_op jit(solution)/shard_map/ppermute | solution.py:32
  91.9 13.9 %collective-permute-start.30 = (bf16[8,4,16,512]{3,2,1,0:T(8,128)(2,1)S(1)}, bf16[8,4,16,512]{3,2,1,0:T(8,128)(2,1)S(1)}, u32[]{:S(2)}, u32[]{:S(2)}) collective-permute-start(bf16[8,4,16,512]{3,2,1,0:T(8,128)(2,1)S(1)} %fusion.7), channel_id=1, source_target_pairs={{0,2},{1,3},{2,0},{3,1},{4,6},{5,7},{6,4},{7,5},{8,10},{9,11},{10,... | collective-permute-start | bytes 1572872 | tf_op jit(solution)/shard_map/ppermute | solution.py:32
  101.2 4.9 %collective-permute-start.22 = (bf16[2,4,16,1024]{3,2,1,0:T(8,128)(2,1)S(1)}, bf16[2,4,16,1024]{3,2,1,0:T(8,128)(2,1)S(1)}, u32[]{:S(2)}, u32[]{:S(2)}) collective-permute-start(bf16[2,4,16,1024]{3,2,1,0:T(8,128)(2,1)S(1)} %get-tuple-element.53), channel_id=1, source_target_pairs={{0,1},{1,0},{2,3},{3,2},{4,5},{5,4},{6,7},{7,6},{8,9},{9,8},{10,11... | collective-permute-start | bytes 786440 | tf_op jit(solution)/shard_map/ppermute | solution.py:32
  101.4 4.7 %collective-permute-start.23 = (bf16[2,4,16,1024]{3,2,1,0:T(8,128)(2,1)S(1)}, bf16[2,4,16,1024]{3,2,1,0:T(8,128)(2,1)S(1)}, u32[]{:S(2)}, u32[]{:S(2)}) collective-permute-start(bf16[2,4,16,1024]{3,2,1,0:T(8,128)(2,1)S(1)} %get-tuple-element.56), channel_id=1, source_target_pairs={{0,1},{1,0},{2,3},{3,2},{4,5},{5,4},{6,7},{7,6},{8,9},{9,8},{10,11... | collective-permute-start | bytes 786440 | tf_op jit(solution)/shard_map/ppermute | solution.py:32
  106.5 13.1 %collective-permute-start.31 = (bf16[8,4,16,512]{3,2,1,0:T(8,128)(2,1)S(1)}, bf16[8,4,16,512]{3,2,1,0:T(8,128)(2,1)S(1)}, u32[]{:S(2)}, u32[]{:S(2)}) collective-permute-start(bf16[8,4,16,512]{3,2,1,0:T(8,128)(2,1)S(1)} %slice_add_fusion.3), channel_id=1, source_target_pairs={{0,2},{1,3},{2,0},{3,1},{4,6},{5,7},{6,4},{7,5},{8,10},{9,11},{10,... | collective-permute-start | bytes 1572872 | tf_op jit(solution)/shard_map/ppermute | solution.py:32
  107.7 12.3 %collective-permute-start.32 = (bf16[64,512]{1,0:T(8,128)(2,1)S(1)}, bf16[64,512]{1,0:T(8,128)(2,1)S(1)}, u32[]{:S(2)}, u32[]{:S(2)}) collective-permute-start(bf16[64,512]{1,0:T(8,128)(2,1)S(1)} %get-tuple-element.81), channel_id=1, source_target_pairs={{0,16},{4,20},{8,24},{12,28},{16,0},{20,4},{24,8},{28,12},{1,17},{... | collective-permute-start | bytes 196616 | tf_op jit(solution)/shard_map/ppermute | solution.py:32
  111.2 9.0 %collective-permute-start.33 = (bf16[64,512]{1,0:T(8,128)(2,1)S(1)}, bf16[64,512]{1,0:T(8,128)(2,1)S(1)}, u32[]{:S(2)}, u32[]{:S(2)}) collective-permute-start(bf16[64,512]{1,0:T(8,128)(2,1)S(1)} %get-tuple-element.80), channel_id=1, source_target_pairs={{0,20},{4,16},{8,28},{12,24},{16,4},{20,0},{24,12},{28,8},{1,21},{... | collective-permute-start | bytes 196616 | tf_op jit(solution)/shard_map/ppermute | solution.py:32
  111.4 8.8 %collective-permute-start.34 = (bf16[64,512]{1,0:T(8,128)(2,1)S(1)}, bf16[64,512]{1,0:T(8,128)(2,1)S(1)}, u32[]{:S(2)}, u32[]{:S(2)}) collective-permute-start(bf16[64,512]{1,0:T(8,128)(2,1)S(1)} %get-tuple-element.79), channel_id=1, source_target_pairs={{0,24},{4,28},{8,16},{12,20},{16,8},{20,12},{24,0},{28,4},{1,25},{... | collective-permute-start | bytes 196616 | tf_op jit(solution)/shard_map/ppermute | solution.py:32
  114.4 7.1 %collective-permute-start.35 = (bf16[64,512]{1,0:T(8,128)(2,1)S(1)}, bf16[64,512]{1,0:T(8,128)(2,1)S(1)}, u32[]{:S(2)}, u32[]{:S(2)}) collective-permute-start(bf16[64,512]{1,0:T(8,128)(2,1)S(1)} %get-tuple-element.78), channel_id=1, source_target_pairs={{0,28},{4,24},{8,20},{12,16},{16,12},{20,8},{24,4},{28,0},{1,29},{... | collective-permute-start | bytes 196616 | tf_op jit(solution)/shard_map/ppermute | solution.py:32
  121.5 7.6 %collective-permute-start.36 = (bf16[128,512]{1,0:T(8,128)(2,1)S(1)}, bf16[128,512]{1,0:T(8,128)(2,1)S(1)}, u32[]{:S(2)}, u32[]{:S(2)}) collective-permute-start(bf16[128,512]{1,0:T(8,128)(2,1)S(1)} %get-tuple-element.38), channel_id=1, source_target_pairs={{0,4},{4,0},{8,12},{12,8},{16,20},{20,16},{24,28},{28,24},{1,5},{5... | collective-permute-start | bytes 393224 | tf_op jit(solution)/shard_map/ppermute | solution.py:32
  122.5 8.5 %collective-permute-start.37 = (bf16[128,512]{1,0:T(8,128)(2,1)S(1)}, bf16[128,512]{1,0:T(8,128)(2,1)S(1)}, u32[]{:S(2)}, u32[]{:S(2)}) collective-permute-start(bf16[128,512]{1,0:T(8,128)(2,1)S(1)} %get-tuple-element.39), channel_id=1, source_target_pairs={{0,8},{4,12},{8,0},{12,4},{16,24},{20,28},{24,16},{28,20},{1,9},{5... | collective-permute-start | bytes 393224 | tf_op jit(solution)/shard_map/ppermute | solution.py:32
  125.2 9.5 %collective-permute-start.38 = (bf16[128,512]{1,0:T(8,128)(2,1)S(1)}, bf16[128,512]{1,0:T(8,128)(2,1)S(1)}, u32[]{:S(2)}, u32[]{:S(2)}) collective-permute-start(bf16[128,512]{1,0:T(8,128)(2,1)S(1)} %pad_maximum_fusion.2), channel_id=1, source_target_pairs={{0,12},{4,8},{8,4},{12,0},{16,28},{20,24},{24,20},{28,16},{1,13},{... | collective-permute-start | bytes 393224 | tf_op jit(solution)/shard_map/ppermute | solution.py:32
  125.7 9.1 %collective-permute-start.39 = (bf16[64,512]{1,0:T(8,128)(2,1)S(1)}, bf16[64,512]{1,0:T(8,128)(2,1)S(1)}, u32[]{:S(2)}, u32[]{:S(2)}) collective-permute-start(bf16[64,512]{1,0:T(8,128)(2,1)S(1)} %bitcast.68), channel_id=1, source_target_pairs={{0,16},{4,20},{8,24},{12,28},{16,0},{20,4},{24,8},{28,12},{1,17},{... | collective-permute-start | bytes 196616 | tf_op jit(solution)/shard_map/ppermute | solution.py:32
  127.9 11.3 %collective-permute-start.40 = (bf16[64,512]{1,0:T(8,128)(2,1)S(1)}, bf16[64,512]{1,0:T(8,128)(2,1)S(1)}, u32[]{:S(2)}, u32[]{:S(2)}) collective-permute-start(bf16[64,512]{1,0:T(8,128)(2,1)S(1)} %bitcast.67), channel_id=1, source_target_pairs={{0,20},{4,16},{8,28},{12,24},{16,4},{20,0},{24,12},{28,8},{1,21},{... | collective-permute-start | bytes 196616 | tf_op jit(solution)/shard_map/ppermute | solution.py:32
  129.1 10.1 %collective-permute-start.41 = (bf16[64,512]{1,0:T(8,128)(2,1)S(1)}, bf16[64,512]{1,0:T(8,128)(2,1)S(1)}, u32[]{:S(2)}, u32[]{:S(2)}) collective-permute-start(bf16[64,512]{1,0:T(8,128)(2,1)S(1)} %bitcast.66), channel_id=1, source_target_pairs={{0,24},{4,28},{8,16},{12,20},{16,8},{20,12},{24,0},{28,4},{1,25},{... | collective-permute-start | bytes 196616 | tf_op jit(solution)/shard_map/ppermute | solution.py:32
  131.0 8.2 %collective-permute-start.42 = (bf16[64,512]{1,0:T(8,128)(2,1)S(1)}, bf16[64,512]{1,0:T(8,128)(2,1)S(1)}, u32[]{:S(2)}, u32[]{:S(2)}) collective-permute-start(bf16[64,512]{1,0:T(8,128)(2,1)S(1)} %bitcast.65), channel_id=1, source_target_pairs={{0,28},{4,24},{8,20},{12,16},{16,12},{20,8},{24,4},{28,0},{1,29},{... | collective-permute-start | bytes 196616 | tf_op jit(solution)/shard_map/ppermute | solution.py:32
  (26 other events, 175.5 us)

commit v4 on v3

--- a/solution.py
+++ b/solution.py
@@ -153,7 +153,7 @@
     weights = refs[n_head : n_head + 3]
     shared_in = refs[n_head + 3 : n_head + 6]
     own, near, far, held, scales = refs[n_head + 6 : n_head + 11]
-    gate, up, down, shared_gate, shared_up, shared_down, sems = refs[n_head + 11 :]
+    gate, up, down, shared_gate, shared_up, shared_down, cat, sems = refs[n_head + 11 :]
     copies = {
         (i, e): pltpu.make_async_copy(weights[i].at[first + e], kept.at[e], sems.at[i, e])
         for e in range(group)
@@ -167,11 +167,11 @@
     size = pieces[0].shape[0]
     cols = own.shape[-1]
 
+    for i in range(n_head):
+        cat[i * size : (i + 1) * size, :] = pieces[i][...]
     for e in range(group):
         span = slice(e * count, (e + 1) * count)
-        value = dot(regroup[span, :size], pieces[0][...])
-        for i in range(1, n_head):
-            value += dot(regroup[span, i * size : (i + 1) * size], pieces[i][...])
+        value = dot(regroup[span, :], cat[...])
         held[span, :] = value.astype(BF16)
         scale = lax.rsqrt(jnp.mean(value * value, axis=-1, keepdims=True) + EPS)
         scales[span, :] = jnp.broadcast_to(scale, (count, scales.shape[1]))
@@ -235,7 +235,7 @@
         scratch_shapes=[pltpu.VMEM((rows, width), BF16), pltpu.VMEM((rows, 128), F32)]
         + [pltpu.VMEM((group,) + w.shape[1:], w.dtype) for w in weights[:3]]
         + [pltpu.VMEM(w.shape, w.dtype) for w in weights[3:]]
-        + [pltpu.SemaphoreType.DMA((3, group + 1))],
+        + [pltpu.VMEM((rows, width), BF16), pltpu.SemaphoreType.DMA((3, group + 1))],
         cost_estimate=pl.CostEstimate(
             flops=2 * rows * width * (rows + 6 * weights[0].shape[2]),
             transcendentals=rows * weights[0].shape[2],

time: 141 us -> 141 us (level)
  waiting for transfers between devices: 45.8 us -> 47.5 us
  Pallas kernels: 16.8 us -> 15.2 us
    pallas_call x2, Pallas kernels: 14.9 us -> 13.2 us  [experts(): pl.pallas_call(functools.partial(expert_kernel, n_head, n_seq, first, gro...]
    ppermute x43, waiting for transfers between devices: 45.8 us -> 47.5 us  [swap(): return lax.ppermute(array, axis, [(i, i ^ mask) for i in range(size)])]
  transfers between devices with their start and end apart: 43 -> 43, of which waited for: 16 -> 16; matrix products, arithmetic and copies ran while one was open for 8% -> 8% of each run, Pallas kernels for 11% -> 9%
where the time goes in v4:
time: 141 us
  starting transfers between devices  55.7 us (40%)
  waiting for transfers between devices  47.5 us (34%)
  Pallas kernels  15.2 us (11%)
  matrix products  11.5 us (8%)
  other arithmetic  7.3 us (5%)
  local copies, waits for them, and re-layouts  2.97 us (2%)
    ppermute x43, starting transfers between devices, swap(): return lax.ppermute(array, axis, [(i, i ^ mask) for i in range(size)])  55.7 us
    ppermute x43, waiting for transfers between devices, swap(): return lax.ppermute(array, axis, [(i, i ^ mask) for i in range(size)])  47.5 us
    pallas_call x2, Pallas kernels, experts(): pl.pallas_call(functools.partial(expert_kernel, n_head, n_seq, first, gro...  13.2 us
    dot_general x1, matrix products, shards(): jnp.dot(deal, project(w_query, scale), preferred_element_type=F32)  3.97 us
  transfers between devices with their start and end apart: 43, of which 16 were waited for; matrix products, arithmetic and copies ran while one was open for 8% of the time, Pallas kernels for 9%

profile of v4, /device:TPU:0, one launch (start us, length us, event | category | flops | bytes accessed | tf_op | source)
XLA Modules:
  0.0 140.8 jit_solution(427869953825790340)
XLA Ops:
  0.0 2.2 %multiply_reduce_fusion = f32[512]{0:T(512)S(1)} fusion(bf16[512,2048]{1,0:T(8,128)(2,1)} %param.12), kind=kLoop, calls=%fused_computation.1 | loop fusion | flops 3145216 | bytes 2099200 | tf_op jit(solution)/shard_map/reduce_sum | solution.py:315
  6.6 3.0 %collective-permute-start = (bf16[4,128,128]{2,1,0:T(8,128)(2,1)S(1)}, bf16[4,128,128]{2,1,0:T(8,128)(2,1)S(1)}, u32[]{:S(2)}, u32[]{:S(2)}) collective-permute-start(bf16[4,128,128]{2,1,0:T(8,128)(2,1)S(1)} %get-tuple-element.93), channel_id=1, source_target_pairs={{0,4},{4,0},{8,12},{12,8},{16,20},{20,16},{24,28},{28,24},{1,5},{5... | collective-permute-start | bytes 393224 | tf_op jit(solution)/shard_map/ppermute | solution.py:32
  13.1 1.9 %collective-permute-start.1 = (bf16[4,128,128]{2,1,0:T(8,128)(2,1)S(1)}, bf16[4,128,128]{2,1,0:T(8,128)(2,1)S(1)}, u32[]{:S(2)}, u32[]{:S(2)}) collective-permute-start(bf16[4,128,128]{2,1,0:T(8,128)(2,1)S(1)} %fusion.24), channel_id=1, source_target_pairs={{0,8},{4,12},{8,0},{12,4},{16,24},{20,28},{24,16},{28,20},{1,9},{5... | collective-permute-start | bytes 393224 | tf_op jit(solution)/shard_map/ppermute | solution.py:32
  14.9 4.0 %convolution_convert_fusion.1.query = bf16[512,512]{1,0:T(8,128)(2,1)} fusion(f32[512]{0:T(512)S(1)} %add_rsqrt_fusion, s32[512]{0:T(512)S(1)} %get-tuple-element.92, bf16[512,2048]{1,0:T(8,128)(2,1)S(1)} %copy-done.8, bf16[2048,512]{1,0:T(8,128)(2,1)} %param.13), kind=kOutput, calls=%fused_computation.9 | convolution fusion | flops 1343225856 | bytes 4722688 | tf_op jit(solution)/shard_map/dot_general | solution.py:326
  19.6 2.6 %collective-permute-start.2 = (bf16[4,128,128]{2,1,0:T(8,128)(2,1)}, bf16[4,128,128]{2,1,0:T(8,128)(2,1)S(1)}, u32[]{:S(2)}, u32[]{:S(2)}) collective-permute-start(bf16[4,128,128]{2,1,0:T(8,128)(2,1)} %fusion.22), channel_id=1, source_target_pairs={{0,16},{4,20},{8,24},{12,28},{16,0},{20,4},{24,8},{28,12},{1,17},{... | collective-permute-start | bytes 393224 | tf_op jit(solution)/shard_map/ppermute | solution.py:32
  22.2 2.7 %fusion.1.within = f32[4,512,128]{2,1,0:T(8,128)S(1)} fusion(bf16[512,4,128]{0,2,1:T(8,128)(2,1)} %bitcast.60, bf16[512,4,128]{0,2,1:T(8,128)(2,1)} %bitcast.58, pred[512,512]{1,0:T(8,128)(4,1)} %iota_compare_fusion.4, bf16[512,512]{1,0:T(8,128)(2,1)} %convolution_convert_fusion.1.query), kind=kOutput, calls=%fused_computation.5 | convolution fusion | flops 538968064 | bytes 2883584 | tf_op jit(solution)/shard_map/hts,shd->htd/dot_general | solution.py:331
  24.9 2.7 %collective-permute-done.2 = bf16[4,128,128]{2,1,0:T(8,128)(2,1)S(1)} collective-permute-done((bf16[4,128,128]{2,1,0:T(8,128)(2,1)}, bf16[4,128,128]{2,1,0:T(8,128)(2,1)S(1)}, u32[]{:S(2)}, u32[]{:S(2)}) %collective-permute-start.2) | collective-permute-done | bytes 131104 | tf_op jit(solution)/shard_map/ppermute | solution.py:32
  30.5 2.5 %collective-permute-done.3 = bf16[256,2048]{1,0:T(8,128)(2,1)S(1)} collective-permute-done((bf16[256,2048]{1,0:T(8,128)(2,1)S(1)}, bf16[256,2048]{1,0:T(8,128)(2,1)S(1)}, u32[]{:S(2)}, u32[]{:S(2)}) %collective-permute-start.3) | collective-permute-done | bytes 1048608 | tf_op jit(solution)/shard_map/ppermute | solution.py:32
  35.4 11.9 %collective-permute-done.4.got = bf16[128,2048]{1,0:T(8,128)(2,1)S(1)} collective-permute-done((bf16[128,2048]{1,0:T(8,128)(2,1)S(1)}, bf16[128,2048]{1,0:T(8,128)(2,1)S(1)}, u32[]{:S(2)}, u32[]{:S(2)}) %collective-permute-start.4) | collective-permute-done | bytes 524320 | tf_op jit(solution)/shard_map/ppermute | solution.py:32
  49.4 2.0 %collective-permute-start.7 = (bf16[32,2048]{1,0:T(8,128)(2,1)S(1)}, bf16[32,2048]{1,0:T(8,128)(2,1)S(1)}, u32[]{:S(2)}, u32[]{:S(2)}) collective-permute-start(bf16[32,2048]{1,0:T(8,128)(2,1)S(1)} %get-tuple-element.67), channel_id=1, source_target_pairs={{0,12},{4,8},{8,4},{12,0},{16,28},{20,24},{24,20},{28,16},{1,13},{... | collective-permute-start | bytes 393224 | tf_op jit(solution)/shard_map/ppermute | solution.py:32
  52.6 2.7 %collective-permute-start.14 = (bf16[16,2048]{1,0:T(8,128)(2,1)S(1)}, bf16[16,2048]{1,0:T(8,128)(2,1)S(1)}, u32[]{:S(2)}, u32[]{:S(2)}) collective-permute-start(bf16[16,2048]{1,0:T(8,128)(2,1)S(1)} %get-tuple-element.59), channel_id=1, source_target_pairs={{0,20},{4,16},{8,28},{12,24},{16,4},{20,0},{24,12},{28,8},{1,21},{... | collective-permute-start | bytes 196616 | tf_op jit(solution)/shard_map/ppermute | solution.py:32
  55.3 2.6 %collective-permute-start.15 = (bf16[16,2048]{1,0:T(8,128)(2,1)S(1)}, bf16[16,2048]{1,0:T(8,128)(2,1)S(1)}, u32[]{:S(2)}, u32[]{:S(2)}) collective-permute-start(bf16[16,2048]{1,0:T(8,128)(2,1)S(1)} %get-tuple-element.58), channel_id=1, source_target_pairs={{0,24},{4,28},{8,16},{12,20},{16,8},{20,12},{24,0},{28,4},{1,25},{... | collective-permute-start | bytes 196616 | tf_op jit(solution)/shard_map/ppermute | solution.py:32
  59.3 4.6 %collective-permute-done.14 = bf16[16,2048]{1,0:T(8,128)(2,1)S(1)} collective-permute-done((bf16[16,2048]{1,0:T(8,128)(2,1)S(1)}, bf16[16,2048]{1,0:T(8,128)(2,1)S(1)}, u32[]{:S(2)}, u32[]{:S(2)}) %collective-permute-start.14) | collective-permute-done | bytes 65568 | tf_op jit(solution)/shard_map/ppermute | solution.py:32
  66.6 2.2 %collective-permute-start.8 = (bf16[16,2048]{1,0:T(8,128)(2,1)S(1)}, bf16[16,2048]{1,0:T(8,128)(2,1)S(1)}, u32[]{:S(2)}, u32[]{:S(2)}) collective-permute-start(bf16[16,2048]{1,0:T(8,128)(2,1)S(1)} %get-tuple-element.65), channel_id=1, source_target_pairs={{0,16},{4,20},{8,24},{12,28},{16,0},{20,4},{24,8},{28,12},{1,17},{... | collective-permute-start | bytes 196616 | tf_op jit(solution)/shard_map/ppermute | solution.py:32
  69.9 1.8 %collective-permute-start.10 = (bf16[16,2048]{1,0:T(8,128)(2,1)S(1)}, bf16[16,2048]{1,0:T(8,128)(2,1)S(1)}, u32[]{:S(2)}, u32[]{:S(2)}) collective-permute-start(bf16[16,2048]{1,0:T(8,128)(2,1)S(1)} %get-tuple-element.63), channel_id=1, source_target_pairs={{0,24},{4,28},{8,16},{12,20},{16,8},{20,12},{24,0},{28,4},{1,25},{... | collective-permute-start | bytes 196616 | tf_op jit(solution)/shard_map/ppermute | solution.py:32
  71.7 2.7 %collective-permute-start.11 = (bf16[16,2048]{1,0:T(8,128)(2,1)S(1)}, bf16[16,2048]{1,0:T(8,128)(2,1)S(1)}, u32[]{:S(2)}, u32[]{:S(2)}) collective-permute-start(bf16[16,2048]{1,0:T(8,128)(2,1)S(1)} %get-tuple-element.62), channel_id=1, source_target_pairs={{0,28},{4,24},{8,20},{12,16},{16,12},{20,8},{24,4},{28,0},{1,29},{... | collective-permute-start | bytes 196616 | tf_op jit(solution)/shard_map/ppermute | solution.py:32
  74.4 2.0 %collective-permute-done.8 = bf16[16,2048]{1,0:T(8,128)(2,1)S(1)} collective-permute-done((bf16[16,2048]{1,0:T(8,128)(2,1)S(1)}, bf16[16,2048]{1,0:T(8,128)(2,1)S(1)}, u32[]{:S(2)}, u32[]{:S(2)}) %collective-permute-start.8) | collective-permute-done | bytes 65568 | tf_op jit(solution)/shard_map/ppermute | solution.py:32
  77.0 2.0 %collective-permute-done.9 = bf16[16,2048]{1,0:T(8,128)(2,1)S(1)} collective-permute-done((bf16[16,2048]{1,0:T(8,128)(2,1)S(1)}, bf16[16,2048]{1,0:T(8,128)(2,1)S(1)}, u32[]{:S(2)}, u32[]{:S(2)}) %collective-permute-start.9) | collective-permute-done | bytes 65568 | tf_op jit(solution)/shard_map/ppermute | solution.py:32
  79.6 6.6 %shard_map.120 = (f32[8,4,16,512]{3,2,1,0:T(8,128)S(1)}, bf16[8,4,16,512]{3,2,1,0:T(8,128)(2,1)S(1)}, bf16[8,4,16,1024]{3,2,1,0:T(8,128)(2,1)S(1)}) custom-call(s32[1]{0:T(128)} %bitcast.4.head, bf16[512,512]{1,0:T(8,128)(2,1)S(1)} %fusion.12.regroup, bf16[128,2048]{1,0:T(8,128)(2,1)S(1)} %constant_dynamic-update-slice_fusion.4.refs_0_, ...), custom_call_target="tpu_custom_call" | custom-call | flops 4294967296 | bytes 24117248 | tf_op jit(solution)/shard_map/pallas_call | solution.py:228
  87.4 3.6 %collective-permute-done.12.refs_1_ = bf16[128,2048]{1,0:T(8,128)(2,1)S(1)} collective-permute-done((bf16[128,2048]{1,0:T(8,128)(2,1)S(1)}, bf16[128,2048]{1,0:T(8,128)(2,1)S(1)}, u32[]{:S(2)}, u32[]{:S(2)}) %collective-permute-start.12) | collective-permute-done | bytes 524320 | tf_op jit(solution)/shard_map/ppermute | solution.py:32
  93.6 6.6 %shard_map.121 = (f32[8,4,16,512]{3,2,1,0:T(8,128)S(1)}, bf16[8,4,16,512]{3,2,1,0:T(8,128)(2,1)S(1)}, bf16[8,4,16,1024]{3,2,1,0:T(8,128)(2,1)S(1)}) custom-call(s32[1]{0:T(128)} %bitcast.4.head, bf16[512,512]{1,0:T(8,128)(2,1)S(1)} %fusion.12.regroup, bf16[128,2048]{1,0:T(8,128)(2,1)S(1)} %constant_dynamic-update-slice_fusion.refs_0_, ...), custom_call_target="tpu_custom_call" | custom-call | flops 4294967296 | bytes 24117248 | tf_op jit(solution)/shard_map/pallas_call | solution.py:228
  101.4 4.4 %collective-permute-done.30 = bf16[8,4,16,512]{3,2,1,0:T(8,128)(2,1)S(1)} collective-permute-done((bf16[8,4,16,512]{3,2,1,0:T(8,128)(2,1)S(1)}, bf16[8,4,16,512]{3,2,1,0:T(8,128)(2,1)S(1)}, u32[]{:S(2)}, u32[]{:S(2)}) %collective-permute-start.30) | collective-permute-done | bytes 524320 | tf_op jit(solution)/shard_map/ppermute | solution.py:32
  107.7 3.5 %collective-permute-start.32 = (bf16[64,512]{1,0:T(8,128)(2,1)S(1)}, bf16[64,512]{1,0:T(8,128)(2,1)S(1)}, u32[]{:S(2)}, u32[]{:S(2)}) collective-permute-start(bf16[64,512]{1,0:T(8,128)(2,1)S(1)} %get-tuple-element.81), channel_id=1, source_target_pairs={{0,16},{4,20},{8,24},{12,28},{16,0},{20,4},{24,8},{28,12},{1,17},{... | collective-permute-start | bytes 196616 | tf_op jit(solution)/shard_map/ppermute | solution.py:32
  111.4 3.0 %collective-permute-start.34 = (bf16[64,512]{1,0:T(8,128)(2,1)S(1)}, bf16[64,512]{1,0:T(8,128)(2,1)S(1)}, u32[]{:S(2)}, u32[]{:S(2)}) collective-permute-start(bf16[64,512]{1,0:T(8,128)(2,1)S(1)} %get-tuple-element.79), channel_id=1, source_target_pairs={{0,24},{4,28},{8,16},{12,20},{16,8},{20,12},{24,0},{28,4},{1,25},{... | collective-permute-start | bytes 196616 | tf_op jit(solution)/shard_map/ppermute | solution.py:32
  114.4 1.6 %collective-permute-start.35 = (bf16[64,512]{1,0:T(8,128)(2,1)S(1)}, bf16[64,512]{1,0:T(8,128)(2,1)S(1)}, u32[]{:S(2)}, u32[]{:S(2)}) collective-permute-start(bf16[64,512]{1,0:T(8,128)(2,1)S(1)} %get-tuple-element.78), channel_id=1, source_target_pairs={{0,28},{4,24},{8,20},{12,16},{16,12},{20,8},{24,4},{28,0},{1,29},{... | collective-permute-start | bytes 196616 | tf_op jit(solution)/shard_map/ppermute | solution.py:32
  116.0 3.6 %collective-permute-done.31 = bf16[8,4,16,512]{3,2,1,0:T(8,128)(2,1)S(1)} collective-permute-done((bf16[8,4,16,512]{3,2,1,0:T(8,128)(2,1)S(1)}, bf16[8,4,16,512]{3,2,1,0:T(8,128)(2,1)S(1)}, u32[]{:S(2)}, u32[]{:S(2)}) %collective-permute-start.31) | collective-permute-done | bytes 524320 | tf_op jit(solution)/shard_map/ppermute | solution.py:32
  122.5 2.7 %collective-permute-start.37 = (bf16[128,512]{1,0:T(8,128)(2,1)S(1)}, bf16[128,512]{1,0:T(8,128)(2,1)S(1)}, u32[]{:S(2)}, u32[]{:S(2)}) collective-permute-start(bf16[128,512]{1,0:T(8,128)(2,1)S(1)} %get-tuple-element.39), channel_id=1, source_target_pairs={{0,8},{4,12},{8,0},{12,4},{16,24},{20,28},{24,16},{28,20},{1,9},{5... | collective-permute-start | bytes 393224 | tf_op jit(solution)/shard_map/ppermute | solution.py:32
  125.7 2.2 %collective-permute-start.39 = (bf16[64,512]{1,0:T(8,128)(2,1)S(1)}, bf16[64,512]{1,0:T(8,128)(2,1)S(1)}, u32[]{:S(2)}, u32[]{:S(2)}) collective-permute-start(bf16[64,512]{1,0:T(8,128)(2,1)S(1)} %bitcast.68), channel_id=1, source_target_pairs={{0,16},{4,20},{8,24},{12,28},{16,0},{20,4},{24,8},{28,12},{1,17},{... | collective-permute-start | bytes 196616 | tf_op jit(solution)/shard_map/ppermute | solution.py:32
  129.1 1.9 %collective-permute-start.41 = (bf16[64,512]{1,0:T(8,128)(2,1)S(1)}, bf16[64,512]{1,0:T(8,128)(2,1)S(1)}, u32[]{:S(2)}, u32[]{:S(2)}) collective-permute-start(bf16[64,512]{1,0:T(8,128)(2,1)S(1)} %bitcast.66), channel_id=1, source_target_pairs={{0,24},{4,28},{8,16},{12,20},{16,8},{20,12},{24,0},{28,4},{1,25},{... | collective-permute-start | bytes 196616 | tf_op jit(solution)/shard_map/ppermute | solution.py:32
  131.0 2.5 %collective-permute-start.42 = (bf16[64,512]{1,0:T(8,128)(2,1)S(1)}, bf16[64,512]{1,0:T(8,128)(2,1)S(1)}, u32[]{:S(2)}, u32[]{:S(2)}) collective-permute-start(bf16[64,512]{1,0:T(8,128)(2,1)S(1)} %bitcast.65), channel_id=1, source_target_pairs={{0,28},{4,24},{8,20},{12,16},{16,12},{20,8},{24,4},{28,0},{1,29},{... | collective-permute-start | bytes 196616 | tf_op jit(solution)/shard_map/ppermute | solution.py:32
  134.8 4.4 %collective-permute-done.40 = bf16[64,512]{1,0:T(8,128)(2,1)S(1)} collective-permute-done((bf16[64,512]{1,0:T(8,128)(2,1)S(1)}, bf16[64,512]{1,0:T(8,128)(2,1)S(1)}, u32[]{:S(2)}, u32[]{:S(2)}) %collective-permute-start.40) | collective-permute-done | bytes 65568 | tf_op jit(solution)/shard_map/ppermute | solution.py:32
  139.2 1.5 %fusion.2 = bf16[512,512]{1,0:T(8,128)(2,1)} fusion(bf16[1024,512]{1,0:T(8,128)(2,1)S(1)} %constant_dynamic-update-slice_fusion.8, s32[512]{0:T(512)S(1)} %bitcast.73), kind=kOutput, calls=%fused_computation.8 | convolution fusion | flops 537657344 | bytes 1574912 | tf_op jit(solution)/shard_map/dot_general | solution.py:115
  (149 shorter events, 36.2 us)
Async XLA Ops:
  6.6 6.5 %collective-permute-start = (bf16[4,128,128]{2,1,0:T(8,128)(2,1)S(1)}, bf16[4,128,128]{2,1,0:T(8,128)(2,1)S(1)}, u32[]{:S(2)}, u32[]{:S(2)}) collective-permute-start(bf16[4,128,128]{2,1,0:T(8,128)(2,1)S(1)} %get-tuple-element.93), channel_id=1, source_target_pairs={{0,4},{4,0},{8,12},{12,8},{16,20},{20,16},{24,28},{28,24},{1,5},{5... | collective-permute-start | bytes 393224 | tf_op jit(solution)/shard_map/ppermute | solution.py:32
  13.1 5.8 %collective-permute-start.1 = (bf16[4,128,128]{2,1,0:T(8,128)(2,1)S(1)}, bf16[4,128,128]{2,1,0:T(8,128)(2,1)S(1)}, u32[]{:S(2)}, u32[]{:S(2)}) collective-permute-start(bf16[4,128,128]{2,1,0:T(8,128)(2,1)S(1)} %fusion.24), channel_id=1, source_target_pairs={{0,8},{4,12},{8,0},{12,4},{16,24},{20,28},{24,16},{28,20},{1,9},{5... | collective-permute-start | bytes 393224 | tf_op jit(solution)/shard_map/ppermute | solution.py:32
  19.6 8.0 %collective-permute-start.2 = (bf16[4,128,128]{2,1,0:T(8,128)(2,1)}, bf16[4,128,128]{2,1,0:T(8,128)(2,1)S(1)}, u32[]{:S(2)}, u32[]{:S(2)}) collective-permute-start(bf16[4,128,128]{2,1,0:T(8,128)(2,1)} %fusion.22), channel_id=1, source_target_pairs={{0,16},{4,20},{8,24},{12,28},{16,0},{20,4},{24,8},{28,12},{1,17},{... | collective-permute-start | bytes 393224 | tf_op jit(solution)/shard_map/ppermute | solution.py:32
  33.3 14.0 %collective-permute-start.4 = (bf16[128,2048]{1,0:T(8,128)(2,1)S(1)}, bf16[128,2048]{1,0:T(8,128)(2,1)S(1)}, u32[]{:S(2)}, u32[]{:S(2)}) collective-permute-start(bf16[128,2048]{1,0:T(8,128)(2,1)S(1)} %get-tuple-element.47), channel_id=1, source_target_pairs={{0,2},{1,3},{2,0},{3,1},{4,6},{5,7},{6,4},{7,5},{8,10},{9,11},{10,... | collective-permute-start | bytes 1572872 | tf_op jit(solution)/shard_map/ppermute | solution.py:32
  47.8 7.5 %collective-permute-start.5 = (bf16[32,2048]{1,0:T(8,128)(2,1)S(1)}, bf16[32,2048]{1,0:T(8,128)(2,1)S(1)}, u32[]{:S(2)}, u32[]{:S(2)}) collective-permute-start(bf16[32,2048]{1,0:T(8,128)(2,1)S(1)} %get-tuple-element.69), channel_id=1, source_target_pairs={{0,4},{4,0},{8,12},{12,8},{16,20},{20,16},{24,28},{28,24},{1,5},{5... | collective-permute-start | bytes 393224 | tf_op jit(solution)/shard_map/ppermute | solution.py:32
  49.4 8.5 %collective-permute-start.6 = (bf16[32,2048]{1,0:T(8,128)(2,1)S(1)}, bf16[32,2048]{1,0:T(8,128)(2,1)S(1)}, u32[]{:S(2)}, u32[]{:S(2)}) collective-permute-start(bf16[32,2048]{1,0:T(8,128)(2,1)S(1)} %get-tuple-element.68), channel_id=1, source_target_pairs={{0,8},{4,12},{8,0},{12,4},{16,24},{20,28},{24,16},{28,20},{1,9},{5... | collective-permute-start | bytes 393224 | tf_op jit(solution)/shard_map/ppermute | solution.py:32
  49.4 9.8 %collective-permute-start.7 = (bf16[32,2048]{1,0:T(8,128)(2,1)S(1)}, bf16[32,2048]{1,0:T(8,128)(2,1)S(1)}, u32[]{:S(2)}, u32[]{:S(2)}) collective-permute-start(bf16[32,2048]{1,0:T(8,128)(2,1)S(1)} %get-tuple-element.67), channel_id=1, source_target_pairs={{0,12},{4,8},{8,4},{12,0},{16,28},{20,24},{24,20},{28,16},{1,13},{... | collective-permute-start | bytes 393224 | tf_op jit(solution)/shard_map/ppermute | solution.py:32
  51.5 7.8 %collective-permute-start.13 = (bf16[16,2048]{1,0:T(8,128)(2,1)S(1)}, bf16[16,2048]{1,0:T(8,128)(2,1)S(1)}, u32[]{:S(2)}, u32[]{:S(2)}) collective-permute-start(bf16[16,2048]{1,0:T(8,128)(2,1)S(1)} %get-tuple-element.60), channel_id=1, source_target_pairs={{0,16},{4,20},{8,24},{12,28},{16,0},{20,4},{24,8},{28,12},{1,17},{... | collective-permute-start | bytes 196616 | tf_op jit(solution)/shard_map/ppermute | solution.py:32
  52.6 11.3 %collective-permute-start.14 = (bf16[16,2048]{1,0:T(8,128)(2,1)S(1)}, bf16[16,2048]{1,0:T(8,128)(2,1)S(1)}, u32[]{:S(2)}, u32[]{:S(2)}) collective-permute-start(bf16[16,2048]{1,0:T(8,128)(2,1)S(1)} %get-tuple-element.59), channel_id=1, source_target_pairs={{0,20},{4,16},{8,28},{12,24},{16,4},{20,0},{24,12},{28,8},{1,21},{... | collective-permute-start | bytes 196616 | tf_op jit(solution)/shard_map/ppermute | solution.py:32
  55.3 8.6 %collective-permute-start.15 = (bf16[16,2048]{1,0:T(8,128)(2,1)S(1)}, bf16[16,2048]{1,0:T(8,128)(2,1)S(1)}, u32[]{:S(2)}, u32[]{:S(2)}) collective-permute-start(bf16[16,2048]{1,0:T(8,128)(2,1)S(1)} %get-tuple-element.58), channel_id=1, source_target_pairs={{0,24},{4,28},{8,16},{12,20},{16,8},{20,12},{24,0},{28,4},{1,25},{... | collective-permute-start | bytes 196616 | tf_op jit(solution)/shard_map/ppermute | solution.py:32
  57.9 7.1 %collective-permute-start.16 = (bf16[16,2048]{1,0:T(8,128)(2,1)S(1)}, bf16[16,2048]{1,0:T(8,128)(2,1)S(1)}, u32[]{:S(2)}, u32[]{:S(2)}) collective-permute-start(bf16[16,2048]{1,0:T(8,128)(2,1)S(1)} %get-tuple-element.57), channel_id=1, source_target_pairs={{0,28},{4,24},{8,20},{12,16},{16,12},{20,8},{24,4},{28,0},{1,29},{... | collective-permute-start | bytes 196616 | tf_op jit(solution)/shard_map/ppermute | solution.py:32
  65.0 11.4 %collective-permute-start.17 = (bf16[128,2048]{1,0:T(8,128)(2,1)S(1)}, bf16[128,2048]{1,0:T(8,128)(2,1)S(1)}, u32[]{:S(2)}, u32[]{:S(2)}) collective-permute-start(bf16[128,2048]{1,0:T(8,128)(2,1)S(1)} %constant_dynamic-update-slice_fusion.4.refs_0_), channel_id=1, source_target_pairs={{0,2},{1,3},{2,0},{3,1},{4,6},{5,7},{6,4},{7,5},{8,10},{9,11},{10,... | collective-permute-start | bytes 1572872 | tf_op jit(solution)/shard_map/ppermute | solution.py:32
  66.6 9.8 %collective-permute-start.8 = (bf16[16,2048]{1,0:T(8,128)(2,1)S(1)}, bf16[16,2048]{1,0:T(8,128)(2,1)S(1)}, u32[]{:S(2)}, u32[]{:S(2)}) collective-permute-start(bf16[16,2048]{1,0:T(8,128)(2,1)S(1)} %get-tuple-element.65), channel_id=1, source_target_pairs={{0,16},{4,20},{8,24},{12,28},{16,0},{20,4},{24,8},{28,12},{1,17},{... | collective-permute-start | bytes 196616 | tf_op jit(solution)/shard_map/ppermute | solution.py:32
  68.9 10.0 %collective-permute-start.9 = (bf16[16,2048]{1,0:T(8,128)(2,1)S(1)}, bf16[16,2048]{1,0:T(8,128)(2,1)S(1)}, u32[]{:S(2)}, u32[]{:S(2)}) collective-permute-start(bf16[16,2048]{1,0:T(8,128)(2,1)S(1)} %get-tuple-element.64), channel_id=1, source_target_pairs={{0,20},{4,16},{8,28},{12,24},{16,4},{20,0},{24,12},{28,8},{1,21},{... | collective-permute-start | bytes 196616 | tf_op jit(solution)/shard_map/ppermute | solution.py:32
  69.9 9.0 %collective-permute-start.10 = (bf16[16,2048]{1,0:T(8,128)(2,1)S(1)}, bf16[16,2048]{1,0:T(8,128)(2,1)S(1)}, u32[]{:S(2)}, u32[]{:S(2)}) collective-permute-start(bf16[16,2048]{1,0:T(8,128)(2,1)S(1)} %get-tuple-element.63), channel_id=1, source_target_pairs={{0,24},{4,28},{8,16},{12,20},{16,8},{20,12},{24,0},{28,4},{1,25},{... | collective-permute-start | bytes 196616 | tf_op jit(solution)/shard_map/ppermute | solution.py:32
  71.7 7.3 %collective-permute-start.11 = (bf16[16,2048]{1,0:T(8,128)(2,1)S(1)}, bf16[16,2048]{1,0:T(8,128)(2,1)S(1)}, u32[]{:S(2)}, u32[]{:S(2)}) collective-permute-start(bf16[16,2048]{1,0:T(8,128)(2,1)S(1)} %get-tuple-element.62), channel_id=1, source_target_pairs={{0,28},{4,24},{8,20},{12,16},{16,12},{20,8},{24,4},{28,0},{1,29},{... | collective-permute-start | bytes 196616 | tf_op jit(solution)/shard_map/ppermute | solution.py:32
  79.0 12.0 %collective-permute-start.12 = (bf16[128,2048]{1,0:T(8,128)(2,1)S(1)}, bf16[128,2048]{1,0:T(8,128)(2,1)S(1)}, u32[]{:S(2)}, u32[]{:S(2)}) collective-permute-start(bf16[128,2048]{1,0:T(8,128)(2,1)S(1)} %constant_dynamic-update-slice_fusion.refs_0_), channel_id=1, source_target_pairs={{0,2},{1,3},{2,0},{3,1},{4,6},{5,7},{6,4},{7,5},{8,10},{9,11},{10,... | collective-permute-start | bytes 1572872 | tf_op jit(solution)/shard_map/ppermute | solution.py:32
  91.9 13.9 %collective-permute-start.30 = (bf16[8,4,16,512]{3,2,1,0:T(8,128)(2,1)S(1)}, bf16[8,4,16,512]{3,2,1,0:T(8,128)(2,1)S(1)}, u32[]{:S(2)}, u32[]{:S(2)}) collective-permute-start(bf16[8,4,16,512]{3,2,1,0:T(8,128)(2,1)S(1)} %fusion.7), channel_id=1, source_target_pairs={{0,2},{1,3},{2,0},{3,1},{4,6},{5,7},{6,4},{7,5},{8,10},{9,11},{10,... | collective-permute-start | bytes 1572872 | tf_op jit(solution)/shard_map/ppermute | solution.py:32
  100.3 5.8 %collective-permute-start.22 = (bf16[2,4,16,1024]{3,2,1,0:T(8,128)(2,1)S(1)}, bf16[2,4,16,1024]{3,2,1,0:T(8,128)(2,1)S(1)}, u32[]{:S(2)}, u32[]{:S(2)}) collective-permute-start(bf16[2,4,16,1024]{3,2,1,0:T(8,128)(2,1)S(1)} %get-tuple-element.53), channel_id=1, source_target_pairs={{0,1},{1,0},{2,3},{3,2},{4,5},{5,4},{6,7},{7,6},{8,9},{9,8},{10,11... | collective-permute-start | bytes 786440 | tf_op jit(solution)/shard_map/ppermute | solution.py:32
  100.5 5.6 %collective-permute-start.23 = (bf16[2,4,16,1024]{3,2,1,0:T(8,128)(2,1)S(1)}, bf16[2,4,16,1024]{3,2,1,0:T(8,128)(2,1)S(1)}, u32[]{:S(2)}, u32[]{:S(2)}) collective-permute-start(bf16[2,4,16,1024]{3,2,1,0:T(8,128)(2,1)S(1)} %get-tuple-element.56), channel_id=1, source_target_pairs={{0,1},{1,0},{2,3},{3,2},{4,5},{5,4},{6,7},{7,6},{8,9},{9,8},{10,11... | collective-permute-start | bytes 786440 | tf_op jit(solution)/shard_map/ppermute | solution.py:32
  106.5 13.1 %collective-permute-start.31 = (bf16[8,4,16,512]{3,2,1,0:T(8,128)(2,1)S(1)}, bf16[8,4,16,512]{3,2,1,0:T(8,128)(2,1)S(1)}, u32[]{:S(2)}, u32[]{:S(2)}) collective-permute-start(bf16[8,4,16,512]{3,2,1,0:T(8,128)(2,1)S(1)} %slice_add_fusion.3), channel_id=1, source_target_pairs={{0,2},{1,3},{2,0},{3,1},{4,6},{5,7},{6,4},{7,5},{8,10},{9,11},{10,... | collective-permute-start | bytes 1572872 | tf_op jit(solution)/shard_map/ppermute | solution.py:32
  107.7 12.3 %collective-permute-start.32 = (bf16[64,512]{1,0:T(8,128)(2,1)S(1)}, bf16[64,512]{1,0:T(8,128)(2,1)S(1)}, u32[]{:S(2)}, u32[]{:S(2)}) collective-permute-start(bf16[64,512]{1,0:T(8,128)(2,1)S(1)} %get-tuple-element.81), channel_id=1, source_target_pairs={{0,16},{4,20},{8,24},{12,28},{16,0},{20,4},{24,8},{28,12},{1,17},{... | collective-permute-start | bytes 196616 | tf_op jit(solution)/shard_map/ppermute | solution.py:32
  111.2 9.0 %collective-permute-start.33 = (bf16[64,512]{1,0:T(8,128)(2,1)S(1)}, bf16[64,512]{1,0:T(8,128)(2,1)S(1)}, u32[]{:S(2)}, u32[]{:S(2)}) collective-permute-start(bf16[64,512]{1,0:T(8,128)(2,1)S(1)} %get-tuple-element.80), channel_id=1, source_target_pairs={{0,20},{4,16},{8,28},{12,24},{16,4},{20,0},{24,12},{28,8},{1,21},{... | collective-permute-start | bytes 196616 | tf_op jit(solution)/shard_map/ppermute | solution.py:32
  111.4 8.8 %collective-permute-start.34 = (bf16[64,512]{1,0:T(8,128)(2,1)S(1)}, bf16[64,512]{1,0:T(8,128)(2,1)S(1)}, u32[]{:S(2)}, u32[]{:S(2)}) collective-permute-start(bf16[64,512]{1,0:T(8,128)(2,1)S(1)} %get-tuple-element.79), channel_id=1, source_target_pairs={{0,24},{4,28},{8,16},{12,20},{16,8},{20,12},{24,0},{28,4},{1,25},{... | collective-permute-start | bytes 196616 | tf_op jit(solution)/shard_map/ppermute | solution.py:32
  114.4 7.1 %collective-permute-start.35 = (bf16[64,512]{1,0:T(8,128)(2,1)S(1)}, bf16[64,512]{1,0:T(8,128)(2,1)S(1)}, u32[]{:S(2)}, u32[]{:S(2)}) collective-permute-start(bf16[64,512]{1,0:T(8,128)(2,1)S(1)} %get-tuple-element.78), channel_id=1, source_target_pairs={{0,28},{4,24},{8,20},{12,16},{16,12},{20,8},{24,4},{28,0},{1,29},{... | collective-permute-start | bytes 196616 | tf_op jit(solution)/shard_map/ppermute | solution.py:32
  121.5 7.6 %collective-permute-start.36 = (bf16[128,512]{1,0:T(8,128)(2,1)S(1)}, bf16[128,512]{1,0:T(8,128)(2,1)S(1)}, u32[]{:S(2)}, u32[]{:S(2)}) collective-permute-start(bf16[128,512]{1,0:T(8,128)(2,1)S(1)} %get-tuple-element.38), channel_id=1, source_target_pairs={{0,4},{4,0},{8,12},{12,8},{16,20},{20,16},{24,28},{28,24},{1,5},{5... | collective-permute-start | bytes 393224 | tf_op jit(solution)/shard_map/ppermute | solution.py:32
  122.5 8.5 %collective-permute-start.37 = (bf16[128,512]{1,0:T(8,128)(2,1)S(1)}, bf16[128,512]{1,0:T(8,128)(2,1)S(1)}, u32[]{:S(2)}, u32[]{:S(2)}) collective-permute-start(bf16[128,512]{1,0:T(8,128)(2,1)S(1)} %get-tuple-element.39), channel_id=1, source_target_pairs={{0,8},{4,12},{8,0},{12,4},{16,24},{20,28},{24,16},{28,20},{1,9},{5... | collective-permute-start | bytes 393224 | tf_op jit(solution)/shard_map/ppermute | solution.py:32
  125.2 9.5 %collective-permute-start.38 = (bf16[128,512]{1,0:T(8,128)(2,1)S(1)}, bf16[128,512]{1,0:T(8,128)(2,1)S(1)}, u32[]{:S(2)}, u32[]{:S(2)}) collective-permute-start(bf16[128,512]{1,0:T(8,128)(2,1)S(1)} %pad_maximum_fusion.2), channel_id=1, source_target_pairs={{0,12},{4,8},{8,4},{12,0},{16,28},{20,24},{24,20},{28,16},{1,13},{... | collective-permute-start | bytes 393224 | tf_op jit(solution)/shard_map/ppermute | solution.py:32
  125.7 9.1 %collective-permute-start.39 = (bf16[64,512]{1,0:T(8,128)(2,1)S(1)}, bf16[64,512]{1,0:T(8,128)(2,1)S(1)}, u32[]{:S(2)}, u32[]{:S(2)}) collective-permute-start(bf16[64,512]{1,0:T(8,128)(2,1)S(1)} %bitcast.68), channel_id=1, source_target_pairs={{0,16},{4,20},{8,24},{12,28},{16,0},{20,4},{24,8},{28,12},{1,17},{... | collective-permute-start | bytes 196616 | tf_op jit(solution)/shard_map/ppermute | solution.py:32
  127.9 11.3 %collective-permute-start.40 = (bf16[64,512]{1,0:T(8,128)(2,1)S(1)}, bf16[64,512]{1,0:T(8,128)(2,1)S(1)}, u32[]{:S(2)}, u32[]{:S(2)}) collective-permute-start(bf16[64,512]{1,0:T(8,128)(2,1)S(1)} %bitcast.67), channel_id=1, source_target_pairs={{0,20},{4,16},{8,28},{12,24},{16,4},{20,0},{24,12},{28,8},{1,21},{... | collective-permute-start | bytes 196616 | tf_op jit(solution)/shard_map/ppermute | solution.py:32
  129.1 10.1 %collective-permute-start.41 = (bf16[64,512]{1,0:T(8,128)(2,1)S(1)}, bf16[64,512]{1,0:T(8,128)(2,1)S(1)}, u32[]{:S(2)}, u32[]{:S(2)}) collective-permute-start(bf16[64,512]{1,0:T(8,128)(2,1)S(1)} %bitcast.66), channel_id=1, source_target_pairs={{0,24},{4,28},{8,16},{12,20},{16,8},{20,12},{24,0},{28,4},{1,25},{... | collective-permute-start | bytes 196616 | tf_op jit(solution)/shard_map/ppermute | solution.py:32
  131.0 8.2 %collective-permute-start.42 = (bf16[64,512]{1,0:T(8,128)(2,1)S(1)}, bf16[64,512]{1,0:T(8,128)(2,1)S(1)}, u32[]{:S(2)}, u32[]{:S(2)}) collective-permute-start(bf16[64,512]{1,0:T(8,128)(2,1)S(1)} %bitcast.65), channel_id=1, source_target_pairs={{0,28},{4,24},{8,20},{12,16},{16,12},{20,8},{24,4},{28,0},{1,29},{... | collective-permute-start | bytes 196616 | tf_op jit(solution)/shard_map/ppermute | solution.py:32
  (26 other events, 180.6 us)
